TPU v7x, 32 devices: a whole 2x2x4 slice. The times are simulated.
32 devices in a mesh: dp: 8 (over y, x, core), tensor: 4 (over z).
Axes of the slice: x: 2, y: 2, z: 4, core: 2. Of those that a mesh axis runs over, the one named last changes fastest.
Arguments:
- tokens: bfloat16 [4096, 8192], P('dp', 'tensor'), may hold values from -6 to 6
- ref_gain: float32 [8192], P('tensor'), may hold values from 0.1 to 1.9
- ref_weight: bfloat16 [8192, 512], P('tensor'), may hold values from -0.0625 to 0.0625
- pol_gain: float32 [8192], replicated, may hold values from 0.1 to 1.9
- pol_weight: bfloat16 [8192, 512], P('dp'), may hold values from -0.0625 to 0.0625
- lengths: int32 [8, 4, 8], P('dp', 'tensor'), may hold values from 1 to 32, 128 in all within a row
- bins: int32 [8, 4, 8], P('dp', 'tensor'), may hold values from 0 to 7, each once within a row
- advantage: float32 [8, 4, 8], P('dp', 'tensor'), may hold values from -4 to 4
- logprob_gap: float32 [4096], P(('dp', 'tensor')), may hold values from -1 to 1
- cotangent: bfloat16 [8, 4, 256, 512], P('dp', 'tensor'), may hold values from -6 to 6
Outputs:
- policy_values: bfloat16 [8, 4, 256, 512], P('dp', 'tensor')
- grad_weight: float32 [8192, 512], P(('dp', 'tensor'))
Inputs may be any that keep to these rules, and one draw needn't show every extreme that they name: `lengths`: lengths of the 8 sequences of one run, in the order in which they lie in it; they sum to 128, and the longest of every run is exactly 32. The sequences of one run go to distinct bins: each bin takes exactly one sequence of every run.
All inputs are finite; a program needn't handle non-finite values.
Results may differ from a plain program's by a relative error of at most 0.015.
Values may be sent and summed in bfloat16 or wider, within the bound.
No kernel may reach another device: no remote copies, remote signals or barrier semaphores. Data moves between devices by JAX's collectives and lax.ppermute only.
A program may use at most 64 MiB of HBM per device.

v0:
```python
import functools
import math

import jax
import jax.numpy as jnp
from jax import lax
from jax.experimental import pallas as pl
from jax.experimental.pallas import tpu as pltpu
from jax.sharding import PartitionSpec as P

EPS = 1e-06
BETA = 1.0
AXES = ("dp", "tensor")
BF16 = jnp.bfloat16
F32 = jnp.float32
POWER_ROWS = 16
PARTS = 2


def dot(a, b):
    return jnp.dot(a, b, preferred_element_type=F32)


def dot_rows(a, b):
    return lax.dot_general(a, b, (((0,), (0,)), ((), ())), preferred_element_type=F32)


def swapped(array, dp_count):
    return lax.ppermute(array, "dp", [(i, i ^ 1) for i in range(dp_count)])


def turned(index, levels):
    return sum(((index >> i) & 1) << (levels - 1 - i) for i in range(levels))


def crossed(array, count, step):
    return lax.ppermute(array, "tensor", [(i, i ^ step) for i in range(count)])


def prepare_kernel(
    count, steps, at, x_ref, gain_ref, weight_ref, pol_ref, given_ref, kept_ref, *refs
):
    sent_refs, (rows_ref, total, square) = refs[:2], refs[2:]
    f = pl.program_id(0)
    own = x_ref.shape[0] // count
    levels = count.bit_length() - 1
    for i in range(count):
        source = jnp.bitwise_xor(at[0], turned(i, levels))
        rows_ref[i * own : (i + 1) * own, :] = x_ref[pl.ds(pl.multiple_of(source * own, own), own), :]
    wide = rows_ref[...].astype(F32)
    gained = (wide * pol_ref[...]).astype(BF16)

    @pl.when(f < steps // 2)
    def _():
        given_ref[...] = gained

    @pl.when(f >= steps // 2)
    def _():
        kept_ref[...] = gained

    part = dot((wide * gain_ref[...]).astype(BF16), weight_ref[...])
    squares = jnp.sum(wide * wide, axis=1, keepdims=True)

    @pl.when(f == 0)
    def _():
        total[...] = part
        square[...] = squares

    @pl.when(f > 0)
    def _():
        total[...] += part
        square[...] += squares

    @pl.when(f == steps - 1)
    def _():
        for i in range(count):
            sent = sent_refs[i // (count // 2)].at[i % (count // 2)]
            sent[:own, :] = total[i * own : (i + 1) * own, :].astype(BF16)
            power = jnp.broadcast_to(square[i * own : (i + 1) * own, :], (own, 128)).T
            high = power[: POWER_ROWS // 2].astype(BF16).astype(F32)
            low = power[: POWER_ROWS // 2] - high
            sent[own:, :] = jnp.zeros((POWER_ROWS, sent.shape[1]), BF16)
            sent[own:, :own] = jnp.concatenate([high, low], axis=0).astype(BF16)


def row_kernel(
    span, model_width, lengths, bins, advantage, gap_ref, cot_ref, kept_ref, got_ref, *refs
):
    fixed_ref, pull_ref, scale_ref, row_at_ref, sent_ref = refs
    own = pull_ref.shape[0]
    slots = row_at_ref.shape[1]
    row = lax.broadcasted_iota(jnp.int32, (own, slots), 0)
    slot = lax.broadcasted_iota(jnp.int32, (own, slots), 1)
    chosen = jnp.zeros((own, slots), jnp.bool_)
    size = jnp.ones((own, 128), F32)
    weight = jnp.zeros((own, 128), F32)
    start = jnp.int32(0)
    for s in range(lengths.shape[0]):
        end = start + lengths[s]
        inside = (row >= start) & (row < end)
        chosen = chosen | (inside & (slot - bins[s] * span == row - start))
        size = jnp.where(inside[:, :128], lengths[s].astype(F32), size)
        weight = jnp.where(inside[:, :128], advantage[s], weight)
        start = end
    row_at = jnp.where(chosen, 1.0, 0.0).astype(BF16)
    row_at_ref[...] = row_at
    importance = jnp.minimum(jnp.exp(jnp.broadcast_to(gap_ref[...], (128, own)).T), 2.0)
    coef_adv = (weight * importance / size).astype(BF16).astype(F32)
    coef_pull = (BETA / size).astype(BF16).astype(F32)
    total = kept_ref[...].astype(F32) + got_ref[...].astype(F32)
    square = jnp.zeros((1, own), F32)
    for power_row in range(own, total.shape[0], POWER_ROWS // 2):
        square = square + total[power_row : power_row + 1, :own]
    scale = lax.rsqrt(jnp.broadcast_to(square, (128, own)).T / model_width + EPS)
    reference = (total[:own] * scale[:, :1]).astype(BF16).astype(F32)
    upstream = dot(row_at, cot_ref[...])
    fixed = (coef_adv[:, :1] * upstream - coef_pull[:, :1] * reference) * scale[:, :1]
    pull = coef_pull * scale * scale
    high = pull.astype(BF16).astype(F32)
    width = fixed.shape[1]
    fixed_ref[...] = fixed
    pull_ref[...] = pull
    scale_ref[...] = scale
    sent_ref[:, :width] = fixed.astype(BF16)
    lane = lax.broadcasted_iota(jnp.int32, pull.shape, 1)
    sent_ref[:, width:] = jnp.where(lane < 64, high, pull - high).astype(BF16)


def grad_kernel(factor, at, kept_ref, got_ref, slope_ref, slope_got_ref, *refs):
    *out_refs, grad = refs
    total = dot_rows(kept_ref[...], slope_ref[...]) + dot_rows(got_ref[...], slope_got_ref[...])
    grad[...] = total * factor
    rows = grad.shape[0] // at.shape[0]
    count = at.shape[0] // 2
    for s in range(2 * count):
        chunk = grad[pl.ds(pl.multiple_of(at[s] * rows, rows), rows), :]
        out_ref = out_refs[s // count]
        place = s % count
        out_ref[place * rows : (place + 1) * rows, :] = chunk.astype(out_ref.dtype)


def on_device(
    tokens,
    ref_gain,
    ref_weight,
    pol_gain,
    pol_weight,
    lengths,
    bins,
    advantage,
    logprob_gap,
    cotangent,
):
    tensor_count = lax.axis_size("tensor")
    dp_count = lax.axis_size("dp")
    t = lax.axis_index("tensor")
    d = lax.axis_index("dp")
    cores = dp_count // tensor_count
    assert cores == 2
    places = dp_count // cores
    levels = places.bit_length() - 1
    assert 1 << levels == places == tensor_count
    place = d // cores
    core = d % cores
    group_rows, block = tokens.shape
    own_rows = group_rows // tensor_count
    slot_count = cotangent.shape[2]
    span_rows = slot_count // dp_count
    value_width = ref_weight.shape[1]
    model_width = pol_gain.shape[0]
    shard = pol_weight.shape[0]
    width = value_width // PARTS
    factor = 1.0 / math.sqrt(dp_count * tensor_count * lengths.shape[2])
    relative = place ^ t

    def flat(p, c, z):
        return (p * cores + c) * tensor_count + z

    def stage(number, held):
        pairs, is_getter = [], jnp.zeros((), jnp.bool_)
        for c in range(cores):
            holders = [0]
            for before in range(number):
                bit = 1 << ((c + before) % levels)
                holders = holders + [q ^ bit for q in holders]
            bit = 1 << ((c + number) % levels)
            for q in holders:
                pairs += [
                    (flat(q ^ z, c, z), flat(q ^ bit ^ z, c, z)) for z in range(tensor_count)
                ]
                is_getter = is_getter | ((core == c) & (relative == (q ^ bit)))
        return lax.ppermute(held, AXES, pairs), is_getter

    first_got, first_getter = stage(0, pol_weight)

    steps = 4
    feature_step = block // steps
    at = jnp.stack([t, (1 - core) * (steps // 2)]).astype(jnp.int32)
    ref_shape = (tensor_count // 2, own_rows + POWER_ROWS, value_width)

    def at_step(f, at):
        return lax.rem(f + at[1], steps)

    prepared = pl.pallas_call(
        functools.partial(prepare_kernel, tensor_count, steps),
        grid_spec=pltpu.PrefetchScalarGridSpec(
            num_scalar_prefetch=1,
            grid=(steps,),
            in_specs=[
                pl.BlockSpec((group_rows, feature_step), lambda f, at: (0, at_step(f, at))),
                pl.BlockSpec((1, feature_step), lambda f, at: (0, at_step(f, at))),
                pl.BlockSpec((feature_step, value_width), lambda f, at: (at_step(f, at), 0)),
                pl.BlockSpec(
                    (1, feature_step), lambda f, at: (0, at[0] * steps + at_step(f, at))
                ),
            ],
            out_specs=[
                pl.BlockSpec(
                    (group_rows, feature_step), lambda f, at: (0, jnp.minimum(f, steps // 2 - 1))
                ),
                pl.BlockSpec(
                    (group_rows, feature_step), lambda f, at: (0, jnp.maximum(f - steps // 2, 0))
                ),
            ]
            + [pl.BlockSpec(ref_shape, lambda f, at: (0, 0, 0))] * 2,
            scratch_shapes=[
                pltpu.VMEM((group_rows, feature_step), BF16),
                pltpu.VMEM((group_rows, value_width), F32),
                pltpu.VMEM((group_rows, 1), F32),
            ],
        ),
        out_shape=[jax.ShapeDtypeStruct((group_rows, shard), BF16)] * 2
        + [jax.ShapeDtypeStruct(ref_shape, BF16)] * 2,
        compiler_params=pltpu.CompilerParams(vmem_limit_bytes=56 * 2**20),
        cost_estimate=pl.CostEstimate(
            flops=2 * group_rows * block * value_width,
            bytes_accessed=8 * 2**20,
            transcendentals=0,
        ),
        name="prepare",
    )(at, tokens, ref_gain.reshape(1, block), ref_weight, pol_gain.reshape(1, model_width))
    given_rows, kept_rows, ref_kept, ref_sent = prepared
    ref_got = crossed(ref_sent, tensor_count, 1)
    got_rows = swapped(given_rows, dp_count)

    cot = cotangent.reshape(slot_count, value_width)
    held, got, is_getter = [], [], []
    for j in range(PARTS):
        cols = slice(j * width, (j + 1) * width)
        part = jnp.where(first_getter, first_got[:, cols], pol_weight[:, cols])
        if j < PARTS - 1:
            part, first_got = lax.optimization_barrier((part, first_got))
        else:
            part, cot, kept_rows = lax.optimization_barrier((part, cot, kept_rows))
        for number in range(1, levels):
            part_got, part_getter = stage(number, part)
            if number < levels - 1:
                part = jnp.where(part_getter, part_got, part)
        held.append(part)
        got.append(part_got)
        is_getter.append(part_getter)
    for level in range(1, levels):
        ref_sum = ref_kept[:, :own_rows].astype(F32) + ref_got[:, :own_rows].astype(F32)
        ref_all = jnp.concatenate(
            [ref_sum.astype(BF16), ref_kept[:, own_rows:], ref_got[:, own_rows:]], axis=1
        )
        half_count = ref_all.shape[0] // 2
        ref_kept = ref_all[:half_count]
        ref_got = crossed(ref_all[half_count:], tensor_count, 1 << level)
    got_cot = lax.all_to_all(cot, "dp", split_axis=0, concat_axis=0, tiled=True)

    def plane_bit(level):
        return jnp.where(core == 0, 1 << (level % levels), 1 << ((1 + level) % levels))

    chunk_at = []
    for i in range(places):
        away = sum(plane_bit(level) * ((i >> (levels - 1 - level)) & 1) for level in range(levels))
        chunk_at.append(place ^ away ^ turned(t, levels))
    chunk_at = jnp.stack(chunk_at).astype(jnp.int32)

    smem = pl.BlockSpec(memory_space=pltpu.SMEM)
    vmem = pl.BlockSpec(memory_space=pltpu.VMEM)
    got[-1], got_cot = lax.optimization_barrier((got[-1], got_cot))
    fixed, pull, row_scale, row_at, terms_sent = pl.pallas_call(
        functools.partial(row_kernel, span_rows, model_width),
        in_specs=[smem] * 3 + [vmem] * 4,
        out_specs=[vmem] * 5,
        out_shape=[
            jax.ShapeDtypeStruct((own_rows, value_width), F32),
            jax.ShapeDtypeStruct((own_rows, 128), F32),
            jax.ShapeDtypeStruct((own_rows, 128), F32),
            jax.ShapeDtypeStruct((own_rows, slot_count), BF16),
            jax.ShapeDtypeStruct((own_rows, value_width + 128), BF16),
        ],
        compiler_params=pltpu.CompilerParams(vmem_limit_bytes=16 * 2**20),
        cost_estimate=pl.CostEstimate(
            flops=2 * own_rows * slot_count * value_width,
            bytes_accessed=2**21,
            transcendentals=0,
        ),
        name="rows",
    )(
        lengths.reshape(-1),
        bins.reshape(-1),
        advantage.reshape(-1),
        logprob_gap.reshape(1, own_rows),
        got_cot,
        ref_kept[0],
        ref_got[0],
    )
    far = 1 << (levels - 1)
    terms_got = crossed(terms_sent, tensor_count, far).astype(F32)
    pull_got = terms_got[:, value_width : value_width + 1] + terms_got[:, -1:]
    fixed = jnp.concatenate([fixed, terms_got[:, :value_width]], axis=0)
    pull = jnp.concatenate([pull[:, :1], pull_got], axis=0)

    values, slopes = [], []
    for j in range(PARTS):
        weight = jnp.where(is_getter[j], got[j], held[j])
        value_given = dot(got_rows, weight).astype(BF16)
        total = dot(kept_rows, weight) + swapped(value_given, dp_count).astype(F32)
        for level in range(levels - 1):
            rows = total.shape[0] // 2
            total = total[:rows] + crossed(
                total[rows:].astype(BF16), tensor_count, 1 << level
            ).astype(F32)
        other = jnp.concatenate([total[own_rows:], total[:own_rows]], axis=0).astype(BF16)
        total = total + crossed(other, tensor_count, far).astype(F32)
        values.append(total[:own_rows] * row_scale[:, :1])

        cols = slice(j * width, (j + 1) * width)
        slope = (fixed[:, cols] + pull * total).astype(BF16)
        if j < PARTS - 1:
            slope, fixed, pull = lax.optimization_barrier((slope, fixed, pull))
        for level in reversed(range(levels - 1)):
            slope = jnp.concatenate([slope, crossed(slope, tensor_count, 1 << level)], axis=0)
        slopes.append(slope)

    sent = dot_rows(row_at, jnp.concatenate(values, axis=1).astype(BF16)).astype(BF16)
    policy_values = lax.all_to_all(sent, "dp", split_axis=0, concat_axis=0, tiled=True)

    grad_kept, grad_sent = [], []
    for j in range(PARTS):
        slopes_got = swapped(slopes[j], dp_count)
        if j == PARTS - 1:
            slopes_got, policy_values = lax.optimization_barrier((slopes_got, policy_values))
        chunks = pl.pallas_call(
            functools.partial(grad_kernel, factor),
            grid_spec=pltpu.PrefetchScalarGridSpec(
                num_scalar_prefetch=1,
                grid=(1,),
                in_specs=[
                    pl.BlockSpec((group_rows, shard), lambda i, at: (0, 0)),
                    pl.BlockSpec((group_rows, shard), lambda i, at: (0, 0)),
                    pl.BlockSpec((group_rows, width), lambda i, at: (0, 0)),
                    pl.BlockSpec((group_rows, width), lambda i, at: (0, 0)),
                ],
                out_specs=[pl.BlockSpec((shard // 2, width), lambda i, at: (0, 0))] * 2,
                scratch_shapes=[pltpu.VMEM((shard, width), F32)],
            ),
            out_shape=[
                jax.ShapeDtypeStruct((shard // 2, width), F32),
                jax.ShapeDtypeStruct((shard // 2, width), BF16),
            ],
            compiler_params=pltpu.CompilerParams(vmem_limit_bytes=32 * 2**20),
            cost_estimate=pl.CostEstimate(
                flops=4 * group_rows * shard * width,
                bytes_accessed=4 * 2**20,
                transcendentals=0,
            ),
            name="gradient",
        )(chunk_at, kept_rows, got_rows, slopes[j], slopes_got)
        grad_kept.append(chunks[0])
        grad_sent.append(chunks[1])
    grads = []
    for j in range(PARTS):
        total, given = grad_kept[j], grad_sent[j]
        for level in range(levels):
            pairs = [
                (p * cores + c, (p ^ (1 << ((c + level) % levels))) * cores + c)
                for p in range(places)
                for c in range(cores)
            ]
            total = total + lax.ppermute(given, "dp", pairs).astype(F32)
            half_rows = total.shape[0] // 2
            if level < levels - 1:
                total, given = total[:half_rows], total[half_rows:].astype(BF16)
        grads.append(total.astype(BF16))
    pairs = [
        (flat(p, c, z), flat(z, c, p ^ turned(z, levels)))
        for p in range(places)
        for c in range(cores)
        for z in range(tensor_count)
    ]
    grad_weight = lax.ppermute(jnp.concatenate(grads, axis=1), AXES, pairs).astype(F32)
    return (policy_values.reshape(1, 1, slot_count, value_width), grad_weight)


def solution(mesh):
    in_specs = (
        P("dp", "tensor"),
        P("tensor"),
        P("tensor", None),
        P(),
        P("dp", None),
        P("dp", "tensor", None),
        P("dp", "tensor", None),
        P("dp", "tensor", None),
        P(("dp", "tensor")),
        P("dp", "tensor", None, None),
    )
    out_specs = (P("dp", "tensor", None, None), P(("dp", "tensor"), None))
    return jax.shard_map(
        on_device, mesh=mesh, in_specs=in_specs, out_specs=out_specs, check_vma=False
    )
```

profile of v0, /device:TPU:4, one launch (start us, length us, event | category | flops | bytes accessed | tf_op | source)
XLA Modules:
  0.0 112.2 jit_solution(3719849152851872632)
XLA Ops:
  0.6 1.7 %collective-permute-start = (bf16[1024,512]{1,0:T(8,128)(2,1)}, bf16[1024,512]{1,0:T(8,128)(2,1)}, u32[]{:S(2)}, u32[]{:S(2)}) collective-permute-start(bf16[1024,512]{1,0:T(8,128)(2,1)} %param.14), channel_id=1, source_target_pairs={{0,8},{9,1},{18,26},{27,19},{4,20},{13,29},{22,6},{31,15}} | collective-permute-start | bytes 3145736 | tf_op jit(solution)/shard_map/ppermute | solution.py:192
  2.9 7.2 %prepare.1 = (bf16[512,1024]{1,0:T(8,128)(2,1)}, bf16[512,1024]{1,0:T(8,128)(2,1)}, bf16[2,144,512]{2,1,0:T(8,128)(2,1)}, bf16[2,144,512]{2,1,0:T(8,128)(2,1)}) custom-call(s32[2]{0:T(128)} %pad_add_fusion.at, bf16[512,2048]{1,0:T(8,128)(2,1)} %x_ref.1, f32[1,2048]{1,0:T(1,128)} %bitcast.41, bf16[2048,512]{1,0:T(8,128)(2,1)} %weight_ref.1, f32[1,8192]{1,0:T(1,128)} %bitcast.38), custom_call_target="tpu_custom_call" | custom-call | flops 1073741824 | bytes 8388608 | tf_op jit(solution)/shard_map/prepare/pallas_call | solution.py:204
  10.1 1.6 %collective-permute-start.2 = (bf16[2,144,512]{2,1,0:T(8,128)(2,1)}, bf16[2,144,512]{2,1,0:T(8,128)(2,1)S(1)}, u32[]{:S(2)}, u32[]{:S(2)}) collective-permute-start(bf16[2,144,512]{2,1,0:T(8,128)(2,1)} %get-tuple-element.33), channel_id=1, source_target_pairs={{0,1},{1,0},{2,3},{3,2},{4,5},{5,4},{6,7},{7,6},{8,9},{9,8},{10,11... | collective-permute-start | bytes 884744 | tf_op jit(solution)/shard_map/ppermute | solution.py:37
  12.5 1.9 %slice_select_fusion = bf16[1024,256]{1,0:T(8,128)(2,1)} fusion(bf16[1024,512]{1,0:T(8,128)(2,1)} %collective-permute-done, bf16[1024,512]{1,0:T(8,128)(2,1)S(1)} %copy-done.5, pred[]{:T(512)S(6)} %or.15), kind=kLoop, calls=%fused_computation.8 | loop fusion | flops 262144 | bytes 1572865 | tf_op jit(solution)/shard_map/jit(_where)/select_n | solution.py:250
  14.4 1.1 %slice_select_fusion.1 = bf16[1024,256]{1,0:T(8,128)(2,1)S(1)} fusion(bf16[1024,512]{1,0:T(8,128)(2,1)S(1)} %copy-done.5, bf16[1024,512]{1,0:T(8,128)(2,1)} %collective-permute-done, pred[]{:T(512)S(6)} %or.15), kind=kLoop, calls=%fused_computation.12 | loop fusion | flops 262144 | bytes 1572865 | tf_op jit(solution)/shard_map/jit(_where)/select_n | solution.py:250
  15.5 1.3 %collective-permute-start.1 = (bf16[1024,256]{1,0:T(8,128)(2,1)S(1)}, bf16[1024,256]{1,0:T(8,128)(2,1)S(1)}, u32[]{:S(2)}, u32[]{:S(2)}) collective-permute-start(bf16[1024,256]{1,0:T(8,128)(2,1)S(1)} %slice_select_fusion.1), channel_id=1, source_target_pairs={{0,16},{9,25},{18,2},{27,11},{8,24},{1,17},{26,10},{19,3},{4,12},{... | collective-permute-start | bytes 1572872 | tf_op jit(solution)/shard_map/ppermute | solution.py:192
  16.8 1.3 %collective-permute-start.5 = (bf16[1024,256]{1,0:T(8,128)(2,1)}, bf16[1024,256]{1,0:T(8,128)(2,1)}, u32[]{:S(2)}, u32[]{:S(2)}) collective-permute-start(bf16[1024,256]{1,0:T(8,128)(2,1)} %slice_select_fusion), channel_id=1, source_target_pairs={{0,16},{9,25},{18,2},{27,11},{8,24},{1,17},{26,10},{19,3},{4,12},{... | collective-permute-start | bytes 1572872 | tf_op jit(solution)/shard_map/ppermute | solution.py:192
  19.0 8.5 %all-to-all-start = ((bf16[8,32,512]{2,1,0:T(8,128)(2,1)}), bf16[8,32,512]{2,1,0:T(8,128)(2,1)S(1)}, u32[]{:S(2)}, u32[]{:S(2)}) async-start(bf16[8,32,512]{2,1,0:T(8,128)(2,1)} %bitcast.37), calls=%async_computation | async-start | bytes 524288 | tf_op jit(solution)/shard_map/all_to_all | solution.py:270
  27.6 3.6 %collective-permute-start.3 = (bf16[1,160,512]{2,1,0:T(8,128)(2,1)S(1)}, bf16[1,160,512]{2,1,0:T(8,128)(2,1)S(1)}, u32[]{:S(2)}, u32[]{:S(2)}) collective-permute-start(bf16[1,160,512]{2,1,0:T(8,128)(2,1)S(1)} %get-tuple-element.56), channel_id=1, source_target_pairs={{0,2},{1,3},{2,0},{3,1},{4,6},{5,7},{6,4},{7,5},{8,10},{9,11},{10,... | collective-permute-start | bytes 491528 | tf_op jit(solution)/shard_map/ppermute | solution.py:37
  31.2 5.9 %all-to-all-done = bf16[8,32,512]{2,1,0:T(8,128)(2,1)S(1)} async-done(((bf16[8,32,512]{2,1,0:T(8,128)(2,1)}), bf16[8,32,512]{2,1,0:T(8,128)(2,1)S(1)}, u32[]{:S(2)}, u32[]{:S(2)}) %all-to-all-start) | async-done | bytes 262176 | tf_op jit(solution)/shard_map/all_to_all | solution.py:270
  37.1 2.1 %collective-permute-done.3 = bf16[1,160,512]{2,1,0:T(8,128)(2,1)S(1)} collective-permute-done((bf16[1,160,512]{2,1,0:T(8,128)(2,1)S(1)}, bf16[1,160,512]{2,1,0:T(8,128)(2,1)S(1)}, u32[]{:S(2)}, u32[]{:S(2)}) %collective-permute-start.3) | collective-permute-done | bytes 163872 | tf_op jit(solution)/shard_map/ppermute | solution.py:37
  40.8 2.3 %convolution_convert_fusion.2 = bf16[512,256]{1,0:T(8,128)(2,1)} fusion(bf16[512,1024]{1,0:T(8,128)(2,1)S(1)} %collective-permute-done.6.got_ref, bf16[1024,256]{1,0:T(8,128)(2,1)} %collective-permute-done.5, bf16[1024,256]{1,0:T(8,128)(2,1)} %slice_select_fusion, pred[]{:T(512)S(6)} %or.18), kind=kOutput, calls=%fused_computation.4 | convolution fusion | flops 268828672 | bytes 2359297 | tf_op jit(solution)/shard_map/dot_general | solution.py:21
  44.9 5.6 %collective-permute-done.4 = bf16[128,640]{1,0:T(8,128)(2,1)S(1)} collective-permute-done((bf16[128,640]{1,0:T(8,128)(2,1)S(1)}, bf16[128,640]{1,0:T(8,128)(2,1)S(1)}, u32[]{:S(2)}, u32[]{:S(2)}) %collective-permute-start.4) | collective-permute-done | bytes 163872 | tf_op jit(solution)/shard_map/ppermute | solution.py:37
  50.9 1.6 %convolution_add_fusion.1 = f32[512,256]{1,0:T(8,128)S(1)} fusion(bf16[512,1024]{1,0:T(8,128)(2,1)S(1)} %copy-done, bf16[512,256]{1,0:T(8,128)(2,1)} %collective-permute-done.7, bf16[1024,256]{1,0:T(8,128)(2,1)} %collective-permute-done.5, bf16[1024,256]{1,0:T(8,128)(2,1)} %slice_select_fusion, pred[]{:T(512)S(6)} %or.18), kind=kOutput, calls=%fused_computation.1 | convolution fusion | flops 268959744 | bytes 2883585 | tf_op jit(solution)/shard_map/dot_general | solution.py:21
  52.6 1.4 %convolution_add_fusion = f32[512,256]{1,0:T(8,128)S(1)} fusion(bf16[512,1024]{1,0:T(8,128)(2,1)S(1)} %copy-done, bf16[512,256]{1,0:T(8,128)(2,1)} %collective-permute-done.10, bf16[1024,256]{1,0:T(8,128)(2,1)S(1)} %copy-done.8, bf16[1024,256]{1,0:T(8,128)(2,1)S(1)} %slice_select_fusion.1, pred[]{:T(512)S(6)} %or.18), kind=kOutput, calls=%fused_computation | convolution fusion | flops 268959744 | bytes 2883585 | tf_op jit(solution)/shard_map/dot_general | solution.py:21
  54.0 2.1 %collective-permute-start.11 = (bf16[256,256]{1,0:T(8,128)(2,1)S(1)}, bf16[256,256]{1,0:T(8,128)(2,1)S(1)}, u32[]{:S(2)}, u32[]{:S(2)}) collective-permute-start(bf16[256,256]{1,0:T(8,128)(2,1)S(1)} %slice.204), channel_id=1, source_target_pairs={{0,1},{1,0},{2,3},{3,2},{4,5},{5,4},{6,7},{7,6},{8,9},{9,8},{10,11... | collective-permute-start | bytes 393224 | tf_op jit(solution)/shard_map/ppermute | solution.py:37
  56.1 2.8 %collective-permute-done.8 = bf16[256,256]{1,0:T(8,128)(2,1)S(1)} collective-permute-done((bf16[256,256]{1,0:T(8,128)(2,1)S(1)}, bf16[256,256]{1,0:T(8,128)(2,1)S(1)}, u32[]{:S(2)}, u32[]{:S(2)}) %collective-permute-start.8) | collective-permute-done | bytes 131104 | tf_op jit(solution)/shard_map/ppermute | solution.py:37
  59.1 2.2 %collective-permute-done.11 = bf16[256,256]{1,0:T(8,128)(2,1)S(1)} collective-permute-done((bf16[256,256]{1,0:T(8,128)(2,1)S(1)}, bf16[256,256]{1,0:T(8,128)(2,1)S(1)}, u32[]{:S(2)}, u32[]{:S(2)}) %collective-permute-start.11) | collective-permute-done | bytes 131104 | tf_op jit(solution)/shard_map/ppermute | solution.py:37
  62.1 7.1 %collective-permute-done.9 = bf16[256,256]{1,0:T(8,128)(2,1)S(1)} collective-permute-done((bf16[256,256]{1,0:T(8,128)(2,1)S(1)}, bf16[256,256]{1,0:T(8,128)(2,1)S(1)}, u32[]{:S(2)}, u32[]{:S(2)}) %collective-permute-start.9) | collective-permute-done | bytes 131104 | tf_op jit(solution)/shard_map/ppermute | solution.py:37
  69.3 1.4 %collective-permute-done.12 = bf16[256,256]{1,0:T(8,128)(2,1)S(1)} collective-permute-done((bf16[256,256]{1,0:T(8,128)(2,1)S(1)}, bf16[256,256]{1,0:T(8,128)(2,1)S(1)}, u32[]{:S(2)}, u32[]{:S(2)}) %collective-permute-start.12) | collective-permute-done | bytes 131104 | tf_op jit(solution)/shard_map/ppermute | solution.py:37
  71.9 5.4 %all-to-all-start.1 = ((bf16[8,32,512]{2,1,0:T(8,128)(2,1)}), bf16[8,32,512]{2,1,0:T(8,128)(2,1)S(1)}, u32[]{:S(2)}, u32[]{:S(2)}) async-start(bf16[8,32,512]{2,1,0:T(8,128)(2,1)} %bitcast.15), calls=%async_computation.1 | async-start | bytes 524288 | tf_op jit(solution)/shard_map/all_to_all | solution.py:340
  77.3 1.9 %collective-permute-start.15 = (bf16[256,256]{1,0:T(8,128)(2,1)S(1)}, bf16[256,256]{1,0:T(8,128)(2,1)S(1)}, u32[]{:S(2)}, u32[]{:S(2)}) collective-permute-start(bf16[256,256]{1,0:T(8,128)(2,1)S(1)} %get-tuple-element.46), channel_id=1, source_target_pairs={{0,1},{1,0},{2,3},{3,2},{4,5},{5,4},{6,7},{7,6},{8,9},{9,8},{10,11... | collective-permute-start | bytes 393224 | tf_op jit(solution)/shard_map/ppermute | solution.py:37
  79.3 3.7 %collective-permute-done.15 = bf16[256,256]{1,0:T(8,128)(2,1)S(1)} collective-permute-done((bf16[256,256]{1,0:T(8,128)(2,1)S(1)}, bf16[256,256]{1,0:T(8,128)(2,1)S(1)}, u32[]{:S(2)}, u32[]{:S(2)}) %collective-permute-start.15) | collective-permute-done | bytes 131104 | tf_op jit(solution)/shard_map/ppermute | solution.py:37
  83.2 1.4 %gradient.3 = (f32[512,256]{1,0:T(8,128)S(1)}, bf16[512,256]{1,0:T(8,128)(2,1)S(1)}) custom-call(s32[4]{0:T(128)S(1)} %pad_add_fusion.1.at, bf16[512,1024]{1,0:T(8,128)(2,1)S(1)} %copy-done, bf16[512,1024]{1,0:T(8,128)(2,1)S(1)} %collective-permute-done.6.got_ref, bf16[512,256]{1,0:T(8,128)(2,1)S(1)} %pad_maximum_fusion.2.slope_ref, ...), custom_call_target="tpu_custom_call" | custom-call | flops 536870912 | bytes 4194304 | tf_op jit(solution)/shard_map/gradient/pallas_call | solution.py:347
  84.6 1.5 %collective-permute-start.19 = (bf16[512,256]{1,0:T(8,128)(2,1)S(1)}, bf16[512,256]{1,0:T(8,128)(2,1)S(1)}, u32[]{:S(2)}, u32[]{:S(2)}) collective-permute-start(bf16[512,256]{1,0:T(8,128)(2,1)S(1)} %get-tuple-element.51), channel_id=1, source_target_pairs={{0,8},{4,20},{8,0},{12,28},{16,24},{20,4},{24,16},{28,12},{1,9},{5... | collective-permute-start | bytes 786440 | tf_op jit(solution)/shard_map/ppermute | solution.py:384
  86.2 1.4 %gradient.2 = (f32[512,256]{1,0:T(8,128)S(1)}, bf16[512,256]{1,0:T(8,128)(2,1)S(1)}) custom-call(s32[4]{0:T(128)S(1)} %pad_add_fusion.1.at, bf16[512,1024]{1,0:T(8,128)(2,1)S(1)} %copy-done, bf16[512,1024]{1,0:T(8,128)(2,1)S(1)} %collective-permute-done.6.got_ref, bf16[512,256]{1,0:T(8,128)(2,1)S(1)} %constant_dynamic-update-slice_fusion.slope_ref, ...), custom_call_target="tpu_custom_call" | custom-call | flops 536870912 | bytes 4194304 | tf_op jit(solution)/shard_map/gradient/pallas_call | solution.py:347
  88.2 2.9 %collective-permute-done.19 = bf16[512,256]{1,0:T(8,128)(2,1)S(1)} collective-permute-done((bf16[512,256]{1,0:T(8,128)(2,1)S(1)}, bf16[512,256]{1,0:T(8,128)(2,1)S(1)}, u32[]{:S(2)}, u32[]{:S(2)}) %collective-permute-start.19) | collective-permute-done | bytes 262176 | tf_op jit(solution)/shard_map/ppermute | solution.py:384
  92.3 2.2 %collective-permute-done.17 = bf16[512,256]{1,0:T(8,128)(2,1)S(1)} collective-permute-done((bf16[512,256]{1,0:T(8,128)(2,1)S(1)}, bf16[512,256]{1,0:T(8,128)(2,1)S(1)}, u32[]{:S(2)}, u32[]{:S(2)}) %collective-permute-start.17) | collective-permute-done | bytes 262176 | tf_op jit(solution)/shard_map/ppermute | solution.py:384
  94.6 1.6 %collective-permute-start.18 = (bf16[256,256]{1,0:T(8,128)(2,1)S(1)}, bf16[256,256]{1,0:T(8,128)(2,1)S(1)}, u32[]{:S(2)}, u32[]{:S(2)}) collective-permute-start(bf16[256,256]{1,0:T(8,128)(2,1)S(1)} %slice.203), channel_id=1, source_target_pairs={{0,16},{4,12},{8,24},{12,4},{16,0},{20,28},{24,8},{28,20},{1,17},{... | collective-permute-start | bytes 393224 | tf_op jit(solution)/shard_map/ppermute | solution.py:384
  96.2 3.4 %collective-permute-done.18 = bf16[256,256]{1,0:T(8,128)(2,1)S(1)} collective-permute-done((bf16[256,256]{1,0:T(8,128)(2,1)S(1)}, bf16[256,256]{1,0:T(8,128)(2,1)S(1)}, u32[]{:S(2)}, u32[]{:S(2)}) %collective-permute-start.18) | collective-permute-done | bytes 131104 | tf_op jit(solution)/shard_map/ppermute | solution.py:384
  99.7 6.4 %collective-permute-start.21 = (bf16[256,512]{1,0:T(8,128)(2,1)S(1)}, bf16[256,512]{1,0:T(8,128)(2,1)S(1)}, u32[]{:S(2)}, u32[]{:S(2)}) collective-permute-start(bf16[256,512]{1,0:T(8,128)(2,1)S(1)} %pad_maximum_fusion.3), channel_id=1, source_target_pairs={{0,0},{1,10},{2,17},{3,27},{4,4},{5,14},{6,21},{7,31},{8,1},{9,11}... | collective-permute-start | bytes 786440 | tf_op jit(solution)/shard_map/ppermute | solution.py:395
  106.1 4.5 %collective-permute-done.21 = bf16[256,512]{1,0:T(8,128)(2,1)S(1)} collective-permute-done((bf16[256,512]{1,0:T(8,128)(2,1)S(1)}, bf16[256,512]{1,0:T(8,128)(2,1)S(1)}, u32[]{:S(2)}, u32[]{:S(2)}) %collective-permute-start.21) | collective-permute-done | bytes 262176 | tf_op jit(solution)/shard_map/ppermute | solution.py:395
  (86 shorter events, 12.2 us)
Async XLA Ops:
  0.6 11.8 %collective-permute-start = (bf16[1024,512]{1,0:T(8,128)(2,1)}, bf16[1024,512]{1,0:T(8,128)(2,1)}, u32[]{:S(2)}, u32[]{:S(2)}) collective-permute-start(bf16[1024,512]{1,0:T(8,128)(2,1)} %param.14), channel_id=1, source_target_pairs={{0,8},{9,1},{18,26},{27,19},{4,20},{13,29},{22,6},{31,15}} | collective-permute-start | bytes 3145736 | tf_op jit(solution)/shard_map/ppermute | solution.py:192
  2.9 9.6 %copy-start.5 = (bf16[1024,512]{1,0:T(8,128)(2,1)S(1)}, bf16[1024,512]{1,0:T(8,128)(2,1)}, u32[]{:S(2)}) copy-start(bf16[1024,512]{1,0:T(8,128)(2,1)} %param.14) | copy-start | bytes 3145732
  10.0 8.9 %copy-start.9 = (bf16[2,144,512]{2,1,0:T(8,128)(2,1)S(1)}, bf16[2,144,512]{2,1,0:T(8,128)(2,1)}, u32[]{:S(2)}) copy-start(bf16[2,144,512]{2,1,0:T(8,128)(2,1)} %get-tuple-element.32) | copy-start | bytes 884740
  10.1 8.9 %collective-permute-start.2 = (bf16[2,144,512]{2,1,0:T(8,128)(2,1)}, bf16[2,144,512]{2,1,0:T(8,128)(2,1)S(1)}, u32[]{:S(2)}, u32[]{:S(2)}) collective-permute-start(bf16[2,144,512]{2,1,0:T(8,128)(2,1)} %get-tuple-element.33), channel_id=1, source_target_pairs={{0,1},{1,0},{2,3},{3,2},{4,5},{5,4},{6,7},{7,6},{8,9},{9,8},{10,11... | collective-permute-start | bytes 884744 | tf_op jit(solution)/shard_map/ppermute | solution.py:37
  11.7 29.1 %collective-permute-start.6 = (bf16[512,1024]{1,0:T(8,128)(2,1)}, bf16[512,1024]{1,0:T(8,128)(2,1)S(1)}, u32[]{:S(2)}, u32[]{:S(2)}) collective-permute-start(bf16[512,1024]{1,0:T(8,128)(2,1)} %get-tuple-element.39), channel_id=1, source_target_pairs={{0,4},{4,0},{8,12},{12,8},{16,20},{20,16},{24,28},{28,24},{1,5},{5... | collective-permute-start | bytes 3145736 | tf_op jit(solution)/shard_map/ppermute | solution.py:29
  14.3 24.9 %copy-start.1 = (s32[1,1,8]{2,1,0:T(1,128)S(1)}, s32[1,1,8]{2,1,0:T(1,128)}, u32[]{:S(2)}) copy-start(s32[1,1,8]{2,1,0:T(1,128)} %param.15) | copy-start | bytes 100
  14.3 24.9 %copy-start.2 = (s32[1,1,8]{2,1,0:T(1,128)S(1)}, s32[1,1,8]{2,1,0:T(1,128)}, u32[]{:S(2)}) copy-start(s32[1,1,8]{2,1,0:T(1,128)} %param.16) | copy-start | bytes 100
  14.3 24.9 %copy-start.3 = (f32[1,1,8]{2,1,0:T(1,128)S(1)}, f32[1,1,8]{2,1,0:T(1,128)}, u32[]{:S(2)}) copy-start(f32[1,1,8]{2,1,0:T(1,128)} %param.17) | copy-start | bytes 100
  14.4 24.9 %copy-start.4 = (f32[128]{0:T(128)S(1)}, f32[128]{0:T(128)}, u32[]{:S(2)}) copy-start(f32[128]{0:T(128)} %param.18) | copy-start | bytes 1540
  15.5 21.6 %collective-permute-start.1 = (bf16[1024,256]{1,0:T(8,128)(2,1)S(1)}, bf16[1024,256]{1,0:T(8,128)(2,1)S(1)}, u32[]{:S(2)}, u32[]{:S(2)}) collective-permute-start(bf16[1024,256]{1,0:T(8,128)(2,1)S(1)} %slice_select_fusion.1), channel_id=1, source_target_pairs={{0,16},{9,25},{18,2},{27,11},{8,24},{1,17},{26,10},{19,3},{4,12},{... | collective-permute-start | bytes 1572872 | tf_op jit(solution)/shard_map/ppermute | solution.py:192
  16.8 24.0 %collective-permute-start.5 = (bf16[1024,256]{1,0:T(8,128)(2,1)}, bf16[1024,256]{1,0:T(8,128)(2,1)}, u32[]{:S(2)}, u32[]{:S(2)}) collective-permute-start(bf16[1024,256]{1,0:T(8,128)(2,1)} %slice_select_fusion), channel_id=1, source_target_pairs={{0,16},{9,25},{18,2},{27,11},{8,24},{1,17},{26,10},{19,3},{4,12},{... | collective-permute-start | bytes 1572872 | tf_op jit(solution)/shard_map/ppermute | solution.py:192
  19.0 18.0 %all-to-all-start = ((bf16[8,32,512]{2,1,0:T(8,128)(2,1)}), bf16[8,32,512]{2,1,0:T(8,128)(2,1)S(1)}, u32[]{:S(2)}, u32[]{:S(2)}) async-start(bf16[8,32,512]{2,1,0:T(8,128)(2,1)} %bitcast.37), calls=%async_computation | async-start | bytes 524288 | tf_op jit(solution)/shard_map/all_to_all | solution.py:270
  27.6 11.6 %collective-permute-start.3 = (bf16[1,160,512]{2,1,0:T(8,128)(2,1)S(1)}, bf16[1,160,512]{2,1,0:T(8,128)(2,1)S(1)}, u32[]{:S(2)}, u32[]{:S(2)}) collective-permute-start(bf16[1,160,512]{2,1,0:T(8,128)(2,1)S(1)} %get-tuple-element.56), channel_id=1, source_target_pairs={{0,2},{1,3},{2,0},{3,1},{4,6},{5,7},{6,4},{7,5},{8,10},{9,11},{10,... | collective-permute-start | bytes 491528 | tf_op jit(solution)/shard_map/ppermute | solution.py:37
  40.3 10.2 %collective-permute-start.4 = (bf16[128,640]{1,0:T(8,128)(2,1)S(1)}, bf16[128,640]{1,0:T(8,128)(2,1)S(1)}, u32[]{:S(2)}, u32[]{:S(2)}) collective-permute-start(bf16[128,640]{1,0:T(8,128)(2,1)S(1)} %get-tuple-element.35), channel_id=1, source_target_pairs={{0,2},{1,3},{2,0},{3,1},{4,6},{5,7},{6,4},{7,5},{8,10},{9,11},{10,... | collective-permute-start | bytes 491528 | tf_op jit(solution)/shard_map/ppermute | solution.py:37
  40.8 2.3 %copy-start.7 = (bf16[1024,256]{1,0:T(8,128)(2,1)S(1)}, bf16[1024,256]{1,0:T(8,128)(2,1)}, u32[]{:S(2)}) copy-start(bf16[1024,256]{1,0:T(8,128)(2,1)} %copy-done.6) | copy-start | bytes 1572868
  43.1 7.7 %copy-start = (bf16[512,1024]{1,0:T(8,128)(2,1)S(1)}, bf16[512,1024]{1,0:T(8,128)(2,1)}, u32[]{:S(2)}) copy-start(bf16[512,1024]{1,0:T(8,128)(2,1)} %get-tuple-element.37.kept_ref) | copy-start | bytes 3145732
  43.1 7.7 %collective-permute-start.7 = (bf16[512,256]{1,0:T(8,128)(2,1)}, bf16[512,256]{1,0:T(8,128)(2,1)}, u32[]{:S(2)}, u32[]{:S(2)}) collective-permute-start(bf16[512,256]{1,0:T(8,128)(2,1)} %convolution_convert_fusion.2), channel_id=1, source_target_pairs={{0,4},{4,0},{8,12},{12,8},{16,20},{20,16},{24,28},{28,24},{1,5},{5... | collective-permute-start | bytes 786440 | tf_op jit(solution)/shard_map/ppermute | solution.py:29
  44.2 8.3 %collective-permute-start.10 = (bf16[512,256]{1,0:T(8,128)(2,1)}, bf16[512,256]{1,0:T(8,128)(2,1)}, u32[]{:S(2)}, u32[]{:S(2)}) collective-permute-start(bf16[512,256]{1,0:T(8,128)(2,1)} %convolution_convert_fusion.1), channel_id=1, source_target_pairs={{0,4},{4,0},{8,12},{12,8},{16,20},{20,16},{24,28},{28,24},{1,5},{5... | collective-permute-start | bytes 786440 | tf_op jit(solution)/shard_map/ppermute | solution.py:29
  52.5 6.4 %collective-permute-start.8 = (bf16[256,256]{1,0:T(8,128)(2,1)S(1)}, bf16[256,256]{1,0:T(8,128)(2,1)S(1)}, u32[]{:S(2)}, u32[]{:S(2)}) collective-permute-start(bf16[256,256]{1,0:T(8,128)(2,1)S(1)} %slice.205), channel_id=1, source_target_pairs={{0,1},{1,0},{2,3},{3,2},{4,5},{5,4},{6,7},{7,6},{8,9},{9,8},{10,11... | collective-permute-start | bytes 393224 | tf_op jit(solution)/shard_map/ppermute | solution.py:37
  54.0 7.3 %collective-permute-start.11 = (bf16[256,256]{1,0:T(8,128)(2,1)S(1)}, bf16[256,256]{1,0:T(8,128)(2,1)S(1)}, u32[]{:S(2)}, u32[]{:S(2)}) collective-permute-start(bf16[256,256]{1,0:T(8,128)(2,1)S(1)} %slice.204), channel_id=1, source_target_pairs={{0,1},{1,0},{2,3},{3,2},{4,5},{5,4},{6,7},{7,6},{8,9},{9,8},{10,11... | collective-permute-start | bytes 393224 | tf_op jit(solution)/shard_map/ppermute | solution.py:37
  59.0 10.2 %collective-permute-start.9 = (bf16[256,256]{1,0:T(8,128)(2,1)S(1)}, bf16[256,256]{1,0:T(8,128)(2,1)S(1)}, u32[]{:S(2)}, u32[]{:S(2)}) collective-permute-start(bf16[256,256]{1,0:T(8,128)(2,1)S(1)} %pad_maximum_fusion.4), channel_id=1, source_target_pairs={{0,2},{1,3},{2,0},{3,1},{4,6},{5,7},{6,4},{7,5},{8,10},{9,11},{10,... | collective-permute-start | bytes 393224 | tf_op jit(solution)/shard_map/ppermute | solution.py:37
  61.3 9.3 %collective-permute-start.12 = (bf16[256,256]{1,0:T(8,128)(2,1)S(1)}, bf16[256,256]{1,0:T(8,128)(2,1)S(1)}, u32[]{:S(2)}, u32[]{:S(2)}) collective-permute-start(bf16[256,256]{1,0:T(8,128)(2,1)S(1)} %pad_maximum_fusion.5), channel_id=1, source_target_pairs={{0,2},{1,3},{2,0},{3,1},{4,6},{5,7},{6,4},{7,5},{8,10},{9,11},{10,... | collective-permute-start | bytes 393224 | tf_op jit(solution)/shard_map/ppermute | solution.py:37
  70.8 8.4 %collective-permute-start.13 = (bf16[256,256]{1,0:T(8,128)(2,1)S(1)}, bf16[256,256]{1,0:T(8,128)(2,1)S(1)}, u32[]{:S(2)}, u32[]{:S(2)}) collective-permute-start(bf16[256,256]{1,0:T(8,128)(2,1)S(1)} %get-tuple-element.52), channel_id=1, source_target_pairs={{0,1},{1,0},{2,3},{3,2},{4,5},{5,4},{6,7},{7,6},{8,9},{9,8},{10,11... | collective-permute-start | bytes 393224 | tf_op jit(solution)/shard_map/ppermute | solution.py:37
  71.9 11.3 %all-to-all-start.1 = ((bf16[8,32,512]{2,1,0:T(8,128)(2,1)}), bf16[8,32,512]{2,1,0:T(8,128)(2,1)S(1)}, u32[]{:S(2)}, u32[]{:S(2)}) async-start(bf16[8,32,512]{2,1,0:T(8,128)(2,1)} %bitcast.15), calls=%async_computation.1 | async-start | bytes 524288 | tf_op jit(solution)/shard_map/all_to_all | solution.py:340
  77.3 5.7 %collective-permute-start.15 = (bf16[256,256]{1,0:T(8,128)(2,1)S(1)}, bf16[256,256]{1,0:T(8,128)(2,1)S(1)}, u32[]{:S(2)}, u32[]{:S(2)}) collective-permute-start(bf16[256,256]{1,0:T(8,128)(2,1)S(1)} %get-tuple-element.46), channel_id=1, source_target_pairs={{0,1},{1,0},{2,3},{3,2},{4,5},{5,4},{6,7},{7,6},{8,9},{9,8},{10,11... | collective-permute-start | bytes 393224 | tf_op jit(solution)/shard_map/ppermute | solution.py:37
  79.3 4.0 %collective-permute-start.14 = (bf16[512,256]{1,0:T(8,128)(2,1)S(1)}, bf16[512,256]{1,0:T(8,128)(2,1)S(1)}, u32[]{:S(2)}, u32[]{:S(2)}) collective-permute-start(bf16[512,256]{1,0:T(8,128)(2,1)S(1)} %pad_maximum_fusion.2.slope_ref), channel_id=1, source_target_pairs={{0,4},{4,0},{8,12},{12,8},{16,20},{20,16},{24,28},{28,24},{1,5},{5... | collective-permute-start | bytes 786440 | tf_op jit(solution)/shard_map/ppermute | solution.py:29
  83.0 3.1 %collective-permute-start.16 = (bf16[512,256]{1,0:T(8,128)(2,1)S(1)}, bf16[512,256]{1,0:T(8,128)(2,1)S(1)}, u32[]{:S(2)}, u32[]{:S(2)}) collective-permute-start(bf16[512,256]{1,0:T(8,128)(2,1)S(1)} %constant_dynamic-update-slice_fusion.slope_ref), channel_id=1, source_target_pairs={{0,4},{4,0},{8,12},{12,8},{16,20},{20,16},{24,28},{28,24},{1,5},{5... | collective-permute-start | bytes 786440 | tf_op jit(solution)/shard_map/ppermute | solution.py:29
  84.6 6.4 %collective-permute-start.19 = (bf16[512,256]{1,0:T(8,128)(2,1)S(1)}, bf16[512,256]{1,0:T(8,128)(2,1)S(1)}, u32[]{:S(2)}, u32[]{:S(2)}) collective-permute-start(bf16[512,256]{1,0:T(8,128)(2,1)S(1)} %get-tuple-element.51), channel_id=1, source_target_pairs={{0,8},{4,20},{8,0},{12,28},{16,24},{20,4},{24,16},{28,12},{1,9},{5... | collective-permute-start | bytes 786440 | tf_op jit(solution)/shard_map/ppermute | solution.py:384
  87.6 6.9 %collective-permute-start.17 = (bf16[512,256]{1,0:T(8,128)(2,1)S(1)}, bf16[512,256]{1,0:T(8,128)(2,1)S(1)}, u32[]{:S(2)}, u32[]{:S(2)}) collective-permute-start(bf16[512,256]{1,0:T(8,128)(2,1)S(1)} %get-tuple-element.48), channel_id=1, source_target_pairs={{0,8},{4,20},{8,0},{12,28},{16,24},{20,4},{24,16},{28,12},{1,9},{5... | collective-permute-start | bytes 786440 | tf_op jit(solution)/shard_map/ppermute | solution.py:384
  91.1 5.0 %collective-permute-start.20 = (bf16[256,256]{1,0:T(8,128)(2,1)S(1)}, bf16[256,256]{1,0:T(8,128)(2,1)S(1)}, u32[]{:S(2)}, u32[]{:S(2)}) collective-permute-start(bf16[256,256]{1,0:T(8,128)(2,1)S(1)} %slice.202), channel_id=1, source_target_pairs={{0,16},{4,12},{8,24},{12,4},{16,0},{20,28},{24,8},{28,20},{1,17},{... | collective-permute-start | bytes 393224 | tf_op jit(solution)/shard_map/ppermute | solution.py:384
  94.6 5.0 %collective-permute-start.18 = (bf16[256,256]{1,0:T(8,128)(2,1)S(1)}, bf16[256,256]{1,0:T(8,128)(2,1)S(1)}, u32[]{:S(2)}, u32[]{:S(2)}) collective-permute-start(bf16[256,256]{1,0:T(8,128)(2,1)S(1)} %slice.203), channel_id=1, source_target_pairs={{0,16},{4,12},{8,24},{12,4},{16,0},{20,28},{24,8},{28,20},{1,17},{... | collective-permute-start | bytes 393224 | tf_op jit(solution)/shard_map/ppermute | solution.py:384
  99.7 11.0 %collective-permute-start.21 = (bf16[256,512]{1,0:T(8,128)(2,1)S(1)}, bf16[256,512]{1,0:T(8,128)(2,1)S(1)}, u32[]{:S(2)}, u32[]{:S(2)}) collective-permute-start(bf16[256,512]{1,0:T(8,128)(2,1)S(1)} %pad_maximum_fusion.3), channel_id=1, source_target_pairs={{0,0},{1,10},{2,17},{3,27},{4,4},{5,14},{6,21},{7,31},{8,1},{9,11}... | collective-permute-start | bytes 786440 | tf_op jit(solution)/shard_map/ppermute | solution.py:395
  (2 other events, 3.9 us)
where the time goes:
time: 114 us; the launch traced here: 112 us
  waiting for transfers between devices  44.7 us (39%)
  starting transfers between devices  40.7 us (36%)
  Pallas kernels  11 us (10%)
  matrix products  7.36 us (6%)
  other arithmetic  5.28 us (5%)
  local copies, waits for them, and re-layouts  2.05 us (2%)
    ppermute x9, waiting for transfers between devices, crossed(): return lax.ppermute(array, 'tensor', [(i, i ^ step) for i in range(count)])  25.7 us
    ppermute x9, starting transfers between devices, crossed(): return lax.ppermute(array, 'tensor', [(i, i ^ step) for i in range(count)])  10.7 us
    ppermute x4, waiting for transfers between devices, on_device(): total = total + lax.ppermute(given, 'dp', pairs).astype(F32)  8.54 us
    all_to_all x1, starting transfers between devices, on_device(): got_cot = lax.all_to_all(cot, 'dp', split_axis=0, concat_axis=0, tiled=True)  8.51 us
    pallas_call x1, Pallas kernels, on_device(): pl.pallas_call(functools.partial(prepare_kernel, tensor_count, steps), gr...  7.17 us
    ppermute x1, starting transfers between devices, on_device(): lax.ppermute(jnp.concatenate(grads, axis=1), AXES, pairs).astype(F32)  6.41 us
    dot_general x4, matrix products, dot(): return jnp.dot(a, b, preferred_element_type=F32)  6.4 us
    all_to_all x1, waiting for transfers between devices, on_device(): got_cot = lax.all_to_all(cot, 'dp', split_axis=0, concat_axis=0, tiled=True)  5.9 us
  transfers between devices with their start and end apart: 24, of which 13 were waited for; matrix products, arithmetic and copies ran while one was open for 12% of the time, Pallas kernels for 10%

commit v1 on v0

--- a/solution.py
+++ b/solution.py
@@ -191,7 +191,16 @@
                 is_getter = is_getter | ((core == c) & (relative == (q ^ bit)))
         return lax.ppermute(held, AXES, pairs), is_getter
 
-    first_got, first_getter = stage(0, pol_weight)
+    held, got, is_getter = [], [], []
+    rest = pol_weight
+    for j in range(PARTS):
+        part = rest[:, j * width : (j + 1) * width]
+        if j < PARTS - 1:
+            part, rest = lax.optimization_barrier((part, rest))
+        part_got, part_getter = stage(0, part)
+        held.append(part)
+        got.append(part_got)
+        is_getter.append(part_getter)
 
     steps = 4
     feature_step = block // steps
@@ -240,25 +249,17 @@
         name="prepare",
     )(at, tokens, ref_gain.reshape(1, block), ref_weight, pol_gain.reshape(1, model_width))
     given_rows, kept_rows, ref_kept, ref_sent = prepared
+    got[-1], ref_sent = lax.optimization_barrier((got[-1], ref_sent))
     ref_got = crossed(ref_sent, tensor_count, 1)
     got_rows = swapped(given_rows, dp_count)
 
     cot = cotangent.reshape(slot_count, value_width)
-    held, got, is_getter = [], [], []
     for j in range(PARTS):
-        cols = slice(j * width, (j + 1) * width)
-        part = jnp.where(first_getter, first_got[:, cols], pol_weight[:, cols])
-        if j < PARTS - 1:
-            part, first_got = lax.optimization_barrier((part, first_got))
-        else:
-            part, cot, kept_rows = lax.optimization_barrier((part, cot, kept_rows))
         for number in range(1, levels):
-            part_got, part_getter = stage(number, part)
-            if number < levels - 1:
-                part = jnp.where(part_getter, part_got, part)
-        held.append(part)
-        got.append(part_got)
-        is_getter.append(part_getter)
+            held[j] = jnp.where(is_getter[j], got[j], held[j])
+            if j == PARTS - 1 and number == 1:
+                held[j], cot, kept_rows = lax.optimization_barrier((held[j], cot, kept_rows))
+            got[j], is_getter[j] = stage(number, held[j])
     for level in range(1, levels):
         ref_sum = ref_kept[:, :own_rows].astype(F32) + ref_got[:, :own_rows].astype(F32)
         ref_all = jnp.concatenate(
@@ -280,7 +281,6 @@
 
     smem = pl.BlockSpec(memory_space=pltpu.SMEM)
     vmem = pl.BlockSpec(memory_space=pltpu.VMEM)
-    got[-1], got_cot = lax.optimization_barrier((got[-1], got_cot))
     fixed, pull, row_scale, row_at, terms_sent = pl.pallas_call(
         functools.partial(row_kernel, span_rows, model_width),
         in_specs=[smem] * 3 + [vmem] * 4,
@@ -337,13 +337,12 @@
         slopes.append(slope)
 
     sent = dot_rows(row_at, jnp.concatenate(values, axis=1).astype(BF16)).astype(BF16)
+    slopes[0], sent = lax.optimization_barrier((slopes[0], sent))
     policy_values = lax.all_to_all(sent, "dp", split_axis=0, concat_axis=0, tiled=True)
 
     grad_kept, grad_sent = [], []
     for j in range(PARTS):
         slopes_got = swapped(slopes[j], dp_count)
-        if j == PARTS - 1:
-            slopes_got, policy_values = lax.optimization_barrier((slopes_got, policy_values))
         chunks = pl.pallas_call(
             functools.partial(grad_kernel, factor),
             grid_spec=pltpu.PrefetchScalarGridSpec(

time: 114 us -> 114 us (level)
  starting transfers between devices: 40.7 us -> 26.9 us
  blocking collectives: 0 us -> 11.8 us
  local copies, waits for them, and re-layouts: 2.05 us -> 6.56 us
  waiting for transfers between devices: 44.7 us -> 42.9 us
    all_to_all x0 -> x1, blocking collectives: none -> 11.8 us  [on_device(): lax.all_to_all(sent, 'dp', split_axis=0, concat_axis=0, tiled=True)]
    all_to_all x1, waiting for transfers between devices: 5.9 us -> 0.01 us  [on_device(): got_cot = lax.all_to_all(cot, 'dp', split_axis=0, concat_axis=0, tiled=True)]
    ppermute x9, waiting for transfers between devices: 25.7 us -> 31.2 us  [crossed(): return lax.ppermute(array, 'tensor', [(i, i ^ step) for i in range(count)])]
    all_to_all x1 -> x0, starting transfers between devices: 5.41 us -> none  [on_device(): lax.all_to_all(sent, 'dp', split_axis=0, concat_axis=0, tiled=True)]
    ppermute x1, waiting for transfers between devices: 4.54 us -> 0.01 us  [on_device(): lax.ppermute(jnp.concatenate(grads, axis=1), AXES, pairs).astype(F32)]
    ppermute x1, starting transfers between devices: 6.41 us -> 1.92 us  [on_device(): lax.ppermute(jnp.concatenate(grads, axis=1), AXES, pairs).astype(F32)]
    slice x0 -> x2, local copies, waits for them, and re-layouts: none -> 2.95 us  [on_device(): part = rest[:, j * width:(j + 1) * width]]
    ppermute x4, waiting for transfers between devices: 8.54 us -> 11.1 us  [on_device(): total = total + lax.ppermute(given, 'dp', pairs).astype(F32)]
  transfers between devices with their start and end apart: 24 -> 24, of which waited for: 13 -> 12; matrix products, arithmetic and copies ran while one was open for 12% -> 12% of each run, Pallas kernels for 10% -> 10%
where the time goes in v1:
time: 114 us; the launch traced here: 112 us
  waiting for transfers between devices  42.9 us (38%)
  starting transfers between devices  26.9 us (24%)
  blocking collectives  11.8 us (10%)
  Pallas kernels  11 us (10%)
  matrix products  7.77 us (7%)
  local copies, waits for them, and re-layouts  6.56 us (6%)
  other arithmetic  4.2 us (4%)
    ppermute x9, waiting for transfers between devices, crossed(): return lax.ppermute(array, 'tensor', [(i, i ^ step) for i in range(count)])  31.2 us
    all_to_all x1, blocking collectives, on_device(): lax.all_to_all(sent, 'dp', split_axis=0, concat_axis=0, tiled=True)  11.8 us
    ppermute x4, waiting for transfers between devices, on_device(): total = total + lax.ppermute(given, 'dp', pairs).astype(F32)  11.1 us
    ppermute x9, starting transfers between devices, crossed(): return lax.ppermute(array, 'tensor', [(i, i ^ step) for i in range(count)])  9.5 us
    dot_general x4, matrix products, dot(): return jnp.dot(a, b, preferred_element_type=F32)  7.52 us
    all_to_all x1, starting transfers between devices, on_device(): got_cot = lax.all_to_all(cot, 'dp', split_axis=0, concat_axis=0, tiled=True)  7.35 us
    pallas_call x1, Pallas kernels, on_device(): pl.pallas_call(functools.partial(prepare_kernel, tensor_count, steps), gr...  7.17 us
    ppermute x4, starting transfers between devices, stage(): return (lax.ppermute(held, AXES, pairs), is_getter)  4.71 us
  transfers between devices with their start and end apart: 24, of which 12 were waited for; matrix products, arithmetic and copies ran while one was open for 12% of the time, Pallas kernels for 10%

profile of v1, /device:TPU:4, one launch (start us, length us, event | category | flops | bytes accessed | tf_op | source)
XLA Modules:
  0.0 112.3 jit_solution(12874953624104982744)
XLA Ops:
  0.6 1.1 slice.96
  1.7 1.9 %slice.97 = bf16[1024,256]{1,0:T(8,128)(2,1)} slice(bf16[1024,512]{1,0:T(8,128)(2,1)} %param.14), slice={[0:1024], [256:512]} | slice | bytes 1048576 | tf_op jit(solution)/shard_map/slice | solution.py:197
  4.3 1.5 %collective-permute-start.4 = (bf16[1024,256]{1,0:T(8,128)(2,1)S(1)}, bf16[1024,256]{1,0:T(8,128)(2,1)}, u32[]{:S(2)}, u32[]{:S(2)}) collective-permute-start(bf16[1024,256]{1,0:T(8,128)(2,1)S(1)} %slice.96), channel_id=1, source_target_pairs={{0,8},{9,1},{18,26},{27,19},{4,20},{13,29},{22,6},{31,15}} | collective-permute-start | bytes 1572872 | tf_op jit(solution)/shard_map/ppermute | solution.py:192
  6.4 7.2 %prepare.1 = (bf16[512,1024]{1,0:T(8,128)(2,1)}, bf16[512,1024]{1,0:T(8,128)(2,1)}, bf16[2,144,512]{2,1,0:T(8,128)(2,1)}, bf16[2,144,512]{2,1,0:T(8,128)(2,1)}) custom-call(s32[2]{0:T(128)} %pad_add_fusion.at, bf16[512,2048]{1,0:T(8,128)(2,1)} %x_ref.1, f32[1,2048]{1,0:T(1,128)} %bitcast.41, bf16[2048,512]{1,0:T(8,128)(2,1)} %weight_ref.1, f32[1,8192]{1,0:T(1,128)} %bitcast.38), custom_call_target="tpu_custom_call" | custom-call | flops 1073741824 | bytes 8388608 | tf_op jit(solution)/shard_map/prepare/pallas_call | solution.py:213
  15.5 1.4 %collective-permute-start.1 = (bf16[2,144,512]{2,1,0:T(8,128)(2,1)}, bf16[2,144,512]{2,1,0:T(8,128)(2,1)}, u32[]{:S(2)}, u32[]{:S(2)}) collective-permute-start(bf16[2,144,512]{2,1,0:T(8,128)(2,1)} %get-tuple-element.33), channel_id=1, source_target_pairs={{0,1},{1,0},{2,3},{3,2},{4,5},{5,4},{6,7},{7,6},{8,9},{9,8},{10,11... | collective-permute-start | bytes 884744 | tf_op jit(solution)/shard_map/ppermute | solution.py:37
  17.0 7.3 %all-to-all-start = ((bf16[8,32,512]{2,1,0:T(8,128)(2,1)}), bf16[8,32,512]{2,1,0:T(8,128)(2,1)S(1)}, u32[]{:S(2)}, u32[]{:S(2)}) async-start(bf16[8,32,512]{2,1,0:T(8,128)(2,1)} %bitcast.37), calls=%async_computation | async-start | bytes 524288 | tf_op jit(solution)/shard_map/all_to_all | solution.py:271
  25.2 1.3 %collective-permute-start.5 = (bf16[1024,256]{1,0:T(8,128)(2,1)}, bf16[1024,256]{1,0:T(8,128)(2,1)}, u32[]{:S(2)}, u32[]{:S(2)}) collective-permute-start(bf16[1024,256]{1,0:T(8,128)(2,1)} %broadcast_select_fusion.2), channel_id=1, source_target_pairs={{0,16},{9,25},{18,2},{27,11},{8,24},{1,17},{26,10},{19,3},{4,12},{... | collective-permute-start | bytes 1572872 | tf_op jit(solution)/shard_map/ppermute | solution.py:192
  28.3 4.5 %collective-permute-start.2 = (bf16[1,160,512]{2,1,0:T(8,128)(2,1)S(1)}, bf16[1,160,512]{2,1,0:T(8,128)(2,1)S(1)}, u32[]{:S(2)}, u32[]{:S(2)}) collective-permute-start(bf16[1,160,512]{2,1,0:T(8,128)(2,1)S(1)} %get-tuple-element.56), channel_id=1, source_target_pairs={{0,2},{1,3},{2,0},{3,1},{4,6},{5,7},{6,4},{7,5},{8,10},{9,11},{10,... | collective-permute-start | bytes 491528 | tf_op jit(solution)/shard_map/ppermute | solution.py:37
  32.8 1.3 %collective-permute-start.11 = (bf16[1024,256]{1,0:T(8,128)(2,1)S(1)}, bf16[1024,256]{1,0:T(8,128)(2,1)}, u32[]{:S(2)}, u32[]{:S(2)}) collective-permute-start(bf16[1024,256]{1,0:T(8,128)(2,1)S(1)} %broadcast_select_fusion.3), channel_id=1, source_target_pairs={{0,16},{9,25},{18,2},{27,11},{8,24},{1,17},{26,10},{19,3},{4,12},{... | collective-permute-start | bytes 1572872 | tf_op jit(solution)/shard_map/ppermute | solution.py:192
  34.2 7.8 %collective-permute-done.2 = bf16[1,160,512]{2,1,0:T(8,128)(2,1)S(1)} collective-permute-done((bf16[1,160,512]{2,1,0:T(8,128)(2,1)S(1)}, bf16[1,160,512]{2,1,0:T(8,128)(2,1)S(1)}, u32[]{:S(2)}, u32[]{:S(2)}) %collective-permute-start.2) | collective-permute-done | bytes 163872 | tf_op jit(solution)/shard_map/ppermute | solution.py:37
  42.0 1.1 rows.1
  43.3 2.2 %convolution_convert_fusion.2 = bf16[512,256]{1,0:T(8,128)(2,1)} fusion(bf16[512,1024]{1,0:T(8,128)(2,1)S(1)} %collective-permute-done.6.got_ref, bf16[1024,256]{1,0:T(8,128)(2,1)} %collective-permute-done.5, bf16[1024,256]{1,0:T(8,128)(2,1)} %broadcast_select_fusion.2, pred[]{:T(512)S(6)} %or.19), kind=kOutput, calls=%fused_computation.4 | convolution fusion | flops 268828672 | bytes 2359297 | tf_op jit(solution)/shard_map/dot_general | solution.py:21
  45.7 2.3 %convolution_convert_fusion.1 = bf16[512,256]{1,0:T(8,128)(2,1)} fusion(bf16[512,1024]{1,0:T(8,128)(2,1)S(1)} %collective-permute-done.6.got_ref, bf16[1024,256]{1,0:T(8,128)(2,1)} %collective-permute-done.11, bf16[1024,256]{1,0:T(8,128)(2,1)S(1)} %broadcast_select_fusion.3, pred[]{:T(512)S(6)} %or.19), kind=kOutput, calls=%fused_computation.3 | convolution fusion | flops 268828672 | bytes 2359297 | tf_op jit(solution)/shard_map/dot_general | solution.py:21
  47.9 3.8 %collective-permute-done.3 = bf16[128,640]{1,0:T(8,128)(2,1)S(1)} collective-permute-done((bf16[128,640]{1,0:T(8,128)(2,1)S(1)}, bf16[128,640]{1,0:T(8,128)(2,1)S(1)}, u32[]{:S(2)}, u32[]{:S(2)}) %collective-permute-start.3) | collective-permute-done | bytes 163872 | tf_op jit(solution)/shard_map/ppermute | solution.py:37
  52.1 1.6 %convolution_add_fusion.1 = f32[512,256]{1,0:T(8,128)S(1)} fusion(bf16[512,1024]{1,0:T(8,128)(2,1)S(1)} %copy-done, bf16[512,256]{1,0:T(8,128)(2,1)} %collective-permute-done.7, bf16[1024,256]{1,0:T(8,128)(2,1)} %collective-permute-done.5, bf16[1024,256]{1,0:T(8,128)(2,1)} %broadcast_select_fusion.2, pred[]{:T(512)S(6)} %or.19), kind=kOutput, calls=%fused_computation.1 | convolution fusion | flops 268959744 | bytes 2883585 | tf_op jit(solution)/shard_map/dot_general | solution.py:21
  53.7 1.5 %convolution_add_fusion = f32[512,256]{1,0:T(8,128)S(1)} fusion(bf16[512,1024]{1,0:T(8,128)(2,1)S(1)} %copy-done, bf16[512,256]{1,0:T(8,128)(2,1)S(1)} %collective-permute-done.12, bf16[1024,256]{1,0:T(8,128)(2,1)} %collective-permute-done.11, bf16[1024,256]{1,0:T(8,128)(2,1)S(1)} %broadcast_select_fusion.3, pred[]{:T(512)S(6)} %or.19), kind=kOutput, calls=%fused_computation | convolution fusion | flops 268959744 | bytes 2883585 | tf_op jit(solution)/shard_map/dot_general | solution.py:21
  55.3 2.1 %collective-permute-start.13 = (bf16[256,256]{1,0:T(8,128)(2,1)S(1)}, bf16[256,256]{1,0:T(8,128)(2,1)S(1)}, u32[]{:S(2)}, u32[]{:S(2)}) collective-permute-start(bf16[256,256]{1,0:T(8,128)(2,1)S(1)} %slice.192), channel_id=1, source_target_pairs={{0,1},{1,0},{2,3},{3,2},{4,5},{5,4},{6,7},{7,6},{8,9},{9,8},{10,11... | collective-permute-start | bytes 393224 | tf_op jit(solution)/shard_map/ppermute | solution.py:37
  57.3 2.7 %collective-permute-done.8 = bf16[256,256]{1,0:T(8,128)(2,1)S(1)} collective-permute-done((bf16[256,256]{1,0:T(8,128)(2,1)S(1)}, bf16[256,256]{1,0:T(8,128)(2,1)S(1)}, u32[]{:S(2)}, u32[]{:S(2)}) %collective-permute-start.8) | collective-permute-done | bytes 131104 | tf_op jit(solution)/shard_map/ppermute | solution.py:37
  60.2 1.7 %collective-permute-done.13 = bf16[256,256]{1,0:T(8,128)(2,1)S(1)} collective-permute-done((bf16[256,256]{1,0:T(8,128)(2,1)S(1)}, bf16[256,256]{1,0:T(8,128)(2,1)S(1)}, u32[]{:S(2)}, u32[]{:S(2)}) %collective-permute-start.13) | collective-permute-done | bytes 131104 | tf_op jit(solution)/shard_map/ppermute | solution.py:37
  62.0 1.2 %collective-permute-start.14 = (bf16[256,256]{1,0:T(8,128)(2,1)S(1)}, bf16[256,256]{1,0:T(8,128)(2,1)S(1)}, u32[]{:S(2)}, u32[]{:S(2)}) collective-permute-start(bf16[256,256]{1,0:T(8,128)(2,1)S(1)} %pad_maximum_fusion.6), channel_id=1, source_target_pairs={{0,2},{1,3},{2,0},{3,1},{4,6},{5,7},{6,4},{7,5},{8,10},{9,11},{10,... | collective-permute-start | bytes 393224 | tf_op jit(solution)/shard_map/ppermute | solution.py:37
  63.3 7.4 %collective-permute-done.9 = bf16[256,256]{1,0:T(8,128)(2,1)S(1)} collective-permute-done((bf16[256,256]{1,0:T(8,128)(2,1)S(1)}, bf16[256,256]{1,0:T(8,128)(2,1)S(1)}, u32[]{:S(2)}, u32[]{:S(2)}) %collective-permute-start.9) | collective-permute-done | bytes 131104 | tf_op jit(solution)/shard_map/ppermute | solution.py:37
  70.9 2.4 %collective-permute-done.14 = bf16[256,256]{1,0:T(8,128)(2,1)S(1)} collective-permute-done((bf16[256,256]{1,0:T(8,128)(2,1)S(1)}, bf16[256,256]{1,0:T(8,128)(2,1)S(1)}, u32[]{:S(2)}, u32[]{:S(2)}) %collective-permute-start.14) | collective-permute-done | bytes 131104 | tf_op jit(solution)/shard_map/ppermute | solution.py:37
  73.5 5.3 %collective-permute-done.18 = bf16[256,256]{1,0:T(8,128)(2,1)S(1)} collective-permute-done((bf16[256,256]{1,0:T(8,128)(2,1)S(1)}, bf16[256,256]{1,0:T(8,128)(2,1)S(1)}, u32[]{:S(2)}, u32[]{:S(2)}) %collective-permute-start.18) | collective-permute-done | bytes 131104 | tf_op jit(solution)/shard_map/ppermute | solution.py:37
  80.5 1.4 %gradient.3 = (f32[512,256]{1,0:T(8,128)S(1)}, bf16[512,256]{1,0:T(8,128)(2,1)S(1)}) custom-call(s32[4]{0:T(128)S(1)} %pad_add_fusion.1.at, bf16[512,1024]{1,0:T(8,128)(2,1)S(1)} %copy-done, bf16[512,1024]{1,0:T(8,128)(2,1)S(1)} %collective-permute-done.6.got_ref, bf16[512,256]{1,0:T(8,128)(2,1)S(1)} %pad_maximum_fusion.3.slope_ref, ...), custom_call_target="tpu_custom_call" | custom-call | flops 536870912 | bytes 4194304 | tf_op jit(solution)/shard_map/gradient/pallas_call | solution.py:346
  81.9 1.3 %collective-permute-start.20 = (bf16[512,256]{1,0:T(8,128)(2,1)S(1)}, bf16[512,256]{1,0:T(8,128)(2,1)S(1)}, u32[]{:S(2)}, u32[]{:S(2)}) collective-permute-start(bf16[512,256]{1,0:T(8,128)(2,1)S(1)} %get-tuple-element.51), channel_id=1, source_target_pairs={{0,8},{4,20},{8,0},{12,28},{16,24},{20,4},{24,16},{28,12},{1,9},{5... | collective-permute-start | bytes 786440 | tf_op jit(solution)/shard_map/ppermute | solution.py:383
  83.1 1.4 %gradient.2 = (f32[512,256]{1,0:T(8,128)S(1)}, bf16[512,256]{1,0:T(8,128)(2,1)S(1)}) custom-call(s32[4]{0:T(128)S(1)} %pad_add_fusion.1.at, bf16[512,1024]{1,0:T(8,128)(2,1)S(1)} %copy-done, bf16[512,1024]{1,0:T(8,128)(2,1)S(1)} %collective-permute-done.6.got_ref, bf16[512,256]{1,0:T(8,128)(2,1)S(1)} %pad_maximum_fusion.2.slope_ref, ...), custom_call_target="tpu_custom_call" | custom-call | flops 536870912 | bytes 4194304 | tf_op jit(solution)/shard_map/gradient/pallas_call | solution.py:346
  85.4 2.9 %collective-permute-done.20 = bf16[512,256]{1,0:T(8,128)(2,1)S(1)} collective-permute-done((bf16[512,256]{1,0:T(8,128)(2,1)S(1)}, bf16[512,256]{1,0:T(8,128)(2,1)S(1)}, u32[]{:S(2)}, u32[]{:S(2)}) %collective-permute-start.20) | collective-permute-done | bytes 262176 | tf_op jit(solution)/shard_map/ppermute | solution.py:383
  88.5 3.3 %collective-permute-done.16 = bf16[512,256]{1,0:T(8,128)(2,1)S(1)} collective-permute-done((bf16[512,256]{1,0:T(8,128)(2,1)S(1)}, bf16[512,256]{1,0:T(8,128)(2,1)S(1)}, u32[]{:S(2)}, u32[]{:S(2)}) %collective-permute-start.16) | collective-permute-done | bytes 262176 | tf_op jit(solution)/shard_map/ppermute | solution.py:383
  92.0 1.5 %collective-permute-done.21 = bf16[256,256]{1,0:T(8,128)(2,1)S(1)} collective-permute-done((bf16[256,256]{1,0:T(8,128)(2,1)S(1)}, bf16[256,256]{1,0:T(8,128)(2,1)S(1)}, u32[]{:S(2)}, u32[]{:S(2)}) %collective-permute-start.21) | collective-permute-done | bytes 131104 | tf_op jit(solution)/shard_map/ppermute | solution.py:383
  93.5 3.5 %collective-permute-done.17 = bf16[256,256]{1,0:T(8,128)(2,1)S(1)} collective-permute-done((bf16[256,256]{1,0:T(8,128)(2,1)S(1)}, bf16[256,256]{1,0:T(8,128)(2,1)S(1)}, u32[]{:S(2)}, u32[]{:S(2)}) %collective-permute-start.17) | collective-permute-done | bytes 131104 | tf_op jit(solution)/shard_map/ppermute | solution.py:383
  97.0 1.9 %collective-permute-start.22 = (bf16[256,512]{1,0:T(8,128)(2,1)S(1)}, bf16[256,512]{1,0:T(8,128)(2,1)S(1)}, u32[]{:S(2)}, u32[]{:S(2)}) collective-permute-start(bf16[256,512]{1,0:T(8,128)(2,1)S(1)} %pad_maximum_fusion.4), channel_id=1, source_target_pairs={{0,0},{1,10},{2,17},{3,27},{4,4},{5,14},{6,21},{7,31},{8,1},{9,11}... | collective-permute-start | bytes 786440 | tf_op jit(solution)/shard_map/ppermute | solution.py:394
  98.9 11.8 %all_to_all.20 = bf16[8,32,512]{2,1,0:T(8,128)(2,1)S(1)} all-to-all(bf16[8,32,512]{2,1,0:T(8,128)(2,1)S(1)} %bitcast.35), channel_id=1, replica_groups=mesh['dp'=8,'tensor'=4] {'dp'}, dimensions={0} | all-to-all | bytes 524288 | tf_op jit(solution)/shard_map/all_to_all | solution.py:341
  (84 shorter events, 11.8 us)
Async XLA Ops:
  3.6 11.1 %collective-permute-start = (bf16[1024,256]{1,0:T(8,128)(2,1)}, bf16[1024,256]{1,0:T(8,128)(2,1)S(1)}, u32[]{:S(2)}, u32[]{:S(2)}) collective-permute-start(bf16[1024,256]{1,0:T(8,128)(2,1)} %slice.97), channel_id=1, source_target_pairs={{0,8},{9,1},{18,26},{27,19},{4,20},{13,29},{22,6},{31,15}} | collective-permute-start | bytes 1572872 | tf_op jit(solution)/shard_map/ppermute | solution.py:192
  4.3 20.0 %collective-permute-start.4 = (bf16[1024,256]{1,0:T(8,128)(2,1)S(1)}, bf16[1024,256]{1,0:T(8,128)(2,1)}, u32[]{:S(2)}, u32[]{:S(2)}) collective-permute-start(bf16[1024,256]{1,0:T(8,128)(2,1)S(1)} %slice.96), channel_id=1, source_target_pairs={{0,8},{9,1},{18,26},{27,19},{4,20},{13,29},{22,6},{31,15}} | collective-permute-start | bytes 1572872 | tf_op jit(solution)/shard_map/ppermute | solution.py:192
  6.4 10.5 %copy-start.5 = (bf16[1024,512]{1,0:T(8,128)(2,1)S(1)}, bf16[1024,512]{1,0:T(8,128)(2,1)}, u32[]{:S(2)}) copy-start(bf16[1024,512]{1,0:T(8,128)(2,1)} %param.14) | copy-start | bytes 3145732
  13.6 13.7 %copy-start.7 = (bf16[2,144,512]{2,1,0:T(8,128)(2,1)S(1)}, bf16[2,144,512]{2,1,0:T(8,128)(2,1)}, u32[]{:S(2)}) copy-start(bf16[2,144,512]{2,1,0:T(8,128)(2,1)} %get-tuple-element.32) | copy-start | bytes 884740
  13.6 29.7 %collective-permute-start.6 = (bf16[512,1024]{1,0:T(8,128)(2,1)}, bf16[512,1024]{1,0:T(8,128)(2,1)S(1)}, u32[]{:S(2)}, u32[]{:S(2)}) collective-permute-start(bf16[512,1024]{1,0:T(8,128)(2,1)} %get-tuple-element.39), channel_id=1, source_target_pairs={{0,4},{4,0},{8,12},{12,8},{16,20},{20,16},{24,28},{28,24},{1,5},{5... | collective-permute-start | bytes 3145736 | tf_op jit(solution)/shard_map/ppermute | solution.py:29
  14.7 0.8 copy-start.6
  15.5 11.0 %collective-permute-start.1 = (bf16[2,144,512]{2,1,0:T(8,128)(2,1)}, bf16[2,144,512]{2,1,0:T(8,128)(2,1)}, u32[]{:S(2)}, u32[]{:S(2)}) collective-permute-start(bf16[2,144,512]{2,1,0:T(8,128)(2,1)} %get-tuple-element.33), channel_id=1, source_target_pairs={{0,1},{1,0},{2,3},{3,2},{4,5},{5,4},{6,7},{7,6},{8,9},{9,8},{10,11... | collective-permute-start | bytes 884744 | tf_op jit(solution)/shard_map/ppermute | solution.py:37
  16.9 25.1 %copy-start.1 = (s32[1,1,8]{2,1,0:T(1,128)S(1)}, s32[1,1,8]{2,1,0:T(1,128)}, u32[]{:S(2)}) copy-start(s32[1,1,8]{2,1,0:T(1,128)} %param.15) | copy-start | bytes 100
  16.9 25.1 %copy-start.2 = (s32[1,1,8]{2,1,0:T(1,128)S(1)}, s32[1,1,8]{2,1,0:T(1,128)}, u32[]{:S(2)}) copy-start(s32[1,1,8]{2,1,0:T(1,128)} %param.16) | copy-start | bytes 100
  16.9 25.0 %copy-start.3 = (f32[1,1,8]{2,1,0:T(1,128)S(1)}, f32[1,1,8]{2,1,0:T(1,128)}, u32[]{:S(2)}) copy-start(f32[1,1,8]{2,1,0:T(1,128)} %param.17) | copy-start | bytes 100
  16.9 25.0 %copy-start.4 = (f32[128]{0:T(128)S(1)}, f32[128]{0:T(128)}, u32[]{:S(2)}) copy-start(f32[128]{0:T(128)} %param.18) | copy-start | bytes 1540
  17.0 17.2 %all-to-all-start = ((bf16[8,32,512]{2,1,0:T(8,128)(2,1)}), bf16[8,32,512]{2,1,0:T(8,128)(2,1)S(1)}, u32[]{:S(2)}, u32[]{:S(2)}) async-start(bf16[8,32,512]{2,1,0:T(8,128)(2,1)} %bitcast.37), calls=%async_computation | async-start | bytes 524288 | tf_op jit(solution)/shard_map/all_to_all | solution.py:271
  25.2 18.2 %collective-permute-start.5 = (bf16[1024,256]{1,0:T(8,128)(2,1)}, bf16[1024,256]{1,0:T(8,128)(2,1)}, u32[]{:S(2)}, u32[]{:S(2)}) collective-permute-start(bf16[1024,256]{1,0:T(8,128)(2,1)} %broadcast_select_fusion.2), channel_id=1, source_target_pairs={{0,16},{9,25},{18,2},{27,11},{8,24},{1,17},{26,10},{19,3},{4,12},{... | collective-permute-start | bytes 1572872 | tf_op jit(solution)/shard_map/ppermute | solution.py:192
  28.3 13.7 %collective-permute-start.2 = (bf16[1,160,512]{2,1,0:T(8,128)(2,1)S(1)}, bf16[1,160,512]{2,1,0:T(8,128)(2,1)S(1)}, u32[]{:S(2)}, u32[]{:S(2)}) collective-permute-start(bf16[1,160,512]{2,1,0:T(8,128)(2,1)S(1)} %get-tuple-element.56), channel_id=1, source_target_pairs={{0,2},{1,3},{2,0},{3,1},{4,6},{5,7},{6,4},{7,5},{8,10},{9,11},{10,... | collective-permute-start | bytes 491528 | tf_op jit(solution)/shard_map/ppermute | solution.py:37
  32.8 12.8 %collective-permute-start.11 = (bf16[1024,256]{1,0:T(8,128)(2,1)S(1)}, bf16[1024,256]{1,0:T(8,128)(2,1)}, u32[]{:S(2)}, u32[]{:S(2)}) collective-permute-start(bf16[1024,256]{1,0:T(8,128)(2,1)S(1)} %broadcast_select_fusion.3), channel_id=1, source_target_pairs={{0,16},{9,25},{18,2},{27,11},{8,24},{1,17},{26,10},{19,3},{4,12},{... | collective-permute-start | bytes 1572872 | tf_op jit(solution)/shard_map/ppermute | solution.py:192
  43.1 8.7 %collective-permute-start.3 = (bf16[128,640]{1,0:T(8,128)(2,1)S(1)}, bf16[128,640]{1,0:T(8,128)(2,1)S(1)}, u32[]{:S(2)}, u32[]{:S(2)}) collective-permute-start(bf16[128,640]{1,0:T(8,128)(2,1)S(1)} %get-tuple-element.35), channel_id=1, source_target_pairs={{0,2},{1,3},{2,0},{3,1},{4,6},{5,7},{6,4},{7,5},{8,10},{9,11},{10,... | collective-permute-start | bytes 491528 | tf_op jit(solution)/shard_map/ppermute | solution.py:37
  45.5 6.5 %copy-start = (bf16[512,1024]{1,0:T(8,128)(2,1)S(1)}, bf16[512,1024]{1,0:T(8,128)(2,1)}, u32[]{:S(2)}) copy-start(bf16[512,1024]{1,0:T(8,128)(2,1)} %get-tuple-element.37.kept_ref) | copy-start | bytes 3145732
  45.5 6.5 %collective-permute-start.7 = (bf16[512,256]{1,0:T(8,128)(2,1)}, bf16[512,256]{1,0:T(8,128)(2,1)}, u32[]{:S(2)}, u32[]{:S(2)}) collective-permute-start(bf16[512,256]{1,0:T(8,128)(2,1)} %convolution_convert_fusion.2), channel_id=1, source_target_pairs={{0,4},{4,0},{8,12},{12,8},{16,20},{20,16},{24,28},{28,24},{1,5},{5... | collective-permute-start | bytes 786440 | tf_op jit(solution)/shard_map/ppermute | solution.py:29
  47.9 5.8 %collective-permute-start.12 = (bf16[512,256]{1,0:T(8,128)(2,1)}, bf16[512,256]{1,0:T(8,128)(2,1)S(1)}, u32[]{:S(2)}, u32[]{:S(2)}) collective-permute-start(bf16[512,256]{1,0:T(8,128)(2,1)} %convolution_convert_fusion.1), channel_id=1, source_target_pairs={{0,4},{4,0},{8,12},{12,8},{16,20},{20,16},{24,28},{28,24},{1,5},{5... | collective-permute-start | bytes 786440 | tf_op jit(solution)/shard_map/ppermute | solution.py:29
  53.7 6.4 %collective-permute-start.8 = (bf16[256,256]{1,0:T(8,128)(2,1)S(1)}, bf16[256,256]{1,0:T(8,128)(2,1)S(1)}, u32[]{:S(2)}, u32[]{:S(2)}) collective-permute-start(bf16[256,256]{1,0:T(8,128)(2,1)S(1)} %slice.193), channel_id=1, source_target_pairs={{0,1},{1,0},{2,3},{3,2},{4,5},{5,4},{6,7},{7,6},{8,9},{9,8},{10,11... | collective-permute-start | bytes 393224 | tf_op jit(solution)/shard_map/ppermute | solution.py:37
  55.3 6.7 %collective-permute-start.13 = (bf16[256,256]{1,0:T(8,128)(2,1)S(1)}, bf16[256,256]{1,0:T(8,128)(2,1)S(1)}, u32[]{:S(2)}, u32[]{:S(2)}) collective-permute-start(bf16[256,256]{1,0:T(8,128)(2,1)S(1)} %slice.192), channel_id=1, source_target_pairs={{0,1},{1,0},{2,3},{3,2},{4,5},{5,4},{6,7},{7,6},{8,9},{9,8},{10,11... | collective-permute-start | bytes 393224 | tf_op jit(solution)/shard_map/ppermute | solution.py:37
  60.1 10.5 %collective-permute-start.9 = (bf16[256,256]{1,0:T(8,128)(2,1)S(1)}, bf16[256,256]{1,0:T(8,128)(2,1)S(1)}, u32[]{:S(2)}, u32[]{:S(2)}) collective-permute-start(bf16[256,256]{1,0:T(8,128)(2,1)S(1)} %pad_maximum_fusion.5), channel_id=1, source_target_pairs={{0,2},{1,3},{2,0},{3,1},{4,6},{5,7},{6,4},{7,5},{8,10},{9,11},{10,... | collective-permute-start | bytes 393224 | tf_op jit(solution)/shard_map/ppermute | solution.py:37
  62.0 11.2 %collective-permute-start.14 = (bf16[256,256]{1,0:T(8,128)(2,1)S(1)}, bf16[256,256]{1,0:T(8,128)(2,1)S(1)}, u32[]{:S(2)}, u32[]{:S(2)}) collective-permute-start(bf16[256,256]{1,0:T(8,128)(2,1)S(1)} %pad_maximum_fusion.6), channel_id=1, source_target_pairs={{0,2},{1,3},{2,0},{3,1},{4,6},{5,7},{6,4},{7,5},{8,10},{9,11},{10,... | collective-permute-start | bytes 393224 | tf_op jit(solution)/shard_map/ppermute | solution.py:37
  70.8 8.4 %collective-permute-start.10 = (bf16[256,256]{1,0:T(8,128)(2,1)S(1)}, bf16[256,256]{1,0:T(8,128)(2,1)S(1)}, u32[]{:S(2)}, u32[]{:S(2)}) collective-permute-start(bf16[256,256]{1,0:T(8,128)(2,1)S(1)} %get-tuple-element.40), channel_id=1, source_target_pairs={{0,1},{1,0},{2,3},{3,2},{4,5},{5,4},{6,7},{7,6},{8,9},{9,8},{10,11... | collective-permute-start | bytes 393224 | tf_op jit(solution)/shard_map/ppermute | solution.py:37
  73.4 5.5 %collective-permute-start.18 = (bf16[256,256]{1,0:T(8,128)(2,1)S(1)}, bf16[256,256]{1,0:T(8,128)(2,1)S(1)}, u32[]{:S(2)}, u32[]{:S(2)}) collective-permute-start(bf16[256,256]{1,0:T(8,128)(2,1)S(1)} %get-tuple-element.52), channel_id=1, source_target_pairs={{0,1},{1,0},{2,3},{3,2},{4,5},{5,4},{6,7},{7,6},{8,9},{9,8},{10,11... | collective-permute-start | bytes 393224 | tf_op jit(solution)/shard_map/ppermute | solution.py:37
  78.9 1.6 %collective-permute-start.19 = (bf16[512,256]{1,0:T(8,128)(2,1)S(1)}, bf16[512,256]{1,0:T(8,128)(2,1)S(1)}, u32[]{:S(2)}, u32[]{:S(2)}) collective-permute-start(bf16[512,256]{1,0:T(8,128)(2,1)S(1)} %pad_maximum_fusion.3.slope_ref), channel_id=1, source_target_pairs={{0,4},{4,0},{8,12},{12,8},{16,20},{20,16},{24,28},{28,24},{1,5},{5... | collective-permute-start | bytes 786440 | tf_op jit(solution)/shard_map/ppermute | solution.py:29
  79.2 3.9 %collective-permute-start.15 = (bf16[512,256]{1,0:T(8,128)(2,1)S(1)}, bf16[512,256]{1,0:T(8,128)(2,1)S(1)}, u32[]{:S(2)}, u32[]{:S(2)}) collective-permute-start(bf16[512,256]{1,0:T(8,128)(2,1)S(1)} %pad_maximum_fusion.2.slope_ref), channel_id=1, source_target_pairs={{0,4},{4,0},{8,12},{12,8},{16,20},{20,16},{24,28},{28,24},{1,5},{5... | collective-permute-start | bytes 786440 | tf_op jit(solution)/shard_map/ppermute | solution.py:29
  81.9 6.4 %collective-permute-start.20 = (bf16[512,256]{1,0:T(8,128)(2,1)S(1)}, bf16[512,256]{1,0:T(8,128)(2,1)S(1)}, u32[]{:S(2)}, u32[]{:S(2)}) collective-permute-start(bf16[512,256]{1,0:T(8,128)(2,1)S(1)} %get-tuple-element.51), channel_id=1, source_target_pairs={{0,8},{4,20},{8,0},{12,28},{16,24},{20,4},{24,16},{28,12},{1,9},{5... | collective-permute-start | bytes 786440 | tf_op jit(solution)/shard_map/ppermute | solution.py:383
  84.5 7.3 %collective-permute-start.16 = (bf16[512,256]{1,0:T(8,128)(2,1)S(1)}, bf16[512,256]{1,0:T(8,128)(2,1)S(1)}, u32[]{:S(2)}, u32[]{:S(2)}) collective-permute-start(bf16[512,256]{1,0:T(8,128)(2,1)S(1)} %get-tuple-element.47), channel_id=1, source_target_pairs={{0,8},{4,20},{8,0},{12,28},{16,24},{20,4},{24,16},{28,12},{1,9},{5... | collective-permute-start | bytes 786440 | tf_op jit(solution)/shard_map/ppermute | solution.py:383
  88.4 5.0 %collective-permute-start.21 = (bf16[256,256]{1,0:T(8,128)(2,1)S(1)}, bf16[256,256]{1,0:T(8,128)(2,1)S(1)}, u32[]{:S(2)}, u32[]{:S(2)}) collective-permute-start(bf16[256,256]{1,0:T(8,128)(2,1)S(1)} %slice.190), channel_id=1, source_target_pairs={{0,16},{4,12},{8,24},{12,4},{16,0},{20,28},{24,8},{28,20},{1,17},{... | collective-permute-start | bytes 393224 | tf_op jit(solution)/shard_map/ppermute | solution.py:383
  91.9 5.0 %collective-permute-start.17 = (bf16[256,256]{1,0:T(8,128)(2,1)S(1)}, bf16[256,256]{1,0:T(8,128)(2,1)S(1)}, u32[]{:S(2)}, u32[]{:S(2)}) collective-permute-start(bf16[256,256]{1,0:T(8,128)(2,1)S(1)} %slice.191), channel_id=1, source_target_pairs={{0,16},{4,12},{8,24},{12,4},{16,0},{20,28},{24,8},{28,20},{1,17},{... | collective-permute-start | bytes 393224 | tf_op jit(solution)/shard_map/ppermute | solution.py:383
  97.0 13.8 %collective-permute-start.22 = (bf16[256,512]{1,0:T(8,128)(2,1)S(1)}, bf16[256,512]{1,0:T(8,128)(2,1)S(1)}, u32[]{:S(2)}, u32[]{:S(2)}) collective-permute-start(bf16[256,512]{1,0:T(8,128)(2,1)S(1)} %pad_maximum_fusion.4), channel_id=1, source_target_pairs={{0,0},{1,10},{2,17},{3,27},{4,4},{5,14},{6,21},{7,31},{8,1},{9,11}... | collective-permute-start | bytes 786440 | tf_op jit(solution)/shard_map/ppermute | solution.py:394

commit v2 on v0

--- a/solution.py
+++ b/solution.py
@@ -243,22 +243,13 @@
     ref_got = crossed(ref_sent, tensor_count, 1)
     got_rows = swapped(given_rows, dp_count)
 
+    held, got, is_getter = pol_weight, first_got, first_getter
     cot = cotangent.reshape(slot_count, value_width)
-    held, got, is_getter = [], [], []
-    for j in range(PARTS):
-        cols = slice(j * width, (j + 1) * width)
-        part = jnp.where(first_getter, first_got[:, cols], pol_weight[:, cols])
-        if j < PARTS - 1:
-            part, first_got = lax.optimization_barrier((part, first_got))
-        else:
-            part, cot, kept_rows = lax.optimization_barrier((part, cot, kept_rows))
-        for number in range(1, levels):
-            part_got, part_getter = stage(number, part)
-            if number < levels - 1:
-                part = jnp.where(part_getter, part_got, part)
-        held.append(part)
-        got.append(part_got)
-        is_getter.append(part_getter)
+    for number in range(1, levels):
+        held = jnp.where(is_getter, got, held)
+        if number == 1:
+            held, cot, kept_rows = lax.optimization_barrier((held, cot, kept_rows))
+        got, is_getter = stage(number, held)
     for level in range(1, levels):
         ref_sum = ref_kept[:, :own_rows].astype(F32) + ref_got[:, :own_rows].astype(F32)
         ref_all = jnp.concatenate(
@@ -280,7 +271,11 @@
 
     smem = pl.BlockSpec(memory_space=pltpu.SMEM)
     vmem = pl.BlockSpec(memory_space=pltpu.VMEM)
-    got[-1], got_cot = lax.optimization_barrier((got[-1], got_cot))
+    weight = jnp.where(is_getter, got, held)
+    value_given = dot(got_rows, weight).astype(BF16)
+    value_kept = dot(kept_rows, weight)
+    tied = lax.optimization_barrier((value_given, lengths, bins, advantage, logprob_gap))
+    value_given, lengths, bins, advantage, logprob_gap = tied
     fixed, pull, row_scale, row_at, terms_sent = pl.pallas_call(
         functools.partial(row_kernel, span_rows, model_width),
         in_specs=[smem] * 3 + [vmem] * 4,
@@ -316,9 +311,8 @@
 
     values, slopes = [], []
     for j in range(PARTS):
-        weight = jnp.where(is_getter[j], got[j], held[j])
-        value_given = dot(got_rows, weight).astype(BF16)
-        total = dot(kept_rows, weight) + swapped(value_given, dp_count).astype(F32)
+        cols = slice(j * width, (j + 1) * width)
+        total = value_kept[:, cols] + swapped(value_given[:, cols], dp_count).astype(F32)
         for level in range(levels - 1):
             rows = total.shape[0] // 2
             total = total[:rows] + crossed(
@@ -328,10 +322,11 @@
         total = total + crossed(other, tensor_count, far).astype(F32)
         values.append(total[:own_rows] * row_scale[:, :1])
 
-        cols = slice(j * width, (j + 1) * width)
         slope = (fixed[:, cols] + pull * total).astype(BF16)
         if j < PARTS - 1:
             slope, fixed, pull = lax.optimization_barrier((slope, fixed, pull))
+        else:
+            slope, *values = lax.optimization_barrier((slope, *values))
         for level in reversed(range(levels - 1)):
             slope = jnp.concatenate([slope, crossed(slope, tensor_count, 1 << level)], axis=0)
         slopes.append(slope)

time: 114 us -> 113 us (level)
  waiting for transfers between devices: 44.7 us -> 42.1 us
  starting transfers between devices: 40.7 us -> 42.8 us
    ppermute x9, starting transfers between devices: 10.7 us -> 19.2 us  [crossed(): return lax.ppermute(array, 'tensor', [(i, i ^ step) for i in range(count)])]
    all_to_all x1, starting transfers between devices: 8.51 us -> 3.79 us  [on_device(): got_cot = lax.all_to_all(cot, 'dp', split_axis=0, concat_axis=0, tiled=True)]
    all_to_all x1, waiting for transfers between devices: 5.9 us -> 2.58 us  [on_device(): got_cot = lax.all_to_all(cot, 'dp', split_axis=0, concat_axis=0, tiled=True)]
    ppermute x3 -> x2, starting transfers between devices: 4.24 us -> 2.01 us  [stage(): return (lax.ppermute(held, AXES, pairs), is_getter)]
    select_n x2 -> x1, other arithmetic: 3.03 us -> 1.09 us  [on_device(): held = jnp.where(is_getter, got, held)]
    slice x0 -> x1, local copies, waits for them, and re-layouts: none -> 1.86 us  [on_device(): value_given[:, cols]]
    ppermute x9, waiting for transfers between devices: 25.7 us -> 27 us  [crossed(): return lax.ppermute(array, 'tensor', [(i, i ^ step) for i in range(count)])]
    add x0 -> x1, other arithmetic: none -> 1.31 us  [on_device(): value_kept[:, cols] + swapped(value_given[:, cols], dp_count).astype(F32)]
  transfers between devices with their start and end apart: 24 -> 23, of which waited for: 13 -> 12; matrix products, arithmetic and copies ran while one was open for 12% -> 10% of each run, Pallas kernels for 10% -> 9%
where the time goes in v2:
time: 113 us; the launch traced here: 111 us
  starting transfers between devices  42.8 us (38%)
  waiting for transfers between devices  42.1 us (37%)
  Pallas kernels  11 us (10%)
  matrix products  6.74 us (6%)
  other arithmetic  4.61 us (4%)
  local copies, waits for them, and re-layouts  3.15 us (3%)
    ppermute x9, waiting for transfers between devices, crossed(): return lax.ppermute(array, 'tensor', [(i, i ^ step) for i in range(count)])  27 us
    ppermute x9, starting transfers between devices, crossed(): return lax.ppermute(array, 'tensor', [(i, i ^ step) for i in range(count)])  19.2 us
    ppermute x4, waiting for transfers between devices, on_device(): total = total + lax.ppermute(given, 'dp', pairs).astype(F32)  8.08 us
    pallas_call x1, Pallas kernels, on_device(): pl.pallas_call(functools.partial(prepare_kernel, tensor_count, steps), gr...  7.11 us
    ppermute x1, starting transfers between devices, on_device(): lax.ppermute(jnp.concatenate(grads, axis=1), AXES, pairs).astype(F32)  6.54 us
    dot_general x2, matrix products, dot(): return jnp.dot(a, b, preferred_element_type=F32)  5.78 us
    ppermute x4, starting transfers between devices, on_device(): total = total + lax.ppermute(given, 'dp', pairs).astype(F32)  5.32 us
    all_to_all x1, starting transfers between devices, on_device(): lax.all_to_all(sent, 'dp', split_axis=0, concat_axis=0, tiled=True)  4.79 us
  transfers between devices with their start and end apart: 23, of which 12 were waited for; matrix products, arithmetic and copies ran while one was open for 10% of the time, Pallas kernels for 9%

profile of v2, /device:TPU:4, one launch (start us, length us, event | category | flops | bytes accessed | tf_op | source)
XLA Modules:
  0.0 111.4 jit_solution(277761313390503430)
XLA Ops:
  1.9 7.1 %prepare.1 = (bf16[512,1024]{1,0:T(8,128)(2,1)}, bf16[512,1024]{1,0:T(8,128)(2,1)}, bf16[2,144,512]{2,1,0:T(8,128)(2,1)}, bf16[2,144,512]{2,1,0:T(8,128)(2,1)}) custom-call(s32[2]{0:T(128)} %pad_add_fusion.at, bf16[512,2048]{1,0:T(8,128)(2,1)} %x_ref.1, f32[1,2048]{1,0:T(1,128)} %bitcast.38, bf16[2048,512]{1,0:T(8,128)(2,1)} %weight_ref.1, f32[1,8192]{1,0:T(1,128)} %bitcast.35), custom_call_target="tpu_custom_call" | custom-call | flops 1073741824 | bytes 8388608 | tf_op jit(solution)/shard_map/prepare/pallas_call | solution.py:204
  9.5 1.1 broadcast_select_fusion
  10.6 1.3 %collective-permute-start.2 = (bf16[1024,512]{1,0:T(8,128)(2,1)}, bf16[1024,512]{1,0:T(8,128)(2,1)}, u32[]{:S(2)}, u32[]{:S(2)}) collective-permute-start(bf16[1024,512]{1,0:T(8,128)(2,1)} %broadcast_select_fusion), channel_id=1, source_target_pairs={{0,16},{9,25},{18,2},{27,11},{8,24},{1,17},{26,10},{19,3},{4,12},{... | collective-permute-start | bytes 3145736 | tf_op jit(solution)/shard_map/ppermute | solution.py:192
  11.9 1.3 %collective-permute-start.3 = (bf16[2,144,512]{2,1,0:T(8,128)(2,1)}, bf16[2,144,512]{2,1,0:T(8,128)(2,1)S(1)}, u32[]{:S(2)}, u32[]{:S(2)}) collective-permute-start(bf16[2,144,512]{2,1,0:T(8,128)(2,1)} %get-tuple-element.40), channel_id=1, source_target_pairs={{0,1},{1,0},{2,3},{3,2},{4,5},{5,4},{6,7},{7,6},{8,9},{9,8},{10,11... | collective-permute-start | bytes 884744 | tf_op jit(solution)/shard_map/ppermute | solution.py:37
  13.2 5.7 %collective-permute-done.3 = bf16[2,144,512]{2,1,0:T(8,128)(2,1)S(1)} collective-permute-done((bf16[2,144,512]{2,1,0:T(8,128)(2,1)}, bf16[2,144,512]{2,1,0:T(8,128)(2,1)S(1)}, u32[]{:S(2)}, u32[]{:S(2)}) %collective-permute-start.3) | collective-permute-done | bytes 294944 | tf_op jit(solution)/shard_map/ppermute | solution.py:37
  19.0 12.0 %collective-permute-start.4 = (bf16[1,160,512]{2,1,0:T(8,128)(2,1)S(1)}, bf16[1,160,512]{2,1,0:T(8,128)(2,1)S(1)}, u32[]{:S(2)}, u32[]{:S(2)}) collective-permute-start(bf16[1,160,512]{2,1,0:T(8,128)(2,1)S(1)} %get-tuple-element.68), channel_id=1, source_target_pairs={{0,2},{1,3},{2,0},{3,1},{4,6},{5,7},{6,4},{7,5},{8,10},{9,11},{10,... | collective-permute-start | bytes 491528 | tf_op jit(solution)/shard_map/ppermute | solution.py:37
  31.1 3.8 %all-to-all-start = ((bf16[8,32,512]{2,1,0:T(8,128)(2,1)}), bf16[8,32,512]{2,1,0:T(8,128)(2,1)S(1)}, u32[]{:S(2)}, u32[]{:S(2)}) async-start(bf16[8,32,512]{2,1,0:T(8,128)(2,1)} %bitcast.9), calls=%async_computation | async-start | bytes 524288 | tf_op jit(solution)/shard_map/all_to_all | solution.py:261
  34.9 2.8 %convolution_convert_fusion = bf16[512,512]{1,0:T(8,128)(2,1)} fusion(bf16[512,1024]{1,0:T(8,128)(2,1)S(1)} %collective-permute-done.got_ref, bf16[1024,512]{1,0:T(8,128)(2,1)} %collective-permute-done.2, bf16[1024,512]{1,0:T(8,128)(2,1)} %broadcast_select_fusion, pred[]{:T(512)S(6)} %or.14), kind=kOutput, calls=%fused_computation | convolution fusion | flops 537657344 | bytes 3670017 | tf_op jit(solution)/shard_map/dot_general | solution.py:21
  37.8 2.6 %all-to-all-done = bf16[8,32,512]{2,1,0:T(8,128)(2,1)S(1)} async-done(((bf16[8,32,512]{2,1,0:T(8,128)(2,1)}), bf16[8,32,512]{2,1,0:T(8,128)(2,1)S(1)}, u32[]{:S(2)}, u32[]{:S(2)}) %all-to-all-start) | async-done | bytes 262176 | tf_op jit(solution)/shard_map/all_to_all | solution.py:261
  40.4 1.1 rows.1
  41.7 1.9 %fusion.12 = (bf16[512,256]{1,0:T(8,128)(2,1)}, bf16[512,256]{1,0:T(8,128)(2,1)}) fusion(bf16[512,512]{1,0:T(8,128)(2,1)} %convolution_convert_fusion), kind=kLoop, calls=%fused_computation.50 | loop fusion | bytes 1048576 | tf_op jit(solution)/shard_map/slice | solution.py:315
  44.1 2.9 %fusion = f32[512,512]{1,0:T(8,128)} fusion(bf16[512,1024]{1,0:T(8,128)(2,1)S(1)} %copy-done, bf16[1024,512]{1,0:T(8,128)(2,1)} %collective-permute-done.2, bf16[1024,512]{1,0:T(8,128)(2,1)} %broadcast_select_fusion, pred[]{:T(512)S(6)} %or.14), kind=kOutput, calls=%fused_computation.12 | convolution fusion | flops 537395200 | bytes 4194305 | tf_op jit(solution)/shard_map/dot_general | solution.py:21
  47.2 4.0 %collective-permute-done.5 = bf16[128,640]{1,0:T(8,128)(2,1)S(1)} collective-permute-done((bf16[128,640]{1,0:T(8,128)(2,1)S(1)}, bf16[128,640]{1,0:T(8,128)(2,1)S(1)}, u32[]{:S(2)}, u32[]{:S(2)}) %collective-permute-start.5) | collective-permute-done | bytes 163872 | tf_op jit(solution)/shard_map/ppermute | solution.py:37
  51.4 1.3 %slice_add_fusion = (f32[512,256]{1,0:T(8,128)S(1)}, f32[512,256]{1,0:T(8,128)S(1)}) fusion(f32[512,512]{1,0:T(8,128)} %fusion, bf16[512,256]{1,0:T(8,128)(2,1)S(1)} %collective-permute-done.9, bf16[512,256]{1,0:T(8,128)(2,1)S(1)} %collective-permute-done.6), kind=kLoop, calls=%fused_computation.7 | loop fusion | flops 524288 | bytes 2621440 | tf_op jit(solution)/shard_map/add | solution.py:315
  53.0 2.1 %collective-permute-start.10 = (bf16[256,256]{1,0:T(8,128)(2,1)S(1)}, bf16[256,256]{1,0:T(8,128)(2,1)S(1)}, u32[]{:S(2)}, u32[]{:S(2)}) collective-permute-start(bf16[256,256]{1,0:T(8,128)(2,1)S(1)} %slice.199), channel_id=1, source_target_pairs={{0,1},{1,0},{2,3},{3,2},{4,5},{5,4},{6,7},{7,6},{8,9},{9,8},{10,11... | collective-permute-start | bytes 393224 | tf_op jit(solution)/shard_map/ppermute | solution.py:37
  55.0 3.2 %collective-permute-done.7 = bf16[256,256]{1,0:T(8,128)(2,1)S(1)} collective-permute-done((bf16[256,256]{1,0:T(8,128)(2,1)S(1)}, bf16[256,256]{1,0:T(8,128)(2,1)S(1)}, u32[]{:S(2)}, u32[]{:S(2)}) %collective-permute-start.7) | collective-permute-done | bytes 131104 | tf_op jit(solution)/shard_map/ppermute | solution.py:37
  59.0 2.1 %collective-permute-done.10 = bf16[256,256]{1,0:T(8,128)(2,1)S(1)} collective-permute-done((bf16[256,256]{1,0:T(8,128)(2,1)S(1)}, bf16[256,256]{1,0:T(8,128)(2,1)S(1)}, u32[]{:S(2)}, u32[]{:S(2)}) %collective-permute-start.10) | collective-permute-done | bytes 131104 | tf_op jit(solution)/shard_map/ppermute | solution.py:37
  61.8 7.1 %collective-permute-done.8 = bf16[256,256]{1,0:T(8,128)(2,1)S(1)} collective-permute-done((bf16[256,256]{1,0:T(8,128)(2,1)S(1)}, bf16[256,256]{1,0:T(8,128)(2,1)S(1)}, u32[]{:S(2)}, u32[]{:S(2)}) %collective-permute-start.8) | collective-permute-done | bytes 131104 | tf_op jit(solution)/shard_map/ppermute | solution.py:37
  69.0 1.3 %collective-permute-done.11 = bf16[256,256]{1,0:T(8,128)(2,1)S(1)} collective-permute-done((bf16[256,256]{1,0:T(8,128)(2,1)S(1)}, bf16[256,256]{1,0:T(8,128)(2,1)S(1)}, u32[]{:S(2)}, u32[]{:S(2)}) %collective-permute-start.11) | collective-permute-done | bytes 131104 | tf_op jit(solution)/shard_map/ppermute | solution.py:37
  71.9 4.8 %all-to-all-start.1 = ((bf16[8,32,512]{2,1,0:T(8,128)(2,1)}), bf16[8,32,512]{2,1,0:T(8,128)(2,1)S(1)}, u32[]{:S(2)}, u32[]{:S(2)}) async-start(bf16[8,32,512]{2,1,0:T(8,128)(2,1)} %bitcast.15), calls=%async_computation.1 | async-start | bytes 524288 | tf_op jit(solution)/shard_map/all_to_all | solution.py:335
  76.7 1.7 %collective-permute-start.14 = (bf16[256,256]{1,0:T(8,128)(2,1)S(1)}, bf16[256,256]{1,0:T(8,128)(2,1)S(1)}, u32[]{:S(2)}, u32[]{:S(2)}) collective-permute-start(bf16[256,256]{1,0:T(8,128)(2,1)S(1)} %get-tuple-element.54), channel_id=1, source_target_pairs={{0,1},{1,0},{2,3},{3,2},{4,5},{5,4},{6,7},{7,6},{8,9},{9,8},{10,11... | collective-permute-start | bytes 393224 | tf_op jit(solution)/shard_map/ppermute | solution.py:37
  78.5 3.7 %collective-permute-done.14 = bf16[256,256]{1,0:T(8,128)(2,1)S(1)} collective-permute-done((bf16[256,256]{1,0:T(8,128)(2,1)S(1)}, bf16[256,256]{1,0:T(8,128)(2,1)S(1)}, u32[]{:S(2)}, u32[]{:S(2)}) %collective-permute-start.14) | collective-permute-done | bytes 131104 | tf_op jit(solution)/shard_map/ppermute | solution.py:37
  82.4 1.4 %gradient.3 = (f32[512,256]{1,0:T(8,128)S(1)}, bf16[512,256]{1,0:T(8,128)(2,1)S(1)}) custom-call(s32[4]{0:T(128)S(1)} %pad_add_fusion.1.at, bf16[512,1024]{1,0:T(8,128)(2,1)S(1)} %copy-done, bf16[512,1024]{1,0:T(8,128)(2,1)S(1)} %collective-permute-done.got_ref, bf16[512,256]{1,0:T(8,128)(2,1)S(1)} %constant_dynamic-update-slice_fusion.slope_ref, ...), custom_call_target="tpu_custom_call" | custom-call | flops 536870912 | bytes 4194304 | tf_op jit(solution)/shard_map/gradient/pallas_call | solution.py:342
  83.8 1.5 %collective-permute-start.18 = (bf16[512,256]{1,0:T(8,128)(2,1)S(1)}, bf16[512,256]{1,0:T(8,128)(2,1)S(1)}, u32[]{:S(2)}, u32[]{:S(2)}) collective-permute-start(bf16[512,256]{1,0:T(8,128)(2,1)S(1)} %get-tuple-element.59), channel_id=1, source_target_pairs={{0,8},{4,20},{8,0},{12,28},{16,24},{20,4},{24,16},{28,12},{1,9},{5... | collective-permute-start | bytes 786440 | tf_op jit(solution)/shard_map/ppermute | solution.py:379
  85.4 1.4 %gradient.2 = (f32[512,256]{1,0:T(8,128)S(1)}, bf16[512,256]{1,0:T(8,128)(2,1)S(1)}) custom-call(s32[4]{0:T(128)S(1)} %pad_add_fusion.1.at, bf16[512,1024]{1,0:T(8,128)(2,1)S(1)} %copy-done, bf16[512,1024]{1,0:T(8,128)(2,1)S(1)} %collective-permute-done.got_ref, bf16[512,256]{1,0:T(8,128)(2,1)S(1)} %constant_dynamic-update-slice_fusion.2.slope_ref, ...), custom_call_target="tpu_custom_call" | custom-call | flops 536870912 | bytes 4194304 | tf_op jit(solution)/shard_map/gradient/pallas_call | solution.py:342
  87.4 2.9 %collective-permute-done.18 = bf16[512,256]{1,0:T(8,128)(2,1)S(1)} collective-permute-done((bf16[512,256]{1,0:T(8,128)(2,1)S(1)}, bf16[512,256]{1,0:T(8,128)(2,1)S(1)}, u32[]{:S(2)}, u32[]{:S(2)}) %collective-permute-start.18) | collective-permute-done | bytes 262176 | tf_op jit(solution)/shard_map/ppermute | solution.py:379
  90.3 1.3 %collective-permute-start.19 = (bf16[256,256]{1,0:T(8,128)(2,1)S(1)}, bf16[256,256]{1,0:T(8,128)(2,1)S(1)}, u32[]{:S(2)}, u32[]{:S(2)}) collective-permute-start(bf16[256,256]{1,0:T(8,128)(2,1)S(1)} %slice.197), channel_id=1, source_target_pairs={{0,16},{4,12},{8,24},{12,4},{16,0},{20,28},{24,8},{28,20},{1,17},{... | collective-permute-start | bytes 393224 | tf_op jit(solution)/shard_map/ppermute | solution.py:379
  91.6 2.1 %collective-permute-done.16 = bf16[512,256]{1,0:T(8,128)(2,1)S(1)} collective-permute-done((bf16[512,256]{1,0:T(8,128)(2,1)S(1)}, bf16[512,256]{1,0:T(8,128)(2,1)S(1)}, u32[]{:S(2)}, u32[]{:S(2)}) %collective-permute-start.16) | collective-permute-done | bytes 262176 | tf_op jit(solution)/shard_map/ppermute | solution.py:379
  93.8 1.9 %collective-permute-start.17 = (bf16[256,256]{1,0:T(8,128)(2,1)S(1)}, bf16[256,256]{1,0:T(8,128)(2,1)S(1)}, u32[]{:S(2)}, u32[]{:S(2)}) collective-permute-start(bf16[256,256]{1,0:T(8,128)(2,1)S(1)} %slice.198), channel_id=1, source_target_pairs={{0,16},{4,12},{8,24},{12,4},{16,0},{20,28},{24,8},{28,20},{1,17},{... | collective-permute-start | bytes 393224 | tf_op jit(solution)/shard_map/ppermute | solution.py:379
  95.7 3.1 %collective-permute-done.17 = bf16[256,256]{1,0:T(8,128)(2,1)S(1)} collective-permute-done((bf16[256,256]{1,0:T(8,128)(2,1)S(1)}, bf16[256,256]{1,0:T(8,128)(2,1)S(1)}, u32[]{:S(2)}, u32[]{:S(2)}) %collective-permute-start.17) | collective-permute-done | bytes 131104 | tf_op jit(solution)/shard_map/ppermute | solution.py:379
  98.9 6.5 %collective-permute-start.20 = (bf16[256,512]{1,0:T(8,128)(2,1)S(1)}, bf16[256,512]{1,0:T(8,128)(2,1)S(1)}, u32[]{:S(2)}, u32[]{:S(2)}) collective-permute-start(bf16[256,512]{1,0:T(8,128)(2,1)S(1)} %pad_maximum_fusion.2), channel_id=1, source_target_pairs={{0,0},{1,10},{2,17},{3,27},{4,4},{5,14},{6,21},{7,31},{8,1},{9,11}... | collective-permute-start | bytes 786440 | tf_op jit(solution)/shard_map/ppermute | solution.py:390
  105.4 4.4 %collective-permute-done.20 = bf16[256,512]{1,0:T(8,128)(2,1)S(1)} collective-permute-done((bf16[256,512]{1,0:T(8,128)(2,1)S(1)}, bf16[256,512]{1,0:T(8,128)(2,1)S(1)}, u32[]{:S(2)}, u32[]{:S(2)}) %collective-permute-start.20) | collective-permute-done | bytes 262176 | tf_op jit(solution)/shard_map/ppermute | solution.py:390
  (78 shorter events, 9.1 us)
Async XLA Ops:
  0.6 8.9 %collective-permute-start.1 = (bf16[1024,512]{1,0:T(8,128)(2,1)}, bf16[1024,512]{1,0:T(8,128)(2,1)S(1)}, u32[]{:S(2)}, u32[]{:S(2)}) collective-permute-start(bf16[1024,512]{1,0:T(8,128)(2,1)} %param.14), channel_id=1, source_target_pairs={{0,8},{9,1},{18,26},{27,19},{4,20},{13,29},{22,6},{31,15}} | collective-permute-start | bytes 3145736 | tf_op jit(solution)/shard_map/ppermute | solution.py:192
  1.9 7.6 %copy-start.5 = (bf16[1024,512]{1,0:T(8,128)(2,1)S(1)}, bf16[1024,512]{1,0:T(8,128)(2,1)}, u32[]{:S(2)}) copy-start(bf16[1024,512]{1,0:T(8,128)(2,1)} %param.14) | copy-start | bytes 3145732
  9.1 4.2 %copy-start.6 = (bf16[2,144,512]{2,1,0:T(8,128)(2,1)S(1)}, bf16[2,144,512]{2,1,0:T(8,128)(2,1)}, u32[]{:S(2)}) copy-start(bf16[2,144,512]{2,1,0:T(8,128)(2,1)} %get-tuple-element.39) | copy-start | bytes 884740
  9.1 25.8 %collective-permute-start = (bf16[512,1024]{1,0:T(8,128)(2,1)}, bf16[512,1024]{1,0:T(8,128)(2,1)S(1)}, u32[]{:S(2)}, u32[]{:S(2)}) collective-permute-start(bf16[512,1024]{1,0:T(8,128)(2,1)} %get-tuple-element.31), channel_id=1, source_target_pairs={{0,4},{4,0},{8,12},{12,8},{16,20},{20,16},{24,28},{28,24},{1,5},{5... | collective-permute-start | bytes 3145736 | tf_op jit(solution)/shard_map/ppermute | solution.py:29
  10.6 24.3 %collective-permute-start.2 = (bf16[1024,512]{1,0:T(8,128)(2,1)}, bf16[1024,512]{1,0:T(8,128)(2,1)}, u32[]{:S(2)}, u32[]{:S(2)}) collective-permute-start(bf16[1024,512]{1,0:T(8,128)(2,1)} %broadcast_select_fusion), channel_id=1, source_target_pairs={{0,16},{9,25},{18,2},{27,11},{8,24},{1,17},{26,10},{19,3},{4,12},{... | collective-permute-start | bytes 3145736 | tf_op jit(solution)/shard_map/ppermute | solution.py:192
  11.9 7.0 %collective-permute-start.3 = (bf16[2,144,512]{2,1,0:T(8,128)(2,1)}, bf16[2,144,512]{2,1,0:T(8,128)(2,1)S(1)}, u32[]{:S(2)}, u32[]{:S(2)}) collective-permute-start(bf16[2,144,512]{2,1,0:T(8,128)(2,1)} %get-tuple-element.40), channel_id=1, source_target_pairs={{0,1},{1,0},{2,3},{3,2},{4,5},{5,4},{6,7},{7,6},{8,9},{9,8},{10,11... | collective-permute-start | bytes 884744 | tf_op jit(solution)/shard_map/ppermute | solution.py:37
  19.0 18.7 %collective-permute-start.4 = (bf16[1,160,512]{2,1,0:T(8,128)(2,1)S(1)}, bf16[1,160,512]{2,1,0:T(8,128)(2,1)S(1)}, u32[]{:S(2)}, u32[]{:S(2)}) collective-permute-start(bf16[1,160,512]{2,1,0:T(8,128)(2,1)S(1)} %get-tuple-element.68), channel_id=1, source_target_pairs={{0,2},{1,3},{2,0},{3,1},{4,6},{5,7},{6,4},{7,5},{8,10},{9,11},{10,... | collective-permute-start | bytes 491528 | tf_op jit(solution)/shard_map/ppermute | solution.py:37
  31.1 9.3 %all-to-all-start = ((bf16[8,32,512]{2,1,0:T(8,128)(2,1)}), bf16[8,32,512]{2,1,0:T(8,128)(2,1)S(1)}, u32[]{:S(2)}, u32[]{:S(2)}) async-start(bf16[8,32,512]{2,1,0:T(8,128)(2,1)} %bitcast.9), calls=%async_computation | async-start | bytes 524288 | tf_op jit(solution)/shard_map/all_to_all | solution.py:261
  34.9 5.5 %copy-start.1 = (s32[1,1,8]{2,1,0:T(1,128)S(1)}, s32[1,1,8]{2,1,0:T(1,128)}, u32[]{:S(2)}) copy-start(s32[1,1,8]{2,1,0:T(1,128)} %param.15) | copy-start | bytes 100
  34.9 5.5 %copy-start.2 = (s32[1,1,8]{2,1,0:T(1,128)S(1)}, s32[1,1,8]{2,1,0:T(1,128)}, u32[]{:S(2)}) copy-start(s32[1,1,8]{2,1,0:T(1,128)} %param.16) | copy-start | bytes 100
  34.9 5.5 %copy-start.3 = (f32[1,1,8]{2,1,0:T(1,128)S(1)}, f32[1,1,8]{2,1,0:T(1,128)}, u32[]{:S(2)}) copy-start(f32[1,1,8]{2,1,0:T(1,128)} %param.17) | copy-start | bytes 100
  34.9 5.5 %copy-start.4 = (f32[128]{0:T(128)S(1)}, f32[128]{0:T(128)}, u32[]{:S(2)}) copy-start(f32[128]{0:T(128)} %param.18) | copy-start | bytes 1540
  34.9 9.2 %copy-start = (bf16[512,1024]{1,0:T(8,128)(2,1)S(1)}, bf16[512,1024]{1,0:T(8,128)(2,1)}, u32[]{:S(2)}) copy-start(bf16[512,1024]{1,0:T(8,128)(2,1)} %get-tuple-element.44.kept_ref) | copy-start | bytes 3145732
  41.4 9.7 %collective-permute-start.5 = (bf16[128,640]{1,0:T(8,128)(2,1)S(1)}, bf16[128,640]{1,0:T(8,128)(2,1)S(1)}, u32[]{:S(2)}, u32[]{:S(2)}) collective-permute-start(bf16[128,640]{1,0:T(8,128)(2,1)S(1)} %get-tuple-element.42), channel_id=1, source_target_pairs={{0,2},{1,3},{2,0},{3,1},{4,6},{5,7},{6,4},{7,5},{8,10},{9,11},{10,... | collective-permute-start | bytes 491528 | tf_op jit(solution)/shard_map/ppermute | solution.py:37
  43.6 7.8 %collective-permute-start.9 = (bf16[512,256]{1,0:T(8,128)(2,1)}, bf16[512,256]{1,0:T(8,128)(2,1)S(1)}, u32[]{:S(2)}, u32[]{:S(2)}) collective-permute-start(bf16[512,256]{1,0:T(8,128)(2,1)} %get-tuple-element.66), channel_id=1, source_target_pairs={{0,4},{4,0},{8,12},{12,8},{16,20},{20,16},{24,28},{28,24},{1,5},{5... | collective-permute-start | bytes 786440 | tf_op jit(solution)/shard_map/ppermute | solution.py:29
  43.6 7.8 %collective-permute-start.6 = (bf16[512,256]{1,0:T(8,128)(2,1)}, bf16[512,256]{1,0:T(8,128)(2,1)S(1)}, u32[]{:S(2)}, u32[]{:S(2)}) collective-permute-start(bf16[512,256]{1,0:T(8,128)(2,1)} %get-tuple-element.67), channel_id=1, source_target_pairs={{0,4},{4,0},{8,12},{12,8},{16,20},{20,16},{24,28},{28,24},{1,5},{5... | collective-permute-start | bytes 786440 | tf_op jit(solution)/shard_map/ppermute | solution.py:29
  52.8 5.5 %collective-permute-start.7 = (bf16[256,256]{1,0:T(8,128)(2,1)S(1)}, bf16[256,256]{1,0:T(8,128)(2,1)S(1)}, u32[]{:S(2)}, u32[]{:S(2)}) collective-permute-start(bf16[256,256]{1,0:T(8,128)(2,1)S(1)} %slice.200), channel_id=1, source_target_pairs={{0,1},{1,0},{2,3},{3,2},{4,5},{5,4},{6,7},{7,6},{8,9},{9,8},{10,11... | collective-permute-start | bytes 393224 | tf_op jit(solution)/shard_map/ppermute | solution.py:37
  53.0 8.1 %collective-permute-start.10 = (bf16[256,256]{1,0:T(8,128)(2,1)S(1)}, bf16[256,256]{1,0:T(8,128)(2,1)S(1)}, u32[]{:S(2)}, u32[]{:S(2)}) collective-permute-start(bf16[256,256]{1,0:T(8,128)(2,1)S(1)} %slice.199), channel_id=1, source_target_pairs={{0,1},{1,0},{2,3},{3,2},{4,5},{5,4},{6,7},{7,6},{8,9},{9,8},{10,11... | collective-permute-start | bytes 393224 | tf_op jit(solution)/shard_map/ppermute | solution.py:37
  58.3 10.6 %collective-permute-start.8 = (bf16[256,256]{1,0:T(8,128)(2,1)S(1)}, bf16[256,256]{1,0:T(8,128)(2,1)S(1)}, u32[]{:S(2)}, u32[]{:S(2)}) collective-permute-start(bf16[256,256]{1,0:T(8,128)(2,1)S(1)} %pad_maximum_fusion.3), channel_id=1, source_target_pairs={{0,2},{1,3},{2,0},{3,1},{4,6},{5,7},{6,4},{7,5},{8,10},{9,11},{10,... | collective-permute-start | bytes 393224 | tf_op jit(solution)/shard_map/ppermute | solution.py:37
  61.2 9.2 %collective-permute-start.11 = (bf16[256,256]{1,0:T(8,128)(2,1)S(1)}, bf16[256,256]{1,0:T(8,128)(2,1)S(1)}, u32[]{:S(2)}, u32[]{:S(2)}) collective-permute-start(bf16[256,256]{1,0:T(8,128)(2,1)S(1)} %pad_maximum_fusion.4), channel_id=1, source_target_pairs={{0,2},{1,3},{2,0},{3,1},{4,6},{5,7},{6,4},{7,5},{8,10},{9,11},{10,... | collective-permute-start | bytes 393224 | tf_op jit(solution)/shard_map/ppermute | solution.py:37
  70.5 7.9 %collective-permute-start.12 = (bf16[256,256]{1,0:T(8,128)(2,1)S(1)}, bf16[256,256]{1,0:T(8,128)(2,1)S(1)}, u32[]{:S(2)}, u32[]{:S(2)}) collective-permute-start(bf16[256,256]{1,0:T(8,128)(2,1)S(1)} %get-tuple-element.49), channel_id=1, source_target_pairs={{0,1},{1,0},{2,3},{3,2},{4,5},{5,4},{6,7},{7,6},{8,9},{9,8},{10,11... | collective-permute-start | bytes 393224 | tf_op jit(solution)/shard_map/ppermute | solution.py:37
  71.9 10.5 %all-to-all-start.1 = ((bf16[8,32,512]{2,1,0:T(8,128)(2,1)}), bf16[8,32,512]{2,1,0:T(8,128)(2,1)S(1)}, u32[]{:S(2)}, u32[]{:S(2)}) async-start(bf16[8,32,512]{2,1,0:T(8,128)(2,1)} %bitcast.15), calls=%async_computation.1 | async-start | bytes 524288 | tf_op jit(solution)/shard_map/all_to_all | solution.py:335
  76.7 5.6 %collective-permute-start.14 = (bf16[256,256]{1,0:T(8,128)(2,1)S(1)}, bf16[256,256]{1,0:T(8,128)(2,1)S(1)}, u32[]{:S(2)}, u32[]{:S(2)}) collective-permute-start(bf16[256,256]{1,0:T(8,128)(2,1)S(1)} %get-tuple-element.54), channel_id=1, source_target_pairs={{0,1},{1,0},{2,3},{3,2},{4,5},{5,4},{6,7},{7,6},{8,9},{9,8},{10,11... | collective-permute-start | bytes 393224 | tf_op jit(solution)/shard_map/ppermute | solution.py:37
  78.4 4.0 %collective-permute-start.13 = (bf16[512,256]{1,0:T(8,128)(2,1)S(1)}, bf16[512,256]{1,0:T(8,128)(2,1)S(1)}, u32[]{:S(2)}, u32[]{:S(2)}) collective-permute-start(bf16[512,256]{1,0:T(8,128)(2,1)S(1)} %constant_dynamic-update-slice_fusion.slope_ref), channel_id=1, source_target_pairs={{0,4},{4,0},{8,12},{12,8},{16,20},{20,16},{24,28},{28,24},{1,5},{5... | collective-permute-start | bytes 786440 | tf_op jit(solution)/shard_map/ppermute | solution.py:29
  82.2 3.1 %collective-permute-start.15 = (bf16[512,256]{1,0:T(8,128)(2,1)S(1)}, bf16[512,256]{1,0:T(8,128)(2,1)S(1)}, u32[]{:S(2)}, u32[]{:S(2)}) collective-permute-start(bf16[512,256]{1,0:T(8,128)(2,1)S(1)} %constant_dynamic-update-slice_fusion.2.slope_ref), channel_id=1, source_target_pairs={{0,4},{4,0},{8,12},{12,8},{16,20},{20,16},{24,28},{28,24},{1,5},{5... | collective-permute-start | bytes 786440 | tf_op jit(solution)/shard_map/ppermute | solution.py:29
  83.8 6.4 %collective-permute-start.18 = (bf16[512,256]{1,0:T(8,128)(2,1)S(1)}, bf16[512,256]{1,0:T(8,128)(2,1)S(1)}, u32[]{:S(2)}, u32[]{:S(2)}) collective-permute-start(bf16[512,256]{1,0:T(8,128)(2,1)S(1)} %get-tuple-element.59), channel_id=1, source_target_pairs={{0,8},{4,20},{8,0},{12,28},{16,24},{20,4},{24,16},{28,12},{1,9},{5... | collective-permute-start | bytes 786440 | tf_op jit(solution)/shard_map/ppermute | solution.py:379
  86.8 6.9 %collective-permute-start.16 = (bf16[512,256]{1,0:T(8,128)(2,1)S(1)}, bf16[512,256]{1,0:T(8,128)(2,1)S(1)}, u32[]{:S(2)}, u32[]{:S(2)}) collective-permute-start(bf16[512,256]{1,0:T(8,128)(2,1)S(1)} %get-tuple-element.56), channel_id=1, source_target_pairs={{0,8},{4,20},{8,0},{12,28},{16,24},{20,4},{24,16},{28,12},{1,9},{5... | collective-permute-start | bytes 786440 | tf_op jit(solution)/shard_map/ppermute | solution.py:379
  90.3 5.3 %collective-permute-start.19 = (bf16[256,256]{1,0:T(8,128)(2,1)S(1)}, bf16[256,256]{1,0:T(8,128)(2,1)S(1)}, u32[]{:S(2)}, u32[]{:S(2)}) collective-permute-start(bf16[256,256]{1,0:T(8,128)(2,1)S(1)} %slice.197), channel_id=1, source_target_pairs={{0,16},{4,12},{8,24},{12,4},{16,0},{20,28},{24,8},{28,20},{1,17},{... | collective-permute-start | bytes 393224 | tf_op jit(solution)/shard_map/ppermute | solution.py:379
  93.8 5.0 %collective-permute-start.17 = (bf16[256,256]{1,0:T(8,128)(2,1)S(1)}, bf16[256,256]{1,0:T(8,128)(2,1)S(1)}, u32[]{:S(2)}, u32[]{:S(2)}) collective-permute-start(bf16[256,256]{1,0:T(8,128)(2,1)S(1)} %slice.198), channel_id=1, source_target_pairs={{0,16},{4,12},{8,24},{12,4},{16,0},{20,28},{24,8},{28,20},{1,17},{... | collective-permute-start | bytes 393224 | tf_op jit(solution)/shard_map/ppermute | solution.py:379
  98.9 11.0 %collective-permute-start.20 = (bf16[256,512]{1,0:T(8,128)(2,1)S(1)}, bf16[256,512]{1,0:T(8,128)(2,1)S(1)}, u32[]{:S(2)}, u32[]{:S(2)}) collective-permute-start(bf16[256,512]{1,0:T(8,128)(2,1)S(1)} %pad_maximum_fusion.2), channel_id=1, source_target_pairs={{0,0},{1,10},{2,17},{3,27},{4,4},{5,14},{6,21},{7,31},{8,1},{9,11}... | collective-permute-start | bytes 786440 | tf_op jit(solution)/shard_map/ppermute | solution.py:390

commit v3 on v2

--- a/solution.py
+++ b/solution.py
@@ -245,10 +245,11 @@
 
     held, got, is_getter = pol_weight, first_got, first_getter
     cot = cotangent.reshape(slot_count, value_width)
+    ref_got, cot = lax.optimization_barrier((ref_got, cot))
     for number in range(1, levels):
         held = jnp.where(is_getter, got, held)
         if number == 1:
-            held, cot, kept_rows = lax.optimization_barrier((held, cot, kept_rows))
+            held, kept_rows = lax.optimization_barrier((held, kept_rows))
         got, is_getter = stage(number, held)
     for level in range(1, levels):
         ref_sum = ref_kept[:, :own_rows].astype(F32) + ref_got[:, :own_rows].astype(F32)
@@ -271,11 +272,14 @@
 
     smem = pl.BlockSpec(memory_space=pltpu.SMEM)
     vmem = pl.BlockSpec(memory_space=pltpu.VMEM)
-    weight = jnp.where(is_getter, got, held)
-    value_given = dot(got_rows, weight).astype(BF16)
-    value_kept = dot(kept_rows, weight)
-    tied = lax.optimization_barrier((value_given, lengths, bins, advantage, logprob_gap))
-    value_given, lengths, bins, advantage, logprob_gap = tied
+    value_kept, value_got = [], []
+    for j in range(PARTS):
+        cols = slice(j * width, (j + 1) * width)
+        weight = lax.optimization_barrier(jnp.where(is_getter, got[:, cols], held[:, cols]))
+        value_got.append(swapped(dot(got_rows, weight).astype(BF16), dp_count))
+        value_kept.append(dot(kept_rows, weight))
+    tied = lax.optimization_barrier((value_got[0], lengths, bins, advantage, logprob_gap))
+    value_got[0], lengths, bins, advantage, logprob_gap = tied
     fixed, pull, row_scale, row_at, terms_sent = pl.pallas_call(
         functools.partial(row_kernel, span_rows, model_width),
         in_specs=[smem] * 3 + [vmem] * 4,
@@ -304,20 +308,23 @@
         ref_got[0],
     )
     far = 1 << (levels - 1)
-    terms_got = crossed(terms_sent, tensor_count, far).astype(F32)
-    pull_got = terms_got[:, value_width : value_width + 1] + terms_got[:, -1:]
-    fixed = jnp.concatenate([fixed, terms_got[:, :value_width]], axis=0)
-    pull = jnp.concatenate([pull[:, :1], pull_got], axis=0)
+    terms_got = crossed(terms_sent, tensor_count, far)
 
     values, slopes = [], []
     for j in range(PARTS):
         cols = slice(j * width, (j + 1) * width)
-        total = value_kept[:, cols] + swapped(value_given[:, cols], dp_count).astype(F32)
+        total = value_kept[j] + value_got[j].astype(F32)
         for level in range(levels - 1):
             rows = total.shape[0] // 2
             total = total[:rows] + crossed(
                 total[rows:].astype(BF16), tensor_count, 1 << level
             ).astype(F32)
+        if j == 0:
+            total, terms_got = lax.optimization_barrier((total, terms_got))
+            terms_got = terms_got.astype(F32)
+            pull_got = terms_got[:, value_width : value_width + 1] + terms_got[:, -1:]
+            fixed = jnp.concatenate([fixed, terms_got[:, :value_width]], axis=0)
+            pull = jnp.concatenate([pull[:, :1], pull_got], axis=0)
         other = jnp.concatenate([total[own_rows:], total[:own_rows]], axis=0).astype(BF16)
         total = total + crossed(other, tensor_count, far).astype(F32)
         values.append(total[:own_rows] * row_scale[:, :1])
@@ -332,13 +339,12 @@
         slopes.append(slope)
 
     sent = dot_rows(row_at, jnp.concatenate(values, axis=1).astype(BF16)).astype(BF16)
+    slopes[0], sent = lax.optimization_barrier((slopes[0], sent))
     policy_values = lax.all_to_all(sent, "dp", split_axis=0, concat_axis=0, tiled=True)
 
     grad_kept, grad_sent = [], []
     for j in range(PARTS):
         slopes_got = swapped(slopes[j], dp_count)
-        if j == PARTS - 1:
-            slopes_got, policy_values = lax.optimization_barrier((slopes_got, policy_values))
         chunks = pl.pallas_call(
             functools.partial(grad_kernel, factor),
             grid_spec=pltpu.PrefetchScalarGridSpec(
@@ -378,6 +384,8 @@
             ]
             total = total + lax.ppermute(given, "dp", pairs).astype(F32)
             half_rows = total.shape[0] // 2
+            if j == PARTS - 1 and level == 0:
+                total, policy_values = lax.optimization_barrier((total, policy_values))
             if level < levels - 1:
                 total, given = total[:half_rows], total[half_rows:].astype(BF16)
         grads.append(total.astype(BF16))

time: 113 us -> 117 us (1.035)
  waiting for transfers between devices: 42.1 us -> 47.7 us
  other arithmetic: 4.61 us -> 9.1 us
  starting transfers between devices: 42.8 us -> 38.8 us
  matrix products: 6.74 us -> 3.52 us
    ppermute x9, starting transfers between devices: 19.2 us -> 9.41 us  [crossed(): return lax.ppermute(array, 'tensor', [(i, i ^ step) for i in range(count)])]
    ppermute x5, starting transfers between devices: 1.11 us -> 8.95 us  [swapped(): return lax.ppermute(array, 'dp', [(i, i ^ 1) for i in range(dp_count)])]
    ppermute x9, waiting for transfers between devices: 27 us -> 32.5 us  [crossed(): return lax.ppermute(array, 'tensor', [(i, i ^ step) for i in range(count)])]
    all_to_all x1, waiting for transfers between devices: 0.01 us -> 4.47 us  [on_device(): lax.all_to_all(sent, 'dp', split_axis=0, concat_axis=0, tiled=True)]
    ppermute x4, waiting for transfers between devices: 8.08 us -> 4.38 us  [on_device(): total = total + lax.ppermute(given, 'dp', pairs).astype(F32)]
    dot_general x2 -> x4, matrix products: 5.78 us -> 2.56 us  [dot(): return jnp.dot(a, b, preferred_element_type=F32)]
    all_to_all x1, waiting for transfers between devices: 2.58 us -> 0.01 us  [on_device(): got_cot = lax.all_to_all(cot, 'dp', split_axis=0, concat_axis=0, tiled=True)]
    ppermute x1, starting transfers between devices: 6.54 us -> 4.55 us  [on_device(): lax.ppermute(jnp.concatenate(grads, axis=1), AXES, pairs).astype(F32)]
  transfers between devices with their start and end apart: 23 -> 23, of which waited for: 12 -> 11; matrix products, arithmetic and copies ran while one was open for 10% -> 12% of each run, Pallas kernels for 9% -> 10%
where the time goes in v3:
time: 117 us; the launch traced here: 116 us
  waiting for transfers between devices  47.7 us (41%)
  starting transfers between devices  38.8 us (33%)
  Pallas kernels  11.7 us (10%)
  other arithmetic  9.1 us (8%)
  local copies, waits for them, and re-layouts  3.64 us (3%)
  matrix products  3.52 us (3%)
    ppermute x9, waiting for transfers between devices, crossed(): return lax.ppermute(array, 'tensor', [(i, i ^ step) for i in range(count)])  32.5 us
    ppermute x9, starting transfers between devices, crossed(): return lax.ppermute(array, 'tensor', [(i, i ^ step) for i in range(count)])  9.41 us
    ppermute x5, starting transfers between devices, swapped(): return lax.ppermute(array, 'dp', [(i, i ^ 1) for i in range(dp_count)])  8.95 us
    pallas_call x1, Pallas kernels, on_device(): pl.pallas_call(functools.partial(prepare_kernel, tensor_count, steps), gr...  7.13 us
    ppermute x1, waiting for transfers between devices, on_device(): lax.ppermute(jnp.concatenate(grads, axis=1), AXES, pairs).astype(F32)  6.4 us
    all_to_all x1, starting transfers between devices, on_device(): got_cot = lax.all_to_all(cot, 'dp', split_axis=0, concat_axis=0, tiled=True)  5.5 us
    ppermute x1, starting transfers between devices, on_device(): lax.ppermute(jnp.concatenate(grads, axis=1), AXES, pairs).astype(F32)  4.55 us
    all_to_all x1, waiting for transfers between devices, on_device(): lax.all_to_all(sent, 'dp', split_axis=0, concat_axis=0, tiled=True)  4.47 us
  transfers between devices with their start and end apart: 23, of which 11 were waited for; matrix products, arithmetic and copies ran while one was open for 12% of the time, Pallas kernels for 10%

profile of v3, /device:TPU:4, one launch (start us, length us, event | category | flops | bytes accessed | tf_op | source)
XLA Modules:
  0.0 115.6 jit_solution(11582842518581272419)
XLA Ops:
  2.0 7.1 %prepare.1 = (bf16[512,1024]{1,0:T(8,128)(2,1)}, bf16[512,1024]{1,0:T(8,128)(2,1)}, bf16[2,144,512]{2,1,0:T(8,128)(2,1)}, bf16[2,144,512]{2,1,0:T(8,128)(2,1)}) custom-call(s32[2]{0:T(128)} %pad_add_fusion.1.at, bf16[512,2048]{1,0:T(8,128)(2,1)} %x_ref.1, f32[1,2048]{1,0:T(1,128)} %bitcast.46, bf16[2048,512]{1,0:T(8,128)(2,1)} %weight_ref.1, f32[1,8192]{1,0:T(1,128)} %bitcast.43), custom_call_target="tpu_custom_call" | custom-call | flops 1073741824 | bytes 8388608 | tf_op jit(solution)/shard_map/prepare/pallas_call | solution.py:204
  9.3 1.3 %collective-permute-start.2 = (bf16[1024,512]{1,0:T(8,128)(2,1)S(1)}, bf16[1024,512]{1,0:T(8,128)(2,1)}, u32[]{:S(2)}, u32[]{:S(2)}) collective-permute-start(bf16[1024,512]{1,0:T(8,128)(2,1)S(1)} %broadcast_select_fusion), channel_id=1, source_target_pairs={{0,16},{9,25},{18,2},{27,11},{8,24},{1,17},{26,10},{19,3},{4,12},{... | collective-permute-start | bytes 3145736 | tf_op jit(solution)/shard_map/ppermute | solution.py:192
  10.6 8.0 %collective-permute-start.1 = (bf16[512,1024]{1,0:T(8,128)(2,1)}, bf16[512,1024]{1,0:T(8,128)(2,1)S(1)}, u32[]{:S(2)}, u32[]{:S(2)}) collective-permute-start(bf16[512,1024]{1,0:T(8,128)(2,1)} %get-tuple-element.38), channel_id=1, source_target_pairs={{0,4},{4,0},{8,12},{12,8},{16,20},{20,16},{24,28},{28,24},{1,5},{5... | collective-permute-start | bytes 3145736 | tf_op jit(solution)/shard_map/ppermute | solution.py:29
  18.6 9.1 %collective-permute-done.4 = bf16[2,144,512]{2,1,0:T(8,128)(2,1)S(1)} collective-permute-done((bf16[2,144,512]{2,1,0:T(8,128)(2,1)}, bf16[2,144,512]{2,1,0:T(8,128)(2,1)S(1)}, u32[]{:S(2)}, u32[]{:S(2)}) %collective-permute-start.4) | collective-permute-done | bytes 294944 | tf_op jit(solution)/shard_map/ppermute | solution.py:37
  27.7 5.5 %all-to-all-start = ((bf16[8,32,512]{2,1,0:T(8,128)(2,1)}), bf16[8,32,512]{2,1,0:T(8,128)(2,1)S(1)}, u32[]{:S(2)}, u32[]{:S(2)}) async-start(bf16[8,32,512]{2,1,0:T(8,128)(2,1)} %bitcast.42), calls=%async_computation | async-start | bytes 524288 | tf_op jit(solution)/shard_map/all_to_all | solution.py:262
  33.3 1.3 %slice_select_fusion = (bf16[1024,256]{1,0:T(8,128)(2,1)S(1)}, bf16[1024,256]{1,0:T(8,128)(2,1)S(1)}) fusion(bf16[1024,512]{1,0:T(8,128)(2,1)} %collective-permute-done.2, bf16[1024,512]{1,0:T(8,128)(2,1)S(1)} %broadcast_select_fusion, pred[]{:T(512)S(6)} %or.15), kind=kLoop, calls=%fused_computation.9 | loop fusion | flops 524288 | bytes 3145729 | tf_op jit(solution)/shard_map/jit(_where)/select_n | solution.py:278
  36.3 3.2 %collective-permute-start.5 = (bf16[1,160,512]{2,1,0:T(8,128)(2,1)S(1)}, bf16[1,160,512]{2,1,0:T(8,128)(2,1)S(1)}, u32[]{:S(2)}, u32[]{:S(2)}) collective-permute-start(bf16[1,160,512]{2,1,0:T(8,128)(2,1)S(1)} %get-tuple-element.76), channel_id=1, source_target_pairs={{0,2},{1,3},{2,0},{3,1},{4,6},{5,7},{6,4},{7,5},{8,10},{9,11},{10,... | collective-permute-start | bytes 491528 | tf_op jit(solution)/shard_map/ppermute | solution.py:37
  41.5 1.2 %convolution_add_fusion.1 = f32[512,256]{1,0:T(8,128)} fusion(bf16[512,1024]{1,0:T(8,128)(2,1)S(1)} %copy-done, bf16[1024,256]{1,0:T(8,128)(2,1)S(1)} %get-tuple-element.75, bf16[512,256]{1,0:T(8,128)(2,1)S(1)} %collective-permute-done.3), kind=kOutput, calls=%fused_computation.1 | convolution fusion | flops 268697600 | bytes 2359296 | tf_op jit(solution)/shard_map/dot_general | solution.py:21
  42.7 5.0 %collective-permute-done.5 = bf16[1,160,512]{2,1,0:T(8,128)(2,1)S(1)} collective-permute-done((bf16[1,160,512]{2,1,0:T(8,128)(2,1)S(1)}, bf16[1,160,512]{2,1,0:T(8,128)(2,1)S(1)}, u32[]{:S(2)}, u32[]{:S(2)}) %collective-permute-start.5) | collective-permute-done | bytes 163872 | tf_op jit(solution)/shard_map/ppermute | solution.py:37
  47.7 1.1 rows.1
  48.8 1.0 slice.193
  49.9 3.2 %collective-permute-start.7 = (bf16[128,640]{1,0:T(8,128)(2,1)S(1)}, bf16[128,640]{1,0:T(8,128)(2,1)S(1)}, u32[]{:S(2)}, u32[]{:S(2)}) collective-permute-start(bf16[128,640]{1,0:T(8,128)(2,1)S(1)} %get-tuple-element.50), channel_id=1, source_target_pairs={{0,2},{1,3},{2,0},{3,1},{4,6},{5,7},{6,4},{7,5},{8,10},{9,11},{10,... | collective-permute-start | bytes 491528 | tf_op jit(solution)/shard_map/ppermute | solution.py:37
  53.3 1.1 fusion.4
  55.0 2.4 %collective-permute-done.6 = bf16[256,256]{1,0:T(8,128)(2,1)S(1)} collective-permute-done((bf16[256,256]{1,0:T(8,128)(2,1)S(1)}, bf16[256,256]{1,0:T(8,128)(2,1)S(1)}, u32[]{:S(2)}, u32[]{:S(2)}) %collective-permute-start.6) | collective-permute-done | bytes 131104 | tf_op jit(solution)/shard_map/ppermute | solution.py:37
  57.4 1.0 slice_add_fusion.2
  58.4 5.4 %collective-permute-done.7 = bf16[128,640]{1,0:T(8,128)(2,1)S(1)} collective-permute-done((bf16[128,640]{1,0:T(8,128)(2,1)S(1)}, bf16[128,640]{1,0:T(8,128)(2,1)S(1)}, u32[]{:S(2)}, u32[]{:S(2)}) %collective-permute-start.7) | collective-permute-done | bytes 163872 | tf_op jit(solution)/shard_map/ppermute | solution.py:37
  65.8 7.3 %collective-permute-done.8 = bf16[256,256]{1,0:T(8,128)(2,1)S(1)} collective-permute-done((bf16[256,256]{1,0:T(8,128)(2,1)S(1)}, bf16[256,256]{1,0:T(8,128)(2,1)S(1)}, u32[]{:S(2)}, u32[]{:S(2)}) %collective-permute-start.8) | collective-permute-done | bytes 131104 | tf_op jit(solution)/shard_map/ppermute | solution.py:37
  73.2 1.1 add_convert_fusion.2
  74.8 1.6 %collective-permute-start.15 = (bf16[256,256]{1,0:T(8,128)(2,1)S(1)}, bf16[256,256]{1,0:T(8,128)(2,1)S(1)}, u32[]{:S(2)}, u32[]{:S(2)}) collective-permute-start(bf16[256,256]{1,0:T(8,128)(2,1)S(1)} %get-tuple-element.60), channel_id=1, source_target_pairs={{0,1},{1,0},{2,3},{3,2},{4,5},{5,4},{6,7},{7,6},{8,9},{9,8},{10,11... | collective-permute-start | bytes 393224 | tf_op jit(solution)/shard_map/ppermute | solution.py:37
  76.5 2.9 %collective-permute-done.12 = bf16[256,256]{1,0:T(8,128)(2,1)S(1)} collective-permute-done((bf16[256,256]{1,0:T(8,128)(2,1)S(1)}, bf16[256,256]{1,0:T(8,128)(2,1)S(1)}, u32[]{:S(2)}, u32[]{:S(2)}) %collective-permute-start.12) | collective-permute-done | bytes 131104 | tf_op jit(solution)/shard_map/ppermute | solution.py:37
  79.5 1.0 convolution_convert_fusion
  81.1 2.1 %gradient.2 = (f32[512,256]{1,0:T(8,128)S(1)}, bf16[512,256]{1,0:T(8,128)(2,1)}) custom-call(s32[4]{0:T(128)S(1)} %pad_add_fusion.at, bf16[512,1024]{1,0:T(8,128)(2,1)S(1)} %copy-done, bf16[512,1024]{1,0:T(8,128)(2,1)S(1)} %collective-permute-done.1.got_ref, bf16[512,256]{1,0:T(8,128)(2,1)S(1)} %constant_dynamic-update-slice_fusion.slope_ref, ...), custom_call_target="tpu_custom_call" | custom-call | flops 536870912 | bytes 4194304 | tf_op jit(solution)/shard_map/gradient/pallas_call | solution.py:348
  83.2 1.4 %collective-permute-start.14 = (bf16[512,256]{1,0:T(8,128)(2,1)}, bf16[512,256]{1,0:T(8,128)(2,1)}, u32[]{:S(2)}, u32[]{:S(2)}) collective-permute-start(bf16[512,256]{1,0:T(8,128)(2,1)} %get-tuple-element.59), channel_id=1, source_target_pairs={{0,8},{4,20},{8,0},{12,28},{16,24},{20,4},{24,16},{28,12},{1,9},{5... | collective-permute-start | bytes 786440 | tf_op jit(solution)/shard_map/ppermute | solution.py:385
  84.6 1.4 %gradient.3 = (f32[512,256]{1,0:T(8,128)S(1)}, bf16[512,256]{1,0:T(8,128)(2,1)S(1)}) custom-call(s32[4]{0:T(128)S(1)} %pad_add_fusion.at, bf16[512,1024]{1,0:T(8,128)(2,1)S(1)} %copy-done, bf16[512,1024]{1,0:T(8,128)(2,1)S(1)} %collective-permute-done.1.got_ref, bf16[512,256]{1,0:T(8,128)(2,1)S(1)} %pad_maximum_fusion.2.slope_ref, ...), custom_call_target="tpu_custom_call" | custom-call | flops 536870912 | bytes 4194304 | tf_op jit(solution)/shard_map/gradient/pallas_call | solution.py:348
  86.7 4.1 %all-to-all-start.1 = ((bf16[8,32,512]{2,1,0:T(8,128)(2,1)}), bf16[8,32,512]{2,1,0:T(8,128)(2,1)S(1)}, u32[]{:S(2)}, u32[]{:S(2)}) async-start(bf16[8,32,512]{2,1,0:T(8,128)(2,1)} %bitcast.40), calls=%async_computation.1 | async-start | bytes 524288 | tf_op jit(solution)/shard_map/all_to_all | solution.py:343
  90.9 1.0 convert_add_fusion.1
  91.9 4.5 %all-to-all-done.1 = bf16[8,32,512]{2,1,0:T(8,128)(2,1)S(1)} async-done(((bf16[8,32,512]{2,1,0:T(8,128)(2,1)}), bf16[8,32,512]{2,1,0:T(8,128)(2,1)S(1)}, u32[]{:S(2)}, u32[]{:S(2)}) %all-to-all-start.1) | async-done | bytes 262176 | tf_op jit(solution)/shard_map/all_to_all | solution.py:343
  96.3 1.5 %collective-permute-start.19 = (bf16[256,256]{1,0:T(8,128)(2,1)S(1)}, bf16[256,256]{1,0:T(8,128)(2,1)S(1)}, u32[]{:S(2)}, u32[]{:S(2)}) collective-permute-start(bf16[256,256]{1,0:T(8,128)(2,1)S(1)} %slice.190), channel_id=1, source_target_pairs={{0,16},{4,12},{8,24},{12,4},{16,0},{20,28},{24,8},{28,20},{1,17},{... | collective-permute-start | bytes 393224 | tf_op jit(solution)/shard_map/ppermute | solution.py:385
  98.6 2.8 %collective-permute-done.19 = bf16[256,256]{1,0:T(8,128)(2,1)S(1)} collective-permute-done((bf16[256,256]{1,0:T(8,128)(2,1)S(1)}, bf16[256,256]{1,0:T(8,128)(2,1)S(1)}, u32[]{:S(2)}, u32[]{:S(2)}) %collective-permute-start.19) | collective-permute-done | bytes 131104 | tf_op jit(solution)/shard_map/ppermute | solution.py:385
  101.4 1.6 %collective-permute-done.18 = bf16[256,256]{1,0:T(8,128)(2,1)S(1)} collective-permute-done((bf16[256,256]{1,0:T(8,128)(2,1)S(1)}, bf16[256,256]{1,0:T(8,128)(2,1)S(1)}, u32[]{:S(2)}, u32[]{:S(2)}) %collective-permute-start.18) | collective-permute-done | bytes 131104 | tf_op jit(solution)/shard_map/ppermute | solution.py:385
  103.0 4.6 %collective-permute-start.20 = (bf16[256,512]{1,0:T(8,128)(2,1)S(1)}, bf16[256,512]{1,0:T(8,128)(2,1)S(1)}, u32[]{:S(2)}, u32[]{:S(2)}) collective-permute-start(bf16[256,512]{1,0:T(8,128)(2,1)S(1)} %pad_maximum_fusion.3), channel_id=1, source_target_pairs={{0,0},{1,10},{2,17},{3,27},{4,4},{5,14},{6,21},{7,31},{8,1},{9,11}... | collective-permute-start | bytes 786440 | tf_op jit(solution)/shard_map/ppermute | solution.py:398
  107.6 6.4 %collective-permute-done.20 = bf16[256,512]{1,0:T(8,128)(2,1)S(1)} collective-permute-done((bf16[256,512]{1,0:T(8,128)(2,1)S(1)}, bf16[256,512]{1,0:T(8,128)(2,1)S(1)}, u32[]{:S(2)}, u32[]{:S(2)}) %collective-permute-start.20) | collective-permute-done | bytes 262176 | tf_op jit(solution)/shard_map/ppermute | solution.py:398
  (86 shorter events, 12.3 us)
Async XLA Ops:
  0.6 8.5 %collective-permute-start = (bf16[1024,512]{1,0:T(8,128)(2,1)}, bf16[1024,512]{1,0:T(8,128)(2,1)S(1)}, u32[]{:S(2)}, u32[]{:S(2)}) collective-permute-start(bf16[1024,512]{1,0:T(8,128)(2,1)} %param.14), channel_id=1, source_target_pairs={{0,8},{9,1},{18,26},{27,19},{4,20},{13,29},{22,6},{31,15}} | collective-permute-start | bytes 3145736 | tf_op jit(solution)/shard_map/ppermute | solution.py:192
  2.0 7.2 %copy-start.7 = (bf16[1024,512]{1,0:T(8,128)(2,1)S(1)}, bf16[1024,512]{1,0:T(8,128)(2,1)}, u32[]{:S(2)}) copy-start(bf16[1024,512]{1,0:T(8,128)(2,1)} %param.14) | copy-start | bytes 3145732
  9.1 9.5 %copy-start.8 = (bf16[2,144,512]{2,1,0:T(8,128)(2,1)S(1)}, bf16[2,144,512]{2,1,0:T(8,128)(2,1)}, u32[]{:S(2)}) copy-start(bf16[2,144,512]{2,1,0:T(8,128)(2,1)} %get-tuple-element.46) | copy-start | bytes 884740
  9.3 24.0 %collective-permute-start.2 = (bf16[1024,512]{1,0:T(8,128)(2,1)S(1)}, bf16[1024,512]{1,0:T(8,128)(2,1)}, u32[]{:S(2)}, u32[]{:S(2)}) collective-permute-start(bf16[1024,512]{1,0:T(8,128)(2,1)S(1)} %broadcast_select_fusion), channel_id=1, source_target_pairs={{0,16},{9,25},{18,2},{27,11},{8,24},{1,17},{26,10},{19,3},{4,12},{... | collective-permute-start | bytes 3145736 | tf_op jit(solution)/shard_map/ppermute | solution.py:192
  10.6 24.1 %collective-permute-start.1 = (bf16[512,1024]{1,0:T(8,128)(2,1)}, bf16[512,1024]{1,0:T(8,128)(2,1)S(1)}, u32[]{:S(2)}, u32[]{:S(2)}) collective-permute-start(bf16[512,1024]{1,0:T(8,128)(2,1)} %get-tuple-element.38), channel_id=1, source_target_pairs={{0,4},{4,0},{8,12},{12,8},{16,20},{20,16},{24,28},{28,24},{1,5},{5... | collective-permute-start | bytes 3145736 | tf_op jit(solution)/shard_map/ppermute | solution.py:29
  18.6 9.1 %collective-permute-start.4 = (bf16[2,144,512]{2,1,0:T(8,128)(2,1)}, bf16[2,144,512]{2,1,0:T(8,128)(2,1)S(1)}, u32[]{:S(2)}, u32[]{:S(2)}) collective-permute-start(bf16[2,144,512]{2,1,0:T(8,128)(2,1)} %get-tuple-element.44), channel_id=1, source_target_pairs={{0,1},{1,0},{2,3},{3,2},{4,5},{5,4},{6,7},{7,6},{8,9},{9,8},{10,11... | collective-permute-start | bytes 884744 | tf_op jit(solution)/shard_map/ppermute | solution.py:37
  27.7 6.9 %copy-start.9 = (bf16[2,144,512]{2,1,0:T(8,128)(2,1)}, bf16[2,144,512]{2,1,0:T(8,128)(2,1)S(1)}, u32[]{:S(2)}) copy-start(bf16[2,144,512]{2,1,0:T(8,128)(2,1)S(1)} %collective-permute-done.4) | copy-start | bytes 884740
  27.7 19.9 %all-to-all-start = ((bf16[8,32,512]{2,1,0:T(8,128)(2,1)}), bf16[8,32,512]{2,1,0:T(8,128)(2,1)S(1)}, u32[]{:S(2)}, u32[]{:S(2)}) async-start(bf16[8,32,512]{2,1,0:T(8,128)(2,1)} %bitcast.42), calls=%async_computation | async-start | bytes 524288 | tf_op jit(solution)/shard_map/all_to_all | solution.py:262
  35.1 4.5 %copy-start = (bf16[512,1024]{1,0:T(8,128)(2,1)S(1)}, bf16[512,1024]{1,0:T(8,128)(2,1)}, u32[]{:S(2)}) copy-start(bf16[512,1024]{1,0:T(8,128)(2,1)} %get-tuple-element.37.kept_ref) | copy-start | bytes 3145732
  35.1 4.4 %collective-permute-start.3 = (bf16[512,256]{1,0:T(8,128)(2,1)S(1)}, bf16[512,256]{1,0:T(8,128)(2,1)S(1)}, u32[]{:S(2)}, u32[]{:S(2)}) collective-permute-start(bf16[512,256]{1,0:T(8,128)(2,1)S(1)} %convolution_convert_fusion.2), channel_id=1, source_target_pairs={{0,4},{4,0},{8,12},{12,8},{16,20},{20,16},{24,28},{28,24},{1,5},{5... | collective-permute-start | bytes 786440 | tf_op jit(solution)/shard_map/ppermute | solution.py:29
  35.8 3.8 %collective-permute-start.9 = (bf16[512,256]{1,0:T(8,128)(2,1)S(1)}, bf16[512,256]{1,0:T(8,128)(2,1)S(1)}, u32[]{:S(2)}, u32[]{:S(2)}) collective-permute-start(bf16[512,256]{1,0:T(8,128)(2,1)S(1)} %convolution_convert_fusion.1), channel_id=1, source_target_pairs={{0,4},{4,0},{8,12},{12,8},{16,20},{20,16},{24,28},{28,24},{1,5},{5... | collective-permute-start | bytes 786440 | tf_op jit(solution)/shard_map/ppermute | solution.py:29
  36.3 11.4 %copy-start.1 = (s32[1,1,8]{2,1,0:T(1,128)S(1)}, s32[1,1,8]{2,1,0:T(1,128)}, u32[]{:S(2)}) copy-start(s32[1,1,8]{2,1,0:T(1,128)} %param.15) | copy-start | bytes 100
  36.3 11.4 %copy-start.2 = (s32[1,1,8]{2,1,0:T(1,128)S(1)}, s32[1,1,8]{2,1,0:T(1,128)}, u32[]{:S(2)}) copy-start(s32[1,1,8]{2,1,0:T(1,128)} %param.16) | copy-start | bytes 100
  36.3 11.4 %copy-start.3 = (f32[1,1,8]{2,1,0:T(1,128)S(1)}, f32[1,1,8]{2,1,0:T(1,128)}, u32[]{:S(2)}) copy-start(f32[1,1,8]{2,1,0:T(1,128)} %param.17) | copy-start | bytes 100
  36.3 11.4 %copy-start.4 = (f32[128]{0:T(128)S(1)}, f32[128]{0:T(128)}, u32[]{:S(2)}) copy-start(f32[128]{0:T(128)} %param.18) | copy-start | bytes 1540
  36.3 11.4 %collective-permute-start.5 = (bf16[1,160,512]{2,1,0:T(8,128)(2,1)S(1)}, bf16[1,160,512]{2,1,0:T(8,128)(2,1)S(1)}, u32[]{:S(2)}, u32[]{:S(2)}) collective-permute-start(bf16[1,160,512]{2,1,0:T(8,128)(2,1)S(1)} %get-tuple-element.76), channel_id=1, source_target_pairs={{0,2},{1,3},{2,0},{3,1},{4,6},{5,7},{6,4},{7,5},{8,10},{9,11},{10,... | collective-permute-start | bytes 491528 | tf_op jit(solution)/shard_map/ppermute | solution.py:37
  40.8 12.5 %collective-permute-start.10 = (bf16[256,256]{1,0:T(8,128)(2,1)}, bf16[256,256]{1,0:T(8,128)(2,1)}, u32[]{:S(2)}, u32[]{:S(2)}) collective-permute-start(bf16[256,256]{1,0:T(8,128)(2,1)} %slice.192), channel_id=1, source_target_pairs={{0,1},{1,0},{2,3},{3,2},{4,5},{5,4},{6,7},{7,6},{8,9},{9,8},{10,11... | collective-permute-start | bytes 393224 | tf_op jit(solution)/shard_map/ppermute | solution.py:37
  49.8 7.6 %collective-permute-start.6 = (bf16[256,256]{1,0:T(8,128)(2,1)S(1)}, bf16[256,256]{1,0:T(8,128)(2,1)S(1)}, u32[]{:S(2)}, u32[]{:S(2)}) collective-permute-start(bf16[256,256]{1,0:T(8,128)(2,1)S(1)} %slice.193), channel_id=1, source_target_pairs={{0,1},{1,0},{2,3},{3,2},{4,5},{5,4},{6,7},{7,6},{8,9},{9,8},{10,11... | collective-permute-start | bytes 393224 | tf_op jit(solution)/shard_map/ppermute | solution.py:37
  49.9 13.9 %collective-permute-start.7 = (bf16[128,640]{1,0:T(8,128)(2,1)S(1)}, bf16[128,640]{1,0:T(8,128)(2,1)S(1)}, u32[]{:S(2)}, u32[]{:S(2)}) collective-permute-start(bf16[128,640]{1,0:T(8,128)(2,1)S(1)} %get-tuple-element.50), channel_id=1, source_target_pairs={{0,2},{1,3},{2,0},{3,1},{4,6},{5,7},{6,4},{7,5},{8,10},{9,11},{10,... | collective-permute-start | bytes 491528 | tf_op jit(solution)/shard_map/ppermute | solution.py:37
  55.0 18.2 %collective-permute-start.11 = (bf16[256,256]{1,0:T(8,128)(2,1)}, bf16[256,256]{1,0:T(8,128)(2,1)}, u32[]{:S(2)}, u32[]{:S(2)}) collective-permute-start(bf16[256,256]{1,0:T(8,128)(2,1)} %pad_maximum_fusion.5), channel_id=1, source_target_pairs={{0,2},{1,3},{2,0},{3,1},{4,6},{5,7},{6,4},{7,5},{8,10},{9,11},{10,... | collective-permute-start | bytes 393224 | tf_op jit(solution)/shard_map/ppermute | solution.py:37
  58.4 14.8 %copy-start.6 = (f32[512,256]{1,0:T(8,128)S(1)}, f32[512,256]{1,0:T(8,128)}, u32[]{:S(2)}) copy-start(f32[512,256]{1,0:T(8,128)} %copy-done.5) | copy-start | bytes 1572868
  65.6 7.4 %collective-permute-start.8 = (bf16[256,256]{1,0:T(8,128)(2,1)S(1)}, bf16[256,256]{1,0:T(8,128)(2,1)S(1)}, u32[]{:S(2)}, u32[]{:S(2)}) collective-permute-start(bf16[256,256]{1,0:T(8,128)(2,1)S(1)} %pad_maximum_fusion.4), channel_id=1, source_target_pairs={{0,2},{1,3},{2,0},{3,1},{4,6},{5,7},{6,4},{7,5},{8,10},{9,11},{10,... | collective-permute-start | bytes 393224 | tf_op jit(solution)/shard_map/ppermute | solution.py:37
  74.4 5.0 %collective-permute-start.12 = (bf16[256,256]{1,0:T(8,128)(2,1)S(1)}, bf16[256,256]{1,0:T(8,128)(2,1)S(1)}, u32[]{:S(2)}, u32[]{:S(2)}) collective-permute-start(bf16[256,256]{1,0:T(8,128)(2,1)S(1)} %get-tuple-element.57), channel_id=1, source_target_pairs={{0,1},{1,0},{2,3},{3,2},{4,5},{5,4},{6,7},{7,6},{8,9},{9,8},{10,11... | collective-permute-start | bytes 393224 | tf_op jit(solution)/shard_map/ppermute | solution.py:37
  74.8 6.0 %collective-permute-start.15 = (bf16[256,256]{1,0:T(8,128)(2,1)S(1)}, bf16[256,256]{1,0:T(8,128)(2,1)S(1)}, u32[]{:S(2)}, u32[]{:S(2)}) collective-permute-start(bf16[256,256]{1,0:T(8,128)(2,1)S(1)} %get-tuple-element.60), channel_id=1, source_target_pairs={{0,1},{1,0},{2,3},{3,2},{4,5},{5,4},{6,7},{7,6},{8,9},{9,8},{10,11... | collective-permute-start | bytes 393224 | tf_op jit(solution)/shard_map/ppermute | solution.py:37
  79.4 1.7 %collective-permute-start.13 = (bf16[512,256]{1,0:T(8,128)(2,1)S(1)}, bf16[512,256]{1,0:T(8,128)(2,1)S(1)}, u32[]{:S(2)}, u32[]{:S(2)}) collective-permute-start(bf16[512,256]{1,0:T(8,128)(2,1)S(1)} %constant_dynamic-update-slice_fusion.slope_ref), channel_id=1, source_target_pairs={{0,4},{4,0},{8,12},{12,8},{16,20},{20,16},{24,28},{28,24},{1,5},{5... | collective-permute-start | bytes 786440 | tf_op jit(solution)/shard_map/ppermute | solution.py:29
  80.8 3.8 %collective-permute-start.16 = (bf16[512,256]{1,0:T(8,128)(2,1)S(1)}, bf16[512,256]{1,0:T(8,128)(2,1)S(1)}, u32[]{:S(2)}, u32[]{:S(2)}) collective-permute-start(bf16[512,256]{1,0:T(8,128)(2,1)S(1)} %pad_maximum_fusion.2.slope_ref), channel_id=1, source_target_pairs={{0,4},{4,0},{8,12},{12,8},{16,20},{20,16},{24,28},{28,24},{1,5},{5... | collective-permute-start | bytes 786440 | tf_op jit(solution)/shard_map/ppermute | solution.py:29
  83.2 7.6 %collective-permute-start.14 = (bf16[512,256]{1,0:T(8,128)(2,1)}, bf16[512,256]{1,0:T(8,128)(2,1)}, u32[]{:S(2)}, u32[]{:S(2)}) collective-permute-start(bf16[512,256]{1,0:T(8,128)(2,1)} %get-tuple-element.59), channel_id=1, source_target_pairs={{0,8},{4,20},{8,0},{12,28},{16,24},{20,4},{24,16},{28,12},{1,9},{5... | collective-permute-start | bytes 786440 | tf_op jit(solution)/shard_map/ppermute | solution.py:385
  86.0 11.9 %collective-permute-start.17 = (bf16[512,256]{1,0:T(8,128)(2,1)S(1)}, bf16[512,256]{1,0:T(8,128)(2,1)S(1)}, u32[]{:S(2)}, u32[]{:S(2)}) collective-permute-start(bf16[512,256]{1,0:T(8,128)(2,1)S(1)} %get-tuple-element.68), channel_id=1, source_target_pairs={{0,8},{4,20},{8,0},{12,28},{16,24},{20,4},{24,16},{28,12},{1,9},{5... | collective-permute-start | bytes 786440 | tf_op jit(solution)/shard_map/ppermute | solution.py:385
  86.7 9.6 %all-to-all-start.1 = ((bf16[8,32,512]{2,1,0:T(8,128)(2,1)}), bf16[8,32,512]{2,1,0:T(8,128)(2,1)S(1)}, u32[]{:S(2)}, u32[]{:S(2)}) async-start(bf16[8,32,512]{2,1,0:T(8,128)(2,1)} %bitcast.40), calls=%async_computation.1 | async-start | bytes 524288 | tf_op jit(solution)/shard_map/all_to_all | solution.py:343
  96.3 5.0 %collective-permute-start.19 = (bf16[256,256]{1,0:T(8,128)(2,1)S(1)}, bf16[256,256]{1,0:T(8,128)(2,1)S(1)}, u32[]{:S(2)}, u32[]{:S(2)}) collective-permute-start(bf16[256,256]{1,0:T(8,128)(2,1)S(1)} %slice.190), channel_id=1, source_target_pairs={{0,16},{4,12},{8,24},{12,4},{16,0},{20,28},{24,8},{28,20},{1,17},{... | collective-permute-start | bytes 393224 | tf_op jit(solution)/shard_map/ppermute | solution.py:385
  98.0 5.0 %collective-permute-start.18 = (bf16[256,256]{1,0:T(8,128)(2,1)S(1)}, bf16[256,256]{1,0:T(8,128)(2,1)S(1)}, u32[]{:S(2)}, u32[]{:S(2)}) collective-permute-start(bf16[256,256]{1,0:T(8,128)(2,1)S(1)} %slice.191), channel_id=1, source_target_pairs={{0,16},{4,12},{8,24},{12,4},{16,0},{20,28},{24,8},{28,20},{1,17},{... | collective-permute-start | bytes 393224 | tf_op jit(solution)/shard_map/ppermute | solution.py:385
  103.0 11.0 %collective-permute-start.20 = (bf16[256,512]{1,0:T(8,128)(2,1)S(1)}, bf16[256,512]{1,0:T(8,128)(2,1)S(1)}, u32[]{:S(2)}, u32[]{:S(2)}) collective-permute-start(bf16[256,512]{1,0:T(8,128)(2,1)S(1)} %pad_maximum_fusion.3), channel_id=1, source_target_pairs={{0,0},{1,10},{2,17},{3,27},{4,4},{5,14},{6,21},{7,31},{8,1},{9,11}... | collective-permute-start | bytes 786440 | tf_op jit(solution)/shard_map/ppermute | solution.py:398
  (2 other events, 4.2 us)

commit v4 on v3

--- a/solution.py
+++ b/solution.py
@@ -37,50 +37,63 @@
     return lax.ppermute(array, "tensor", [(i, i ^ step) for i in range(count)])
 
 
-def prepare_kernel(
-    count, steps, at, x_ref, gain_ref, weight_ref, pol_ref, given_ref, kept_ref, *refs
-):
-    sent_refs, (rows_ref, total, square) = refs[:2], refs[2:]
+def chunk_start(count, at, own, i):
+    source = jnp.bitwise_xor(at[0], turned(i, count.bit_length() - 1))
+    return pl.multiple_of(source * own, own)
+
+
+def split_kernel(count, steps, at, x_ref, gain_ref, given_ref, kept_ref):
     f = pl.program_id(0)
     own = x_ref.shape[0] // count
-    levels = count.bit_length() - 1
+
+    def fill(out_ref):
+        for i in range(count):
+            rows = x_ref[pl.ds(chunk_start(count, at, own, i), own), :].astype(F32)
+            out_ref[i * own : (i + 1) * own, :] = (rows * gain_ref[...]).astype(BF16)
+
+    @pl.when(f < steps // 2)
+    def _():
+        fill(given_ref)
+
+    @pl.when(f >= steps // 2)
+    def _():
+        fill(kept_ref)
+
+
+def reference_kernel(
+    count, steps, at, x_ref, gain_ref, weight_ref, kept_ref, sent_ref, rows_ref, total, square
+):
+    f = pl.program_id(0)
+    own = x_ref.shape[0] // count
+
+    @pl.when(f == 0)
+    def _():
+        square[...] = jnp.zeros_like(square)
+
     for i in range(count):
-        source = jnp.bitwise_xor(at[0], turned(i, levels))
-        rows_ref[i * own : (i + 1) * own, :] = x_ref[pl.ds(pl.multiple_of(source * own, own), own), :]
-    wide = rows_ref[...].astype(F32)
-    gained = (wide * pol_ref[...]).astype(BF16)
-
-    @pl.when(f < steps // 2)
-    def _():
-        given_ref[...] = gained
-
-    @pl.when(f >= steps // 2)
-    def _():
-        kept_ref[...] = gained
-
-    part = dot((wide * gain_ref[...]).astype(BF16), weight_ref[...])
-    squares = jnp.sum(wide * wide, axis=1, keepdims=True)
+        wide = x_ref[pl.ds(chunk_start(count, at, own, i), own), :].astype(F32)
+        rows_ref[i * own : (i + 1) * own, :] = (wide * gain_ref[...]).astype(BF16)
+        square[i * own : (i + 1) * own, :] += jnp.sum(wide * wide, axis=1, keepdims=True)
+    part = dot(rows_ref[...], weight_ref[...])
 
     @pl.when(f == 0)
     def _():
         total[...] = part
-        square[...] = squares
 
     @pl.when(f > 0)
     def _():
         total[...] += part
-        square[...] += squares
 
     @pl.when(f == steps - 1)
     def _():
         for i in range(count):
-            sent = sent_refs[i // (count // 2)].at[i % (count // 2)]
-            sent[:own, :] = total[i * own : (i + 1) * own, :].astype(BF16)
+            out = (kept_ref, sent_ref)[i // (count // 2)].at[i % (count // 2)]
+            out[:own, :] = total[i * own : (i + 1) * own, :].astype(BF16)
             power = jnp.broadcast_to(square[i * own : (i + 1) * own, :], (own, 128)).T
             high = power[: POWER_ROWS // 2].astype(BF16).astype(F32)
             low = power[: POWER_ROWS // 2] - high
-            sent[own:, :] = jnp.zeros((POWER_ROWS, sent.shape[1]), BF16)
-            sent[own:, :own] = jnp.concatenate([high, low], axis=0).astype(BF16)
+            out[own:, :] = jnp.zeros((POWER_ROWS, out.shape[1]), BF16)
+            out[own:, :own] = jnp.concatenate([high, low], axis=0).astype(BF16)
 
 
 def row_kernel(
@@ -201,15 +214,42 @@
     def at_step(f, at):
         return lax.rem(f + at[1], steps)
 
-    prepared = pl.pallas_call(
-        functools.partial(prepare_kernel, tensor_count, steps),
+    rows_spec = pl.BlockSpec((group_rows, feature_step), lambda f, at: (0, at_step(f, at)))
+    ref_kept, ref_sent = pl.pallas_call(
+        functools.partial(reference_kernel, tensor_count, steps),
         grid_spec=pltpu.PrefetchScalarGridSpec(
             num_scalar_prefetch=1,
             grid=(steps,),
             in_specs=[
-                pl.BlockSpec((group_rows, feature_step), lambda f, at: (0, at_step(f, at))),
+                rows_spec,
                 pl.BlockSpec((1, feature_step), lambda f, at: (0, at_step(f, at))),
                 pl.BlockSpec((feature_step, value_width), lambda f, at: (at_step(f, at), 0)),
+            ],
+            out_specs=[pl.BlockSpec(ref_shape, lambda f, at: (0, 0, 0))] * 2,
+            scratch_shapes=[
+                pltpu.VMEM((group_rows, feature_step), BF16),
+                pltpu.VMEM((group_rows, value_width), F32),
+                pltpu.VMEM((group_rows, 1), F32),
+            ],
+        ),
+        out_shape=[jax.ShapeDtypeStruct(ref_shape, BF16)] * 2,
+        compiler_params=pltpu.CompilerParams(vmem_limit_bytes=56 * 2**20),
+        cost_estimate=pl.CostEstimate(
+            flops=2 * group_rows * block * value_width,
+            bytes_accessed=5 * 2**20,
+            transcendentals=0,
+        ),
+        name="reference",
+    )(at, tokens, ref_gain.reshape(1, block), ref_weight)
+    ref_sent, tokens = lax.optimization_barrier((ref_sent, tokens))
+    ref_got = crossed(ref_sent, tensor_count, 1)
+    given_rows, kept_rows = pl.pallas_call(
+        functools.partial(split_kernel, tensor_count, steps),
+        grid_spec=pltpu.PrefetchScalarGridSpec(
+            num_scalar_prefetch=1,
+            grid=(steps,),
+            in_specs=[
+                rows_spec,
                 pl.BlockSpec(
                     (1, feature_step), lambda f, at: (0, at[0] * steps + at_step(f, at))
                 ),
@@ -221,35 +261,24 @@
                 pl.BlockSpec(
                     (group_rows, feature_step), lambda f, at: (0, jnp.maximum(f - steps // 2, 0))
                 ),
-            ]
-            + [pl.BlockSpec(ref_shape, lambda f, at: (0, 0, 0))] * 2,
-            scratch_shapes=[
-                pltpu.VMEM((group_rows, feature_step), BF16),
-                pltpu.VMEM((group_rows, value_width), F32),
-                pltpu.VMEM((group_rows, 1), F32),
             ],
         ),
-        out_shape=[jax.ShapeDtypeStruct((group_rows, shard), BF16)] * 2
-        + [jax.ShapeDtypeStruct(ref_shape, BF16)] * 2,
+        out_shape=[jax.ShapeDtypeStruct((group_rows, shard), BF16)] * 2,
         compiler_params=pltpu.CompilerParams(vmem_limit_bytes=56 * 2**20),
         cost_estimate=pl.CostEstimate(
-            flops=2 * group_rows * block * value_width,
-            bytes_accessed=8 * 2**20,
-            transcendentals=0,
+            flops=group_rows * block, bytes_accessed=4 * 2**20, transcendentals=0
         ),
-        name="prepare",
-    )(at, tokens, ref_gain.reshape(1, block), ref_weight, pol_gain.reshape(1, model_width))
-    given_rows, kept_rows, ref_kept, ref_sent = prepared
-    ref_got = crossed(ref_sent, tensor_count, 1)
+        name="split",
+    )(at, tokens, pol_gain.reshape(1, model_width))
     got_rows = swapped(given_rows, dp_count)
 
     held, got, is_getter = pol_weight, first_got, first_getter
     cot = cotangent.reshape(slot_count, value_width)
-    ref_got, cot = lax.optimization_barrier((ref_got, cot))
     for number in range(1, levels):
         held = jnp.where(is_getter, got, held)
         if number == 1:
-            held, kept_rows = lax.optimization_barrier((held, kept_rows))
+            tied = lax.optimization_barrier((held, kept_rows, ref_got, cot))
+            held, kept_rows, ref_got, cot = tied
         got, is_getter = stage(number, held)
     for level in range(1, levels):
         ref_sum = ref_kept[:, :own_rows].astype(F32) + ref_got[:, :own_rows].astype(F32)
@@ -278,8 +307,6 @@
         weight = lax.optimization_barrier(jnp.where(is_getter, got[:, cols], held[:, cols]))
         value_got.append(swapped(dot(got_rows, weight).astype(BF16), dp_count))
         value_kept.append(dot(kept_rows, weight))
-    tied = lax.optimization_barrier((value_got[0], lengths, bins, advantage, logprob_gap))
-    value_got[0], lengths, bins, advantage, logprob_gap = tied
     fixed, pull, row_scale, row_at, terms_sent = pl.pallas_call(
         functools.partial(row_kernel, span_rows, model_width),
         in_specs=[smem] * 3 + [vmem] * 4,
@@ -339,7 +366,6 @@
         slopes.append(slope)
 
     sent = dot_rows(row_at, jnp.concatenate(values, axis=1).astype(BF16)).astype(BF16)
-    slopes[0], sent = lax.optimization_barrier((slopes[0], sent))
     policy_values = lax.all_to_all(sent, "dp", split_axis=0, concat_axis=0, tiled=True)
 
     grad_kept, grad_sent = [], []
@@ -373,6 +399,7 @@
         )(chunk_at, kept_rows, got_rows, slopes[j], slopes_got)
         grad_kept.append(chunks[0])
         grad_sent.append(chunks[1])
+    grad_sent[-1], policy_values = lax.optimization_barrier((grad_sent[-1], policy_values))
     grads = []
     for j in range(PARTS):
         total, given = grad_kept[j], grad_sent[j]
@@ -384,8 +411,6 @@
             ]
             total = total + lax.ppermute(given, "dp", pairs).astype(F32)
             half_rows = total.shape[0] // 2
-            if j == PARTS - 1 and level == 0:
-                total, policy_values = lax.optimization_barrier((total, policy_values))
             if level < levels - 1:
                 total, given = total[:half_rows], total[half_rows:].astype(BF16)
         grads.append(total.astype(BF16))

time: 117 us -> 117 us (level)
  starting transfers between devices: 38.8 us -> 32.3 us
  Pallas kernels: 11.7 us -> 15.4 us
  waiting for transfers between devices: 47.7 us -> 50.8 us
  local copies, waits for them, and re-layouts: 3.64 us -> 5.89 us
    ppermute x5, starting transfers between devices: 8.95 us -> 2.79 us  [swapped(): return lax.ppermute(array, 'dp', [(i, i ^ 1) for i in range(dp_count)])]
    ppermute x4, waiting for transfers between devices: 4.38 us -> 9.46 us  [on_device(): total = total + lax.ppermute(given, 'dp', pairs).astype(F32)]
    pallas_call x1 -> x2, Pallas kernels: 7.13 us -> 10.8 us  [the longest x1 5.93 us: on_device(): pl.pallas_call(functools.partial(reference_kernel, tensor_count, steps),...]
    unnamed x22 -> x23, local copies, waits for them, and re-layouts: 0.77 us -> 4.06 us
    all_to_all x1, waiting for transfers between devices: 4.47 us -> 1.8 us  [on_device(): lax.all_to_all(sent, 'dp', split_axis=0, concat_axis=0, tiled=True)]
    all_to_all x1, starting transfers between devices: 4.12 us -> 6.04 us  [on_device(): lax.all_to_all(sent, 'dp', split_axis=0, concat_axis=0, tiled=True)]
    ppermute x1, waiting for transfers between devices: 6.4 us -> 8.3 us  [on_device(): lax.ppermute(jnp.concatenate(grads, axis=1), AXES, pairs).astype(F32)]
    ppermute x1, starting transfers between devices: 4.55 us -> 2.66 us  [on_device(): lax.ppermute(jnp.concatenate(grads, axis=1), AXES, pairs).astype(F32)]
  transfers between devices with their start and end apart: 23 -> 23, of which waited for: 11 -> 14; matrix products, arithmetic and copies ran while one was open for 12% -> 11% of each run, Pallas kernels for 10% -> 13%
where the time goes in v4:
time: 117 us
  waiting for transfers between devices  50.8 us (43%)
  starting transfers between devices  32.3 us (28%)
  Pallas kernels  15.4 us (13%)
  other arithmetic  8.62 us (7%)
  local copies, waits for them, and re-layouts  5.89 us (5%)
  matrix products  2.71 us (2%)
    ppermute x9, waiting for transfers between devices, crossed(): return lax.ppermute(array, 'tensor', [(i, i ^ step) for i in range(count)])  30.7 us
    ppermute x4, waiting for transfers between devices, on_device(): total = total + lax.ppermute(given, 'dp', pairs).astype(F32)  9.46 us
    ppermute x1, waiting for transfers between devices, on_device(): lax.ppermute(jnp.concatenate(grads, axis=1), AXES, pairs).astype(F32)  8.3 us
    ppermute x9, starting transfers between devices, crossed(): return lax.ppermute(array, 'tensor', [(i, i ^ step) for i in range(count)])  8.09 us
    all_to_all x1, starting transfers between devices, on_device(): got_cot = lax.all_to_all(cot, 'dp', split_axis=0, concat_axis=0, tiled=True)  6.31 us
    all_to_all x1, starting transfers between devices, on_device(): lax.all_to_all(sent, 'dp', split_axis=0, concat_axis=0, tiled=True)  6.04 us
    pallas_call x1, Pallas kernels, on_device(): pl.pallas_call(functools.partial(reference_kernel, tensor_count, steps),...  5.93 us
    pallas_call x1, Pallas kernels, on_device(): pl.pallas_call(functools.partial(split_kernel, tensor_count, steps), grid...  4.91 us
  transfers between devices with their start and end apart: 23, of which 14 were waited for; matrix products, arithmetic and copies ran while one was open for 11% of the time, Pallas kernels for 13%

profile of v4, /device:TPU:4, one launch (start us, length us, event | category | flops | bytes accessed | tf_op | source)
XLA Modules:
  0.0 116.7 jit_solution(12100978704214182438)
XLA Ops:
  2.0 5.9 %reference.1 = (bf16[2,144,512]{2,1,0:T(8,128)(2,1)}, bf16[2,144,512]{2,1,0:T(8,128)(2,1)}) custom-call(s32[2]{0:T(128)} %pad_add_fusion.1.at, bf16[512,2048]{1,0:T(8,128)(2,1)} %x_ref.2, f32[1,2048]{1,0:T(1,128)} %bitcast.43, bf16[2048,512]{1,0:T(8,128)(2,1)} %weight_ref.1), custom_call_target="tpu_custom_call" | custom-call | flops 1073741824 | bytes 5242880 | tf_op jit(solution)/shard_map/reference/pallas_call | solution.py:218
  7.9 1.6 %collective-permute-start.1 = (bf16[2,144,512]{2,1,0:T(8,128)(2,1)}, bf16[2,144,512]{2,1,0:T(8,128)(2,1)S(1)}, u32[]{:S(2)}, u32[]{:S(2)}) collective-permute-start(bf16[2,144,512]{2,1,0:T(8,128)(2,1)} %get-tuple-element.34), channel_id=1, source_target_pairs={{0,1},{1,0},{2,3},{3,2},{4,5},{5,4},{6,7},{7,6},{8,9},{9,8},{10,11... | collective-permute-start | bytes 884744 | tf_op jit(solution)/shard_map/ppermute | solution.py:37
  9.5 4.9 %split.1 = (bf16[512,1024]{1,0:T(8,128)(2,1)}, bf16[512,1024]{1,0:T(8,128)(2,1)}) custom-call(s32[2]{0:T(128)} %pad_add_fusion.1.at, bf16[512,2048]{1,0:T(8,128)(2,1)} %x_ref.2, f32[1,8192]{1,0:T(1,128)} %bitcast.40), custom_call_target="tpu_custom_call" | custom-call | flops 1048576 | bytes 4194304 | tf_op jit(solution)/shard_map/split/pallas_call | solution.py:246
  14.4 1.1 broadcast_select_fusion
  15.5 1.9 %collective-permute-done.1 = bf16[2,144,512]{2,1,0:T(8,128)(2,1)S(1)} collective-permute-done((bf16[2,144,512]{2,1,0:T(8,128)(2,1)}, bf16[2,144,512]{2,1,0:T(8,128)(2,1)S(1)}, u32[]{:S(2)}, u32[]{:S(2)}) %collective-permute-start.1) | collective-permute-done | bytes 294944 | tf_op jit(solution)/shard_map/ppermute | solution.py:37
  17.5 1.3 %collective-permute-start.4 = (bf16[1024,512]{1,0:T(8,128)(2,1)}, bf16[1024,512]{1,0:T(8,128)(2,1)}, u32[]{:S(2)}, u32[]{:S(2)}) collective-permute-start(bf16[1024,512]{1,0:T(8,128)(2,1)} %broadcast_select_fusion), channel_id=1, source_target_pairs={{0,16},{9,25},{18,2},{27,11},{8,24},{1,17},{26,10},{19,3},{4,12},{... | collective-permute-start | bytes 3145736 | tf_op jit(solution)/shard_map/ppermute | solution.py:205
  18.8 2.0 %collective-permute-start.2 = (bf16[512,1024]{1,0:T(8,128)(2,1)}, bf16[512,1024]{1,0:T(8,128)(2,1)S(1)}, u32[]{:S(2)}, u32[]{:S(2)}) collective-permute-start(bf16[512,1024]{1,0:T(8,128)(2,1)} %get-tuple-element.36), channel_id=1, source_target_pairs={{0,4},{4,0},{8,12},{12,8},{16,20},{20,16},{24,28},{28,24},{1,5},{5... | collective-permute-start | bytes 3145736 | tf_op jit(solution)/shard_map/ppermute | solution.py:29
  20.8 6.3 %all-to-all-start = ((bf16[8,32,512]{2,1,0:T(8,128)(2,1)}), bf16[8,32,512]{2,1,0:T(8,128)(2,1)S(1)}, u32[]{:S(2)}, u32[]{:S(2)}) async-start(bf16[8,32,512]{2,1,0:T(8,128)(2,1)} %bitcast.13), calls=%async_computation | async-start | bytes 524288 | tf_op jit(solution)/shard_map/all_to_all | solution.py:291
  27.2 1.0 collective-permute-start.3
  28.2 8.9 %collective-permute-done.3 = bf16[1,160,512]{2,1,0:T(8,128)(2,1)S(1)} collective-permute-done((bf16[1,160,512]{2,1,0:T(8,128)(2,1)S(1)}, bf16[1,160,512]{2,1,0:T(8,128)(2,1)S(1)}, u32[]{:S(2)}, u32[]{:S(2)}) %collective-permute-start.3) | collective-permute-done | bytes 163872 | tf_op jit(solution)/shard_map/ppermute | solution.py:37
  37.2 1.1 rows.1
  39.2 1.6 %slice_select_fusion = (bf16[1024,256]{1,0:T(8,128)(2,1)S(1)}, bf16[1024,256]{1,0:T(8,128)(2,1)S(1)}) fusion(bf16[1024,512]{1,0:T(8,128)(2,1)} %collective-permute-done.4, bf16[1024,512]{1,0:T(8,128)(2,1)} %broadcast_select_fusion, pred[]{:T(512)S(6)} %or.15), kind=kLoop, calls=%fused_computation.9 | loop fusion | flops 524288 | bytes 3145729 | tf_op jit(solution)/shard_map/jit(_where)/select_n | solution.py:307
  43.3 2.4 %collective-permute-start.6 = (bf16[256,256]{1,0:T(8,128)(2,1)S(1)}, bf16[256,256]{1,0:T(8,128)(2,1)S(1)}, u32[]{:S(2)}, u32[]{:S(2)}) collective-permute-start(bf16[256,256]{1,0:T(8,128)(2,1)S(1)} %slice.196), channel_id=1, source_target_pairs={{0,1},{1,0},{2,3},{3,2},{4,5},{5,4},{6,7},{7,6},{8,9},{9,8},{10,11... | collective-permute-start | bytes 393224 | tf_op jit(solution)/shard_map/ppermute | solution.py:37
  47.0 4.6 %collective-permute-done.6 = bf16[256,256]{1,0:T(8,128)(2,1)S(1)} collective-permute-done((bf16[256,256]{1,0:T(8,128)(2,1)S(1)}, bf16[256,256]{1,0:T(8,128)(2,1)S(1)}, u32[]{:S(2)}, u32[]{:S(2)}) %collective-permute-start.6) | collective-permute-done | bytes 131104 | tf_op jit(solution)/shard_map/ppermute | solution.py:37
  55.4 2.0 %collective-permute-start.11 = (bf16[256,256]{1,0:T(8,128)(2,1)S(1)}, bf16[256,256]{1,0:T(8,128)(2,1)S(1)}, u32[]{:S(2)}, u32[]{:S(2)}) collective-permute-start(bf16[256,256]{1,0:T(8,128)(2,1)S(1)} %pad_maximum_fusion.4), channel_id=1, source_target_pairs={{0,2},{1,3},{2,0},{3,1},{4,6},{5,7},{6,4},{7,5},{8,10},{9,11},{10,... | collective-permute-start | bytes 393224 | tf_op jit(solution)/shard_map/ppermute | solution.py:37
  57.6 7.4 %collective-permute-done.8 = bf16[256,256]{1,0:T(8,128)(2,1)S(1)} collective-permute-done((bf16[256,256]{1,0:T(8,128)(2,1)S(1)}, bf16[256,256]{1,0:T(8,128)(2,1)S(1)}, u32[]{:S(2)}, u32[]{:S(2)}) %collective-permute-start.8) | collective-permute-done | bytes 131104 | tf_op jit(solution)/shard_map/ppermute | solution.py:37
  65.2 2.1 %collective-permute-done.11 = bf16[256,256]{1,0:T(8,128)(2,1)S(1)} collective-permute-done((bf16[256,256]{1,0:T(8,128)(2,1)S(1)}, bf16[256,256]{1,0:T(8,128)(2,1)S(1)}, u32[]{:S(2)}, u32[]{:S(2)}) %collective-permute-start.11) | collective-permute-done | bytes 131104 | tf_op jit(solution)/shard_map/ppermute | solution.py:37
  67.3 1.0 add_convert_fusion.1
  68.5 1.6 %collective-permute-done.14 = bf16[256,256]{1,0:T(8,128)(2,1)S(1)} collective-permute-done((bf16[256,256]{1,0:T(8,128)(2,1)S(1)}, bf16[256,256]{1,0:T(8,128)(2,1)S(1)}, u32[]{:S(2)}, u32[]{:S(2)}) %collective-permute-start.14) | collective-permute-done | bytes 131104 | tf_op jit(solution)/shard_map/ppermute | solution.py:37
  70.3 3.1 %collective-permute-done.12 = bf16[256,256]{1,0:T(8,128)(2,1)S(1)} collective-permute-done((bf16[256,256]{1,0:T(8,128)(2,1)S(1)}, bf16[256,256]{1,0:T(8,128)(2,1)S(1)}, u32[]{:S(2)}, u32[]{:S(2)}) %collective-permute-start.12) | collective-permute-done | bytes 131104 | tf_op jit(solution)/shard_map/ppermute | solution.py:37
  73.5 2.1 %gradient.3 = (f32[512,256]{1,0:T(8,128)S(1)}, bf16[512,256]{1,0:T(8,128)(2,1)}) custom-call(s32[4]{0:T(128)S(1)} %pad_add_fusion.at, bf16[512,1024]{1,0:T(8,128)(2,1)S(1)} %copy-done, bf16[512,1024]{1,0:T(8,128)(2,1)S(1)} %collective-permute-done.2.got_ref, bf16[512,256]{1,0:T(8,128)(2,1)S(1)} %constant_dynamic-update-slice_fusion.2.slope_ref, ...), custom_call_target="tpu_custom_call" | custom-call | flops 536870912 | bytes 4194304 | tf_op jit(solution)/shard_map/gradient/pallas_call | solution.py:374
  75.6 1.6 %collective-permute-start.16 = (bf16[512,256]{1,0:T(8,128)(2,1)}, bf16[512,256]{1,0:T(8,128)(2,1)}, u32[]{:S(2)}, u32[]{:S(2)}) collective-permute-start(bf16[512,256]{1,0:T(8,128)(2,1)} %get-tuple-element.57), channel_id=1, source_target_pairs={{0,8},{4,20},{8,0},{12,28},{16,24},{20,4},{24,16},{28,12},{1,9},{5... | collective-permute-start | bytes 786440 | tf_op jit(solution)/shard_map/ppermute | solution.py:412
  78.2 6.0 %all-to-all-start.1 = ((bf16[8,32,512]{2,1,0:T(8,128)(2,1)}), bf16[8,32,512]{2,1,0:T(8,128)(2,1)}, u32[]{:S(2)}, u32[]{:S(2)}) async-start(bf16[8,32,512]{2,1,0:T(8,128)(2,1)} %bitcast.19), calls=%async_computation.1 | async-start | bytes 524288 | tf_op jit(solution)/shard_map/all_to_all | solution.py:369
  85.9 1.4 %gradient.2 = (f32[512,256]{1,0:T(8,128)S(1)}, bf16[512,256]{1,0:T(8,128)(2,1)S(1)}) custom-call(s32[4]{0:T(128)S(1)} %pad_add_fusion.at, bf16[512,1024]{1,0:T(8,128)(2,1)S(1)} %copy-done, bf16[512,1024]{1,0:T(8,128)(2,1)S(1)} %collective-permute-done.2.got_ref, bf16[512,256]{1,0:T(8,128)(2,1)S(1)} %constant_dynamic-update-slice_fusion.slope_ref, ...), custom_call_target="tpu_custom_call" | custom-call | flops 536870912 | bytes 4194304 | tf_op jit(solution)/shard_map/gradient/pallas_call | solution.py:374
  88.0 1.8 %all-to-all-done.1 = bf16[8,32,512]{2,1,0:T(8,128)(2,1)} async-done(((bf16[8,32,512]{2,1,0:T(8,128)(2,1)}), bf16[8,32,512]{2,1,0:T(8,128)(2,1)}, u32[]{:S(2)}, u32[]{:S(2)}) %all-to-all-start.1) | async-done | bytes 262176 | tf_op jit(solution)/shard_map/all_to_all | solution.py:369
  90.4 1.0 convert_add_fusion.1
  91.4 1.5 %collective-permute-start.17 = (bf16[256,256]{1,0:T(8,128)(2,1)S(1)}, bf16[256,256]{1,0:T(8,128)(2,1)S(1)}, u32[]{:S(2)}, u32[]{:S(2)}) collective-permute-start(bf16[256,256]{1,0:T(8,128)(2,1)S(1)} %slice.194), channel_id=1, source_target_pairs={{0,16},{4,12},{8,24},{12,4},{16,0},{20,28},{24,8},{28,20},{1,17},{... | collective-permute-start | bytes 393224 | tf_op jit(solution)/shard_map/ppermute | solution.py:412
  92.9 5.1 %collective-permute-done.18 = bf16[512,256]{1,0:T(8,128)(2,1)S(1)} collective-permute-done((bf16[512,256]{1,0:T(8,128)(2,1)}, bf16[512,256]{1,0:T(8,128)(2,1)S(1)}, u32[]{:S(2)}, u32[]{:S(2)}) %collective-permute-start.18) | collective-permute-done | bytes 262176 | tf_op jit(solution)/shard_map/ppermute | solution.py:412
  98.8 4.3 %collective-permute-done.19 = bf16[256,256]{1,0:T(8,128)(2,1)S(1)} collective-permute-done((bf16[256,256]{1,0:T(8,128)(2,1)S(1)}, bf16[256,256]{1,0:T(8,128)(2,1)S(1)}, u32[]{:S(2)}, u32[]{:S(2)}) %collective-permute-start.19) | collective-permute-done | bytes 131104 | tf_op jit(solution)/shard_map/ppermute | solution.py:412
  103.2 2.7 %collective-permute-start.20 = (bf16[256,512]{1,0:T(8,128)(2,1)S(1)}, bf16[256,512]{1,0:T(8,128)(2,1)S(1)}, u32[]{:S(2)}, u32[]{:S(2)}) collective-permute-start(bf16[256,512]{1,0:T(8,128)(2,1)S(1)} %pad_maximum_fusion.2), channel_id=1, source_target_pairs={{0,0},{1,10},{2,17},{3,27},{4,4},{5,14},{6,21},{7,31},{8,1},{9,11}... | collective-permute-start | bytes 786440 | tf_op jit(solution)/shard_map/ppermute | solution.py:423
  105.9 8.3 %collective-permute-done.20 = bf16[256,512]{1,0:T(8,128)(2,1)S(1)} collective-permute-done((bf16[256,512]{1,0:T(8,128)(2,1)S(1)}, bf16[256,512]{1,0:T(8,128)(2,1)S(1)}, u32[]{:S(2)}, u32[]{:S(2)}) %collective-permute-start.20) | collective-permute-done | bytes 262176 | tf_op jit(solution)/shard_map/ppermute | solution.py:423
  115.0 1.7 %copy.18 = bf16[1,1,256,512]{3,2,1,0:T(8,128)(2,1)} copy(bf16[1,1,256,512]{3,2,1,0:T(8,128)(2,1)} %bitcast.21) | data formatting | bytes 524288
  (87 shorter events, 16.2 us)
Async XLA Ops:
  0.6 13.8 %collective-permute-start = (bf16[1024,512]{1,0:T(8,128)(2,1)}, bf16[1024,512]{1,0:T(8,128)(2,1)S(1)}, u32[]{:S(2)}, u32[]{:S(2)}) collective-permute-start(bf16[1024,512]{1,0:T(8,128)(2,1)} %param.14), channel_id=1, source_target_pairs={{0,8},{9,1},{18,26},{27,19},{4,20},{13,29},{22,6},{31,15}} | collective-permute-start | bytes 3145736 | tf_op jit(solution)/shard_map/ppermute | solution.py:205
  7.9 6.5 %copy-start.8 = (bf16[1024,512]{1,0:T(8,128)(2,1)S(1)}, bf16[1024,512]{1,0:T(8,128)(2,1)}, u32[]{:S(2)}) copy-start(bf16[1024,512]{1,0:T(8,128)(2,1)} %param.14) | copy-start | bytes 3145732
  7.9 9.6 %collective-permute-start.1 = (bf16[2,144,512]{2,1,0:T(8,128)(2,1)}, bf16[2,144,512]{2,1,0:T(8,128)(2,1)S(1)}, u32[]{:S(2)}, u32[]{:S(2)}) collective-permute-start(bf16[2,144,512]{2,1,0:T(8,128)(2,1)} %get-tuple-element.34), channel_id=1, source_target_pairs={{0,1},{1,0},{2,3},{3,2},{4,5},{5,4},{6,7},{7,6},{8,9},{9,8},{10,11... | collective-permute-start | bytes 884744 | tf_op jit(solution)/shard_map/ppermute | solution.py:37
  14.4 6.4 %copy-start.9 = (bf16[2,144,512]{2,1,0:T(8,128)(2,1)S(1)}, bf16[2,144,512]{2,1,0:T(8,128)(2,1)}, u32[]{:S(2)}) copy-start(bf16[2,144,512]{2,1,0:T(8,128)(2,1)} %get-tuple-element.38) | copy-start | bytes 884740
  15.5 21.7 %copy-start.3 = (s32[1,1,8]{2,1,0:T(1,128)S(1)}, s32[1,1,8]{2,1,0:T(1,128)}, u32[]{:S(2)}) copy-start(s32[1,1,8]{2,1,0:T(1,128)} %param.15) | copy-start | bytes 100
  15.5 21.7 %copy-start.4 = (s32[1,1,8]{2,1,0:T(1,128)S(1)}, s32[1,1,8]{2,1,0:T(1,128)}, u32[]{:S(2)}) copy-start(s32[1,1,8]{2,1,0:T(1,128)} %param.16) | copy-start | bytes 100
  15.5 21.7 %copy-start.5 = (f32[1,1,8]{2,1,0:T(1,128)S(1)}, f32[1,1,8]{2,1,0:T(1,128)}, u32[]{:S(2)}) copy-start(f32[1,1,8]{2,1,0:T(1,128)} %param.17) | copy-start | bytes 100
  15.5 21.7 %copy-start.6 = (f32[128]{0:T(128)S(1)}, f32[128]{0:T(128)}, u32[]{:S(2)}) copy-start(f32[128]{0:T(128)} %param.18) | copy-start | bytes 1540
  17.5 21.7 %collective-permute-start.4 = (bf16[1024,512]{1,0:T(8,128)(2,1)}, bf16[1024,512]{1,0:T(8,128)(2,1)}, u32[]{:S(2)}, u32[]{:S(2)}) collective-permute-start(bf16[1024,512]{1,0:T(8,128)(2,1)} %broadcast_select_fusion), channel_id=1, source_target_pairs={{0,16},{9,25},{18,2},{27,11},{8,24},{1,17},{26,10},{19,3},{4,12},{... | collective-permute-start | bytes 3145736 | tf_op jit(solution)/shard_map/ppermute | solution.py:205
  18.8 22.1 %collective-permute-start.2 = (bf16[512,1024]{1,0:T(8,128)(2,1)}, bf16[512,1024]{1,0:T(8,128)(2,1)S(1)}, u32[]{:S(2)}, u32[]{:S(2)}) collective-permute-start(bf16[512,1024]{1,0:T(8,128)(2,1)} %get-tuple-element.36), channel_id=1, source_target_pairs={{0,4},{4,0},{8,12},{12,8},{16,20},{20,16},{24,28},{28,24},{1,5},{5... | collective-permute-start | bytes 3145736 | tf_op jit(solution)/shard_map/ppermute | solution.py:29
  20.8 16.4 %all-to-all-start = ((bf16[8,32,512]{2,1,0:T(8,128)(2,1)}), bf16[8,32,512]{2,1,0:T(8,128)(2,1)S(1)}, u32[]{:S(2)}, u32[]{:S(2)}) async-start(bf16[8,32,512]{2,1,0:T(8,128)(2,1)} %bitcast.13), calls=%async_computation | async-start | bytes 524288 | tf_op jit(solution)/shard_map/all_to_all | solution.py:291
  27.2 9.9 %collective-permute-start.3 = (bf16[1,160,512]{2,1,0:T(8,128)(2,1)S(1)}, bf16[1,160,512]{2,1,0:T(8,128)(2,1)S(1)}, u32[]{:S(2)}, u32[]{:S(2)}) collective-permute-start(bf16[1,160,512]{2,1,0:T(8,128)(2,1)S(1)} %get-tuple-element.66), channel_id=1, source_target_pairs={{0,2},{1,3},{2,0},{3,1},{4,6},{5,7},{6,4},{7,5},{8,10},{9,11},{10,... | collective-permute-start | bytes 491528 | tf_op jit(solution)/shard_map/ppermute | solution.py:37
  38.3 13.3 %collective-permute-start.7 = (bf16[128,640]{1,0:T(8,128)(2,1)S(1)}, bf16[128,640]{1,0:T(8,128)(2,1)S(1)}, u32[]{:S(2)}, u32[]{:S(2)}) collective-permute-start(bf16[128,640]{1,0:T(8,128)(2,1)S(1)} %get-tuple-element.42), channel_id=1, source_target_pairs={{0,2},{1,3},{2,0},{3,1},{4,6},{5,7},{6,4},{7,5},{8,10},{9,11},{10,... | collective-permute-start | bytes 491528 | tf_op jit(solution)/shard_map/ppermute | solution.py:37
  40.8 2.1 %copy-start = (bf16[512,1024]{1,0:T(8,128)(2,1)S(1)}, bf16[512,1024]{1,0:T(8,128)(2,1)}, u32[]{:S(2)}) copy-start(bf16[512,1024]{1,0:T(8,128)(2,1)} %get-tuple-element.35.kept_ref) | copy-start | bytes 3145732
  41.3 1.6 %collective-permute-start.5 = (bf16[512,256]{1,0:T(8,128)(2,1)S(1)}, bf16[512,256]{1,0:T(8,128)(2,1)S(1)}, u32[]{:S(2)}, u32[]{:S(2)}) collective-permute-start(bf16[512,256]{1,0:T(8,128)(2,1)S(1)} %convolution_convert_fusion.2), channel_id=1, source_target_pairs={{0,4},{4,0},{8,12},{12,8},{16,20},{20,16},{24,28},{28,24},{1,5},{5... | collective-permute-start | bytes 786440 | tf_op jit(solution)/shard_map/ppermute | solution.py:29
  41.8 4.0 %collective-permute-start.9 = (bf16[512,256]{1,0:T(8,128)(2,1)S(1)}, bf16[512,256]{1,0:T(8,128)(2,1)S(1)}, u32[]{:S(2)}, u32[]{:S(2)}) collective-permute-start(bf16[512,256]{1,0:T(8,128)(2,1)S(1)} %convolution_convert_fusion.1), channel_id=1, source_target_pairs={{0,4},{4,0},{8,12},{12,8},{16,20},{20,16},{24,28},{28,24},{1,5},{5... | collective-permute-start | bytes 786440 | tf_op jit(solution)/shard_map/ppermute | solution.py:29
  43.3 8.3 %collective-permute-start.6 = (bf16[256,256]{1,0:T(8,128)(2,1)S(1)}, bf16[256,256]{1,0:T(8,128)(2,1)S(1)}, u32[]{:S(2)}, u32[]{:S(2)}) collective-permute-start(bf16[256,256]{1,0:T(8,128)(2,1)S(1)} %slice.196), channel_id=1, source_target_pairs={{0,1},{1,0},{2,3},{3,2},{4,5},{5,4},{6,7},{7,6},{8,9},{9,8},{10,11... | collective-permute-start | bytes 393224 | tf_op jit(solution)/shard_map/ppermute | solution.py:37
  46.9 7.6 %collective-permute-start.10 = (bf16[256,256]{1,0:T(8,128)(2,1)}, bf16[256,256]{1,0:T(8,128)(2,1)}, u32[]{:S(2)}, u32[]{:S(2)}) collective-permute-start(bf16[256,256]{1,0:T(8,128)(2,1)} %slice.195), channel_id=1, source_target_pairs={{0,1},{1,0},{2,3},{3,2},{4,5},{5,4},{6,7},{7,6},{8,9},{9,8},{10,11... | collective-permute-start | bytes 393224 | tf_op jit(solution)/shard_map/ppermute | solution.py:37
  53.4 11.5 %collective-permute-start.8 = (bf16[256,256]{1,0:T(8,128)(2,1)S(1)}, bf16[256,256]{1,0:T(8,128)(2,1)S(1)}, u32[]{:S(2)}, u32[]{:S(2)}) collective-permute-start(bf16[256,256]{1,0:T(8,128)(2,1)S(1)} %pad_maximum_fusion.3), channel_id=1, source_target_pairs={{0,2},{1,3},{2,0},{3,1},{4,6},{5,7},{6,4},{7,5},{8,10},{9,11},{10,... | collective-permute-start | bytes 393224 | tf_op jit(solution)/shard_map/ppermute | solution.py:37
  55.4 11.8 %collective-permute-start.11 = (bf16[256,256]{1,0:T(8,128)(2,1)S(1)}, bf16[256,256]{1,0:T(8,128)(2,1)S(1)}, u32[]{:S(2)}, u32[]{:S(2)}) collective-permute-start(bf16[256,256]{1,0:T(8,128)(2,1)S(1)} %pad_maximum_fusion.4), channel_id=1, source_target_pairs={{0,2},{1,3},{2,0},{3,1},{4,6},{5,7},{6,4},{7,5},{8,10},{9,11},{10,... | collective-permute-start | bytes 393224 | tf_op jit(solution)/shard_map/ppermute | solution.py:37
  65.1 5.0 %collective-permute-start.14 = (bf16[256,256]{1,0:T(8,128)(2,1)S(1)}, bf16[256,256]{1,0:T(8,128)(2,1)S(1)}, u32[]{:S(2)}, u32[]{:S(2)}) collective-permute-start(bf16[256,256]{1,0:T(8,128)(2,1)S(1)} %get-tuple-element.55), channel_id=1, source_target_pairs={{0,1},{1,0},{2,3},{3,2},{4,5},{5,4},{6,7},{7,6},{8,9},{9,8},{10,11... | collective-permute-start | bytes 393224 | tf_op jit(solution)/shard_map/ppermute | solution.py:37
  68.4 5.0 %collective-permute-start.12 = (bf16[256,256]{1,0:T(8,128)(2,1)S(1)}, bf16[256,256]{1,0:T(8,128)(2,1)S(1)}, u32[]{:S(2)}, u32[]{:S(2)}) collective-permute-start(bf16[256,256]{1,0:T(8,128)(2,1)S(1)} %get-tuple-element.49), channel_id=1, source_target_pairs={{0,1},{1,0},{2,3},{3,2},{4,5},{5,4},{6,7},{7,6},{8,9},{9,8},{10,11... | collective-permute-start | bytes 393224 | tf_op jit(solution)/shard_map/ppermute | solution.py:37
  70.1 3.4 %collective-permute-start.15 = (bf16[512,256]{1,0:T(8,128)(2,1)S(1)}, bf16[512,256]{1,0:T(8,128)(2,1)S(1)}, u32[]{:S(2)}, u32[]{:S(2)}) collective-permute-start(bf16[512,256]{1,0:T(8,128)(2,1)S(1)} %constant_dynamic-update-slice_fusion.2.slope_ref), channel_id=1, source_target_pairs={{0,4},{4,0},{8,12},{12,8},{16,20},{20,16},{24,28},{28,24},{1,5},{5... | collective-permute-start | bytes 786440 | tf_op jit(solution)/shard_map/ppermute | solution.py:29
  73.4 10.8 %collective-permute-start.13 = (bf16[512,256]{1,0:T(8,128)(2,1)S(1)}, bf16[512,256]{1,0:T(8,128)(2,1)S(1)}, u32[]{:S(2)}, u32[]{:S(2)}) collective-permute-start(bf16[512,256]{1,0:T(8,128)(2,1)S(1)} %constant_dynamic-update-slice_fusion.slope_ref), channel_id=1, source_target_pairs={{0,4},{4,0},{8,12},{12,8},{16,20},{20,16},{24,28},{28,24},{1,5},{5... | collective-permute-start | bytes 786440 | tf_op jit(solution)/shard_map/ppermute | solution.py:29
  75.6 14.7 %collective-permute-start.16 = (bf16[512,256]{1,0:T(8,128)(2,1)}, bf16[512,256]{1,0:T(8,128)(2,1)}, u32[]{:S(2)}, u32[]{:S(2)}) collective-permute-start(bf16[512,256]{1,0:T(8,128)(2,1)} %get-tuple-element.57), channel_id=1, source_target_pairs={{0,8},{4,20},{8,0},{12,28},{16,24},{20,4},{24,16},{28,12},{1,9},{5... | collective-permute-start | bytes 786440 | tf_op jit(solution)/shard_map/ppermute | solution.py:412
  78.2 11.6 %all-to-all-start.1 = ((bf16[8,32,512]{2,1,0:T(8,128)(2,1)}), bf16[8,32,512]{2,1,0:T(8,128)(2,1)}, u32[]{:S(2)}, u32[]{:S(2)}) async-start(bf16[8,32,512]{2,1,0:T(8,128)(2,1)} %bitcast.19), calls=%async_computation.1 | async-start | bytes 524288 | tf_op jit(solution)/shard_map/all_to_all | solution.py:369
  84.9 0.9 copy-start.2
  87.3 0.7 copy-start.7
  89.8 8.2 %collective-permute-start.18 = (bf16[512,256]{1,0:T(8,128)(2,1)}, bf16[512,256]{1,0:T(8,128)(2,1)S(1)}, u32[]{:S(2)}, u32[]{:S(2)}) collective-permute-start(bf16[512,256]{1,0:T(8,128)(2,1)} %copy-done.7), channel_id=1, source_target_pairs={{0,8},{4,20},{8,0},{12,28},{16,24},{20,4},{24,16},{28,12},{1,9},{5... | collective-permute-start | bytes 786440 | tf_op jit(solution)/shard_map/ppermute | solution.py:412
  91.4 7.4 %collective-permute-start.17 = (bf16[256,256]{1,0:T(8,128)(2,1)S(1)}, bf16[256,256]{1,0:T(8,128)(2,1)S(1)}, u32[]{:S(2)}, u32[]{:S(2)}) collective-permute-start(bf16[256,256]{1,0:T(8,128)(2,1)S(1)} %slice.194), channel_id=1, source_target_pairs={{0,16},{4,12},{8,24},{12,4},{16,0},{20,28},{24,8},{28,20},{1,17},{... | collective-permute-start | bytes 393224 | tf_op jit(solution)/shard_map/ppermute | solution.py:412
  98.1 5.0 %collective-permute-start.19 = (bf16[256,256]{1,0:T(8,128)(2,1)S(1)}, bf16[256,256]{1,0:T(8,128)(2,1)S(1)}, u32[]{:S(2)}, u32[]{:S(2)}) collective-permute-start(bf16[256,256]{1,0:T(8,128)(2,1)S(1)} %slice.193), channel_id=1, source_target_pairs={{0,16},{4,12},{8,24},{12,4},{16,0},{20,28},{24,8},{28,20},{1,17},{... | collective-permute-start | bytes 393224 | tf_op jit(solution)/shard_map/ppermute | solution.py:412
  103.2 11.0 %collective-permute-start.20 = (bf16[256,512]{1,0:T(8,128)(2,1)S(1)}, bf16[256,512]{1,0:T(8,128)(2,1)S(1)}, u32[]{:S(2)}, u32[]{:S(2)}) collective-permute-start(bf16[256,512]{1,0:T(8,128)(2,1)S(1)} %pad_maximum_fusion.2), channel_id=1, source_target_pairs={{0,0},{1,10},{2,17},{3,27},{4,4},{5,14},{6,21},{7,31},{8,1},{9,11}... | collective-permute-start | bytes 786440 | tf_op jit(solution)/shard_map/ppermute | solution.py:423
  (1 other events, 0.7 us)
